TPU v7x, 32 devices: a whole 2x2x4 slice. The times are simulated.
32 devices in a mesh: ctx: 16 (over z, x, core), tp: 2 (over y).
Axes of the slice: x: 2, y: 2, z: 4, core: 2. Of those that a mesh axis runs over, the one named last changes fastest.
Arguments:
- tokens: bfloat16 [2, 1024, 768], P(None, 'ctx'), may hold values from -6 to 6
- out_grad: bfloat16 [2, 1024, 768], P(None, 'ctx'), may hold values from -6 to 6
- block_order: int32 [2, 32], replicated, may hold values from 0 to 31, as said below
- qkv_weight: float32 [768, 3, 768], P('ctx', None, 'tp'), may hold values from -0.21875 to 0.21875
- proj_weight: float32 [768, 768], P('tp', 'ctx'), may hold values from -2.5 to 2.5
- up_weight: float32 [768, 3072], P('ctx', 'tp'), may hold values from -0.21875 to 0.21875
- down_weight: float32 [3072, 768], P('tp', 'ctx'), may hold values from -0.109375 to 0.109375
- qkv_bias: float32 [2, 768], P(None, 'tp'), may hold values from -4 to 4
- up_bias: float32 [3072], P('tp'), may hold values from -4 to 4
- layer_vectors: float32 [6, 768], P(None, 'ctx'), may hold values from -2 to 2, as said below
- qkv_first: float32 [768, 3, 768], P('ctx', None, 'tp'), may hold values from -4 to 4
- qkv_second: float32 [768, 3, 768], P('ctx', None, 'tp'), may hold values from 9.216 to 73.728
- proj_first: float32 [768, 768], P('tp', 'ctx'), may hold values from -3.5 to 3.5
- proj_second: float32 [768, 768], P('tp', 'ctx'), may hold values from 0.256 to 2.048
- up_first: float32 [768, 3072], P('ctx', 'tp'), may hold values from -16 to 16
- up_second: float32 [768, 3072], P('ctx', 'tp'), may hold values from 25.6 to 204.8
- down_first: float32 [3072, 768], P('tp', 'ctx'), may hold values from -16 to 16
- down_second: float32 [3072, 768], P('tp', 'ctx'), may hold values from 25.6 to 204.8
- qbias_first: float32 [2, 768], P(None, 'tp'), may hold values from -4 to 4
- qbias_second: float32 [2, 768], P(None, 'tp'), may hold values from 9.216 to 73.728
- ubias_first: float32 [3072], P('tp'), may hold values from -16 to 16
- ubias_second: float32 [3072], P('tp'), may hold values from 25.6 to 204.8
- vector_first: float32 [6, 768], P(None, 'ctx'), may hold values from -32 to 32
- vector_second: float32 [6, 768], P(None, 'ctx'), may hold values from 102.4 to 819.2
Outputs:
- block_output: bfloat16 [2, 1024, 768], P(None, 'ctx')
- input_grad: float32 [2, 1024, 768], P(None, 'ctx')
- qkv_next: float32 [768, 3, 768], P('ctx', None, 'tp')
- qkvfirst_next: float32 [768, 3, 768], P('ctx', None, 'tp')
- qkvsecond_next: float32 [768, 3, 768], P('ctx', None, 'tp')
- proj_next: float32 [768, 768], P('tp', 'ctx')
- projfirst_next: float32 [768, 768], P('tp', 'ctx')
- projsecond_next: float32 [768, 768], P('tp', 'ctx')
- up_next: float32 [768, 3072], P('ctx', 'tp')
- upfirst_next: float32 [768, 3072], P('ctx', 'tp')
- upsecond_next: float32 [768, 3072], P('ctx', 'tp')
- down_next: float32 [3072, 768], P('tp', 'ctx')
- downfirst_next: float32 [3072, 768], P('tp', 'ctx')
- downsecond_next: float32 [3072, 768], P('tp', 'ctx')
- qbias_next: float32 [2, 768], P(None, 'tp')
- qbiasfirst_next: float32 [2, 768], P(None, 'tp')
- qbiassecond_next: float32 [2, 768], P(None, 'tp')
- ubias_next: float32 [3072], P('tp')
- ubiasfirst_next: float32 [3072], P('tp')
- ubiassecond_next: float32 [3072], P('tp')
- vector_next: float32 [6, 768], P(None, 'ctx')
- vectorfirst_next: float32 [6, 768], P(None, 'ctx')
- vectorsecond_next: float32 [6, 768], P(None, 'ctx')
Inputs may be any that keep to these rules, and one draw needn't show every extreme that they name: `block_order`: each row is a permutation of the block numbers; entries 2 d and 2 d + 1 of a row add up to 31. `layer_vectors`: rows 0 and 2 lie within 0.7 to 1.3.
All inputs are finite; a program needn't handle non-finite values.
Results may differ from a plain program's by a relative error of at most 0.02.
Values may be sent and summed in bfloat16 or wider, within the bound.
A program may use at most 192 MiB of HBM per device.

v0:
```python
from functools import partial
import math

import jax
import jax.numpy as jnp
from jax import lax
from jax.sharding import PartitionSpec as P

HD = 64
STEP = 10


BETA_ONE = 0.9
BETA_TWO = 0.95
EPSILON = 1e-08


def layer_norm(values, gain, shift):
    center = values - jnp.mean(values, axis=-1, keepdims=True)
    spread = jnp.mean(center * center, axis=-1, keepdims=True)
    return center * lax.rsqrt(spread + 1e-05) * gain + shift


def gelu_tanh(values):
    return (
        0.5
        * values
        * (1.0 + jnp.tanh(0.7978845608028654 * (values + 0.044715 * values * values * values)))
    )


def adamw(weight, grad, first, second, rate, decay):
    first_new = BETA_ONE * first + (1.0 - BETA_ONE) * grad
    second_new = BETA_TWO * second + (1.0 - BETA_TWO) * grad * grad
    first_hat = first_new / (1.0 - BETA_ONE**STEP)
    second_hat = second_new / (1.0 - BETA_TWO**STEP)
    weight_new = weight - rate * (first_hat / (jnp.sqrt(second_hat) + EPSILON) + decay * weight)
    return (weight_new, first_new, second_new)


def block_positions(order, start, count, blk):
    blocks = lax.dynamic_slice_in_dim(order, start // blk, count // blk, 1)
    offsets = jnp.arange(blk, dtype=jnp.int32)
    return (blocks[:, :, None] * blk + offsets[None, None, :]).reshape(order.shape[0], count)


def row_blocks(array, size):
    shape = array.shape
    return jnp.moveaxis(array.reshape((shape[0], shape[1] // size, size) + shape[2:]), 1, 0)


def forward_fold(carry, piece, start, queries, query_pos, order, blk):
    key_rows, value_rows = piece
    seqs, count, width = key_rows.shape
    heads = width // HD
    size = math.gcd(count, 512)
    key_pos = block_positions(order, start, count, blk)

    def step(state, block):
        key_block, value_block, place_block = block
        running_max, running_sum, context_sum = state
        key_heads = key_block.reshape(seqs, size, heads, HD)
        value_heads = value_block.reshape(seqs, size, heads, HD)
        scores = (
            jnp.einsum("sqhd,skhd->shqk", queries, key_heads, preferred_element_type=jnp.float32)
            * 0.125
        )
        allowed = query_pos[:, None, :, None] >= place_block[:, None, None, :]
        scores = jnp.where(allowed, scores, -1000000000.0)
        top_now = jnp.maximum(running_max, jnp.max(scores, axis=-1))
        rescale = jnp.exp(running_max - top_now)
        shares = jnp.exp(scores - top_now[..., None])
        running_sum = running_sum * rescale + jnp.sum(shares, axis=-1)
        context_sum = context_sum * rescale[..., None] + jnp.einsum(
            "shqk,skhd->shqd",
            shares.astype(jnp.bfloat16),
            value_heads,
            preferred_element_type=jnp.float32,
        )
        return ((top_now, running_sum, context_sum), None)

    carry, _ = lax.scan(
        step,
        carry,
        (row_blocks(key_rows, size), row_blocks(value_rows, size), row_blocks(key_pos, size)),
    )
    return carry


def keeping_fold(carry, piece, start, forward_step):
    state, key_store, value_store = carry
    key_rows, value_rows = piece
    key_store = key_rows
    value_store = value_rows
    state = forward_step(state, piece, start)
    return (state, key_store, value_store)


def query_fold(carry, piece, start, queries, grad_heads, log_total, delta, query_pos, order, blk):
    key_rows, value_rows = piece
    seqs, count, width = key_rows.shape
    heads = width // HD
    size = math.gcd(count, 512)
    key_pos = block_positions(order, start, count, blk)

    def step(grad_sum, block):
        key_block, value_block, place_block = block
        key_heads = key_block.reshape(seqs, size, heads, HD)
        value_heads = value_block.reshape(seqs, size, heads, HD)
        scores = (
            jnp.einsum("sqhd,skhd->shqk", queries, key_heads, preferred_element_type=jnp.float32)
            * 0.125
        )
        allowed = query_pos[:, None, :, None] >= place_block[:, None, None, :]
        scores = jnp.where(allowed, scores, -1000000000.0)
        shares = jnp.exp(scores - log_total[..., None])
        grad_share = jnp.einsum(
            "sqhd,skhd->shqk", grad_heads, value_heads, preferred_element_type=jnp.float32
        )
        grad_score = shares * (grad_share - delta[..., None])
        grad_sum = (
            grad_sum
            + jnp.einsum(
                "shqk,skhd->shqd",
                grad_score.astype(jnp.bfloat16),
                key_heads,
                preferred_element_type=jnp.float32,
            )
            * 0.125
        )
        return (grad_sum, None)

    carry, _ = lax.scan(
        step,
        carry,
        (row_blocks(key_rows, size), row_blocks(value_rows, size), row_blocks(key_pos, size)),
    )
    return carry


def key_fold(carry, piece, start, key_heads, value_heads, key_pos, order, blk):
    query_rows, grad_rows, log_rows, delta_rows = piece
    seqs, count, width = query_rows.shape
    heads = width // HD
    size = math.gcd(count, 512)
    query_pos = block_positions(order, start, count, blk)

    def step(state, block):
        grad_keys, grad_values = state
        query_block, grad_block, log_block, delta_block, place_block = block
        query_heads = query_block.reshape(seqs, size, heads, HD)
        grad_heads = grad_block.reshape(seqs, size, heads, HD)
        log_heads = jnp.transpose(log_block, (0, 2, 1))
        delta_heads = jnp.transpose(delta_block, (0, 2, 1))
        scores = (
            jnp.einsum(
                "sihd,sjhd->shij", query_heads, key_heads, preferred_element_type=jnp.float32
            )
            * 0.125
        )
        allowed = place_block[:, None, :, None] >= key_pos[:, None, None, :]
        scores = jnp.where(allowed, scores, -1000000000.0)
        shares = jnp.exp(scores - log_heads[..., None])
        grad_values = grad_values + jnp.einsum(
            "shij,sihd->shjd",
            shares.astype(jnp.bfloat16),
            grad_heads,
            preferred_element_type=jnp.float32,
        )
        grad_share = jnp.einsum(
            "sihd,sjhd->shij", grad_heads, value_heads, preferred_element_type=jnp.float32
        )
        grad_score = shares * (grad_share - delta_heads[..., None])
        grad_keys = (
            grad_keys
            + jnp.einsum(
                "shij,sihd->shjd",
                grad_score.astype(jnp.bfloat16),
                query_heads,
                preferred_element_type=jnp.float32,
            )
            * 0.125
        )
        return ((grad_keys, grad_values), None)

    carry, _ = lax.scan(
        step,
        carry,
        (
            row_blocks(query_rows, size),
            row_blocks(grad_rows, size),
            row_blocks(log_rows, size),
            row_blocks(delta_rows, size),
            row_blocks(query_pos, size),
        ),
    )
    return carry


def local(
    tokens,
    out_grad,
    block_order,
    qkv_weight,
    proj_weight,
    up_weight,
    down_weight,
    qkv_bias,
    up_bias,
    layer_vectors,
    qkv_first,
    qkv_second,
    proj_first,
    proj_second,
    up_first,
    up_second,
    down_first,
    down_second,
    qbias_first,
    qbias_second,
    ubias_first,
    ubias_second,
    vector_first,
    vector_second,
):
    device = lax.axis_index("ctx")
    groups = lax.axis_size("ctx")
    seqs, rows, width = tokens.shape
    blk = rows // 2
    query_pos = block_positions(block_order, device * rows, rows, blk)
    qkv_full, up_full, proj_full, down_full = (
        lax.all_gather(qkv_weight.astype(jnp.bfloat16), "ctx", axis=0, tiled=True),
        lax.all_gather(up_weight.astype(jnp.bfloat16), "ctx", axis=0, tiled=True),
        lax.all_gather(proj_weight.astype(jnp.bfloat16), "ctx", axis=1, tiled=True),
        lax.all_gather(down_weight.astype(jnp.bfloat16), "ctx", axis=1, tiled=True),
    )
    layer_vector_rows = lax.all_gather(layer_vectors, "ctx", axis=1, tiled=True)
    inputs = tokens.astype(jnp.float32)
    first_normalized, norm_one_back = jax.vjp(
        layer_norm, inputs, layer_vector_rows[0], layer_vector_rows[1]
    )
    normed_low = first_normalized.astype(jnp.bfloat16)
    projection_output = jnp.einsum(
        "sqd,dcf->sqcf", normed_low, qkv_full, preferred_element_type=jnp.float32
    )
    queries = (projection_output[:, :, 0] + qkv_bias[0]).astype(jnp.bfloat16)
    keys = projection_output[:, :, 1].astype(jnp.bfloat16)
    values = (projection_output[:, :, 2] + qkv_bias[1]).astype(jnp.bfloat16)
    heads = queries.shape[-1] // HD
    query_heads = queries.reshape(seqs, rows, heads, HD)
    key_heads = keys.reshape(seqs, rows, heads, HD)
    value_heads = values.reshape(seqs, rows, heads, HD)
    start_state = (
        jnp.full((seqs, heads, rows), -1e30, jnp.float32),
        jnp.zeros((seqs, heads, rows), jnp.float32),
        jnp.zeros((seqs, heads, rows, HD), jnp.float32),
    )
    forward_step = partial(
        forward_fold, queries=query_heads, query_pos=query_pos, order=block_order, blk=blk
    )
    empty_store = jnp.zeros((seqs, rows * groups, keys.shape[-1]), jnp.bfloat16)
    folded, key_store, value_store = keeping_fold(
        (start_state, empty_store, empty_store),
        (
            lax.all_gather(keys, "ctx", axis=1, tiled=True),
            lax.all_gather(values, "ctx", axis=1, tiled=True),
        ),
        jnp.int32(0),
        forward_step=forward_step,
    )
    running_max, running_sum, context_sum = folded
    whole_pair = (key_store, value_store)
    log_total = running_max + jnp.log(running_sum)
    context_value = context_sum / running_sum[..., None]
    context_rows = jnp.transpose(context_value, (0, 2, 1, 3)).reshape(seqs, rows, heads * HD)
    context_low = context_rows.astype(jnp.bfloat16)
    attn_part = jnp.einsum(
        "sqf,fd->sqd", context_low, proj_full, preferred_element_type=jnp.float32
    )
    attention_result = lax.psum(attn_part, "tp") + layer_vector_rows[4]
    middle = inputs + attention_result
    second_normalized, norm_two_back = jax.vjp(
        layer_norm, middle, layer_vector_rows[2], layer_vector_rows[3]
    )
    normed_mid = second_normalized.astype(jnp.bfloat16)
    hidden_preactivation = (
        jnp.einsum("sqd,df->sqf", normed_mid, up_full, preferred_element_type=jnp.float32) + up_bias
    )
    hidden_activation, gelu_back = jax.vjp(gelu_tanh, hidden_preactivation)
    hidden_low = hidden_activation.astype(jnp.bfloat16)
    mlp_part = jnp.einsum("sqf,fd->sqd", hidden_low, down_full, preferred_element_type=jnp.float32)
    mlp_total = lax.psum(mlp_part, "tp") + layer_vector_rows[5]
    block_output = (middle + mlp_total).astype(jnp.bfloat16)
    grad_out = out_grad.astype(jnp.float32)
    grad_down = jnp.einsum("sqf,sqd->fd", hidden_low, out_grad, preferred_element_type=jnp.float32)
    grad_hidden = jnp.einsum("sqd,fd->sqf", out_grad, down_full, preferred_element_type=jnp.float32)
    grad_pre = gelu_back(grad_hidden)[0].astype(jnp.bfloat16)
    grad_up = jnp.einsum("sqd,sqf->df", normed_mid, grad_pre, preferred_element_type=jnp.float32)
    grad_upbias = jnp.sum(grad_pre.astype(jnp.float32), axis=(0, 1))
    mid_part = jnp.einsum("sqf,df->sqd", grad_pre, up_full, preferred_element_type=jnp.float32)
    grad_normed_two = lax.psum(mid_part, "tp")
    grad_mid_norm, grad_gain_two, grad_shift_two = norm_two_back(grad_normed_two)
    grad_middle = grad_out + grad_mid_norm
    grad_attn = grad_middle.astype(jnp.bfloat16)
    grad_proj = jnp.einsum(
        "sqf,sqd->fd", context_low, grad_attn, preferred_element_type=jnp.float32
    )
    grad_context = jnp.einsum(
        "sqd,fd->sqf", grad_attn, proj_full, preferred_element_type=jnp.float32
    ).astype(jnp.bfloat16)
    grad_heads = grad_context.reshape(seqs, rows, heads, HD)
    row_delta = jnp.sum(
        grad_heads.astype(jnp.float32) * context_rows.reshape(seqs, rows, heads, HD), axis=-1
    )
    delta_heads = jnp.transpose(row_delta, (0, 2, 1))
    log_rows = jnp.transpose(log_total, (0, 2, 1))
    zero_heads = jnp.zeros((seqs, heads, rows, HD), jnp.float32)
    query_step = partial(
        query_fold,
        queries=query_heads,
        grad_heads=grad_heads,
        log_total=log_total,
        delta=delta_heads,
        query_pos=query_pos,
        order=block_order,
        blk=blk,
    )
    grad_q_sum = query_step(zero_heads, whole_pair, 0)
    key_step = partial(
        key_fold,
        key_heads=key_heads,
        value_heads=value_heads,
        key_pos=query_pos,
        order=block_order,
        blk=blk,
    )
    grad_k_sum, grad_v_sum = key_step(
        (zero_heads, zero_heads),
        (
            lax.all_gather(queries.astype(jnp.float32), "ctx", axis=1, tiled=True).astype(
                jnp.bfloat16
            ),
            lax.all_gather(grad_context.astype(jnp.float32), "ctx", axis=1, tiled=True).astype(
                jnp.bfloat16
            ),
            lax.all_gather(log_rows, "ctx", axis=1, tiled=True),
            lax.all_gather(row_delta, "ctx", axis=1, tiled=True),
        ),
        jnp.int32(0),
    )

    def head_rows(array):
        return (
            jnp.transpose(array, (0, 2, 1, 3)).reshape(seqs, rows, heads * HD).astype(jnp.bfloat16)
        )

    grad_qkv_low = jnp.stack(
        [head_rows(grad_q_sum), head_rows(grad_k_sum), head_rows(grad_v_sum)], axis=2
    )
    grad_qkv = jnp.einsum(
        "sqd,sqcf->dcf", normed_low, grad_qkv_low, preferred_element_type=jnp.float32
    )
    grad_qbias = jnp.sum(grad_qkv_low[:, :, 0::2].astype(jnp.float32), axis=(0, 1))
    first_part = jnp.einsum(
        "sqcf,dcf->sqd", grad_qkv_low, qkv_full, preferred_element_type=jnp.float32
    )
    grad_normed_one = lax.psum(first_part, "tp")
    grad_in_norm, grad_gain_one, grad_shift_one = norm_one_back(grad_normed_one)
    input_grad = grad_middle + grad_in_norm
    grad_vectors = jnp.stack(
        [
            grad_gain_one,
            grad_shift_one,
            grad_gain_two,
            grad_shift_two,
            jnp.sum(grad_attn.astype(jnp.float32), axis=(0, 1)),
            jnp.sum(grad_out, axis=(0, 1)),
        ]
    )
    sum_qkv, sum_up, sum_proj, sum_down, sum_vectors = (
        lax.psum_scatter(grad_qkv, "ctx", scatter_dimension=0, tiled=True),
        lax.psum_scatter(grad_up, "ctx", scatter_dimension=0, tiled=True),
        lax.psum_scatter(grad_proj, "ctx", scatter_dimension=1, tiled=True),
        lax.psum_scatter(grad_down, "ctx", scatter_dimension=1, tiled=True),
        lax.psum_scatter(grad_vectors, "ctx", scatter_dimension=1, tiled=True),
    )
    sum_qbias, sum_upbias = lax.psum((grad_qbias, grad_upbias), "ctx")
    qkv_new = adamw(qkv_weight, sum_qkv, qkv_first, qkv_second, 0.1, 0.1)
    proj_new = adamw(proj_weight, sum_proj, proj_first, proj_second, 1.0, 0.1)
    up_new = adamw(up_weight, sum_up, up_first, up_second, 0.1, 0.1)
    down_new = adamw(down_weight, sum_down, down_first, down_second, 0.05, 0.1)
    qbias_new = adamw(qkv_bias, sum_qbias, qbias_first, qbias_second, 1.0, 0.0)
    ubias_new = adamw(up_bias, sum_upbias, ubias_first, ubias_second, 1.0, 0.0)
    vector_new = adamw(layer_vectors, sum_vectors, vector_first, vector_second, 1.0, 0.0)
    return (
        block_output,
        input_grad,
        qkv_new[0],
        qkv_new[1],
        qkv_new[2],
        proj_new[0],
        proj_new[1],
        proj_new[2],
        up_new[0],
        up_new[1],
        up_new[2],
        down_new[0],
        down_new[1],
        down_new[2],
        qbias_new[0],
        qbias_new[1],
        qbias_new[2],
        ubias_new[0],
        ubias_new[1],
        ubias_new[2],
        vector_new[0],
        vector_new[1],
        vector_new[2],
    )


def solution(mesh):
    return jax.shard_map(
        local,
        mesh=mesh,
        in_specs=(
            P(None, "ctx", None),
            P(None, "ctx", None),
            P(),
            P("ctx", None, "tp"),
            P("tp", "ctx"),
            P("ctx", "tp"),
            P("tp", "ctx"),
            P(None, "tp"),
            P("tp"),
            P(None, "ctx"),
            P("ctx", None, "tp"),
            P("ctx", None, "tp"),
            P("tp", "ctx"),
            P("tp", "ctx"),
            P("ctx", "tp"),
            P("ctx", "tp"),
            P("tp", "ctx"),
            P("tp", "ctx"),
            P(None, "tp"),
            P(None, "tp"),
            P("tp"),
            P("tp"),
            P(None, "ctx"),
            P(None, "ctx"),
        ),
        out_specs=(
            P(None, "ctx", None),
            P(None, "ctx", None),
            P("ctx", None, "tp"),
            P("ctx", None, "tp"),
            P("ctx", None, "tp"),
            P("tp", "ctx"),
            P("tp", "ctx"),
            P("tp", "ctx"),
            P("ctx", "tp"),
            P("ctx", "tp"),
            P("ctx", "tp"),
            P("tp", "ctx"),
            P("tp", "ctx"),
            P("tp", "ctx"),
            P(None, "tp"),
            P(None, "tp"),
            P(None, "tp"),
            P("tp"),
            P("tp"),
            P("tp"),
            P(None, "ctx"),
            P(None, "ctx"),
            P(None, "ctx"),
        ),
        check_vma=False,
    )
```

profile of v0, /device:TPU:0, one launch (start us, length us, event | category | flops | bytes accessed | tf_op | source)
XLA Modules:
  0.0 800.5 jit_solution(2160157693031137877)
XLA Ops:
  7.2 1.6 convert_element_type.153
  8.9 23.5 %all-gather.1 = f32[16,48,6]{1,2,0:T(8,128)S(1)} all-gather(f32[1,48,6]{1,2,0:T(8,128)} %bitcast.261), channel_id=1, replica_groups=mesh['ctx'=16,'tp'=2] {'ctx'}, dimensions={0}, use_global_device_ids=true | all-gather | bytes 19584 | tf_op jit(solution)/shard_map/all_gather | solution.py:237
  36.1 18.0 %all-gather.10.cloned.1.call-done = bf16[768,3,384]{2,0,1:T(8,128)(2,1)} async-done(((bf16[48,3,384]{2,0,1:T(8,128)(2,1)}), bf16[768,3,384]{2,0,1:T(8,128)(2,1)}) %all-gather.10.cloned.1.call-update) | async-done | bytes 1769488 | tf_op jit(solution)/shard_map/all_gather | solution.py:232
  54.1 2.1 fusion.38
  58.2 23.1 %all_gather.37 = bf16[384,768]{0,1:T(8,128)(2,1)} all-gather(bf16[384,48]{0,1:T(8,128)(2,1)S(1)} %convert_element_type.160), channel_id=1, replica_groups=mesh['ctx'=16,'tp'=2] {'ctx'}, dimensions={1}, use_global_device_ids=true | all-gather | bytes 626688 | tf_op jit(solution)/shard_map/all_gather | solution.py:234
  82.3 13.9 %all-gather.12.cloned.1.call-done = bf16[2,1024,384]{2,1,0:T(8,128)(2,1)} async-done(((bf16[2,64,384]{2,1,0:T(8,128)(2,1)}), bf16[2,1024,384]{2,1,0:T(8,128)(2,1)}) %all-gather.12.cloned.1.call-update) | async-done | bytes 1572880 | tf_op jit(solution)/shard_map/all_gather | solution.py:266
  96.2 2.6 copy.85
  98.8 38.9 %all-gather.22.cloned.1.call-done = bf16[2,1024,1,384]{3,1,2,0:T(8,128)(2,1)} async-done(((bf16[2,64,1,384]{3,1,2,0:T(8,128)(2,1)}), bf16[2,1024,1,384]{3,1,2,0:T(8,128)(2,1)}) %all-gather.22.cloned.1.call-update) | async-done | bytes 1572880 | tf_op jit(solution)/shard_map/all_gather | solution.py:265
  137.7 2.6 copy.84
  140.3 8.9 %while.39 = (s32[]{:T(128)}, f32[2,6,64]{2,1,0:T(8,128)S(1)}, f32[2,6,64]{2,1,0:T(8,128)S(1)}, f32[2,6,64,64]{3,2,1,0:T(8,128)}, s32[2,2,512]{2,1,0:T(2,128)S(1)...) while((s32[]{:T(128)}, f32[2,6,64]{2,1,0:T(8,128)S(1)}, ...), condition=%wide.region_5.6_spmd.clone, body=%wide.region_2.5_spmd.clone.sunk | while | flops 103632768 | bytes 11696329 | solution.py:82
  140.3 1.5 constant_dynamic-slice_fusion.9
  144.8 1.5 constant_dynamic-slice_fusion.9
  149.9 1.3 bitcast_convert_fusion
  151.5 2.2 fusion.56
  154.6 24.0 %all-reduce.6.cloned.1.call-done = f32[2,64,768]{2,1,0:T(8,128)} async-done(((f32[2,64,768]{2,1,0:T(8,128)}), f32[2,64,768]{2,1,0:T(8,128)}) %all-reduce.6.cloned.1.call-update) | async-done | bytes 393232 | tf_op jit(solution)/shard_map/psum | solution.py:280
  179.9 43.9 %all-gather.14.cloned.1.call-done = bf16[768,1536]{1,0:T(8,128)(2,1)} async-done(((bf16[48,1536]{1,0:T(8,128)(2,1)}), bf16[768,1536]{1,0:T(8,128)(2,1)}) %all-gather.14.cloned.1.call-update) | async-done | bytes 2359312 | tf_op jit(solution)/shard_map/all_gather | solution.py:233
  223.9 2.2 convolution_add_fusion.2
  227.0 3.0 convolution_bitcast_fusion
  230.1 74.4 %reduce-scatter.14.cloned.1.call-done = f32[1536,48]{0,1:T(8,128)} async-done(((f32[1536,768]{0,1:T(8,128)}), f32[1536,48]{0,1:T(8,128)}) %reduce-scatter.14.cloned.1.call-update) | async-done | bytes 294928 | tf_op jit(solution)/shard_map/reduce_scatter | solution.py:384
  304.5 2.1 multiply_subtract_fusion
  307.6 41.2 %all-gather.16.cloned.1.call-done = bf16[1536,768]{0,1:T(8,128)(2,1)} async-done(((bf16[1536,48]{0,1:T(8,128)(2,1)}), bf16[1536,768]{0,1:T(8,128)(2,1)}) %all-gather.16.cloned.1.call-update) | async-done | bytes 2359312 | tf_op jit(solution)/shard_map/all_gather | solution.py:235
  348.8 3.5 convert_reduce_fusion
  353.0 1.6 fusion.33
  357.7 22.3 %all_gather.41 = f32[2,1024,6]{2,0,1:T(2,128)S(1)} all-gather(f32[2,64,6]{2,0,1:T(2,128)S(1)} %bitcast.257), channel_id=1, replica_groups=mesh['ctx'=16,'tp'=2] {'ctx'}, dimensions={1}, use_global_device_ids=true | all-gather | bytes 52224 | tf_op jit(solution)/shard_map/all_gather | solution.py:346
  381.1 11.3 %all-gather.18.cloned.1.call-done = bf16[2,1024,384]{2,1,0:T(8,128)(2,1)} async-done(((bf16[2,64,384]{2,1,0:T(8,128)(2,1)}), bf16[2,1024,384]{2,1,0:T(8,128)(2,1)}) %all-gather.18.cloned.1.call-update) | async-done | bytes 1572880 | tf_op jit(solution)/shard_map/all_gather | solution.py:340
  392.4 2.7 copy.98
  395.1 3.3 fusion.31
  398.4 21.0 %all-reduce.8.cloned.1.call-done = f32[2,64,768]{2,1,0:T(8,128)} async-done(((f32[2,64,768]{2,1,0:T(8,128)}), f32[2,64,768]{2,1,0:T(8,128)}) %all-reduce.8.cloned.1.call-update) | async-done | bytes 393232 | tf_op jit(solution)/shard_map/psum | solution.py:301
  419.4 1.8 multiply_reduce_fusion
  421.2 1.3 fusion.92
  426.5 9.5 %while.40 = (s32[]{:T(128)}, f32[2,6,64,64]{3,2,1,0:T(8,128)}, s32[2,2,512]{2,1,0:T(2,128)S(1)}, bf16[2,2,512,384]{2,3,1,0:T(8,128)(2,1)}, bf16[2,64,6,64]{3,1,2...) while((s32[]{:T(128)}, f32[2,6,64,64]{3,2,1,0:T(8,128)}, ...), condition=%wide.region_15.16_spmd.clone, body=%wide.region_14.15_spmd.clone.sunk | while | flops 153567360 | bytes 9392279 | solution.py:133
  426.5 1.5 constant_dynamic-slice_fusion.10
  428.6 2.5 fusion.154
  431.1 1.5 constant_dynamic-slice_fusion.10
  433.3 2.7 fusion.154
  438.0 25.0 %all_gather.43 = f32[2,1024,6]{2,0,1:T(2,128)S(1)} all-gather(f32[2,64,6]{2,0,1:T(2,128)S(1)} %copy.101), channel_id=1, replica_groups=mesh['ctx'=16,'tp'=2] {'ctx'}, dimensions={1}, use_global_device_ids=true | all-gather | bytes 52224 | tf_op jit(solution)/shard_map/all_gather | solution.py:347
  464.1 2.6 all-gather.20.cloned.1.call-done
  466.7 2.6 copy.100
  469.4 15.6 %while.41 = (s32[]{:T(128)}, f32[2,6,64,64]{3,2,1,0:T(8,128)S(1)}, f32[2,6,64,64]{3,2,1,0:T(8,128)}, s32[2,2,512]{2,1,0:T(2,128)S(1)}, bf16[2,2,512,384]{2,3,1,0...) while((s32[]{:T(128)}, f32[2,6,64,64]{3,2,1,0:T(8,128)S(1)}, ...), condition=%wide.region_17.18_spmd.clone, body=%wide.region_16.17_spmd.clone.sunk | while | flops 204390528 | bytes 12286116 | solution.py:186
  469.4 1.5 constant_dynamic-slice_fusion.11
  470.8 1.4 dynamic-slice_bitcast_fusion.11
  472.5 1.4 subtract_exponential_fusion.5
  473.9 1.1 convolution_add_fusion.6
  475.1 1.6 fusion.162
  476.7 1.5 constant_dynamic-slice_fusion.11
  478.1 1.4 dynamic-slice_bitcast_fusion.11
  479.8 1.4 subtract_exponential_fusion.5
  481.2 2.1 convolution_add_fusion.6
  483.3 1.6 fusion.162
  486.6 1.4 fusion.40
  488.1 1.4 convolution_bitcast_fusion.3
  489.6 33.1 %all-reduce.10.cloned.1.call-done = (f32[2,64,768]{2,1,0:T(8,128)}, f32[2,64,768]{2,1,0:T(8,128)}) async-done(((f32[2,64,768]{2,1,0:T(8,128)}, f32[2,64,768]{2,1,0:T(8,128)}), (f32[2,64,768]{2,1,0:T(8,128)}, f32[2,64,768]{2,1,0:T(8,128)})) %all-reduce.10.cloned.1.call-update) | async-done | bytes 786448 | tf_op jit(solution)/shard_map/psum | solution.py:292
  522.8 1.2 fusion.83
  524.0 1.3 fusion.63
  525.4 2.2 convert_reduce_fusion.2
  528.7 3.0 convolution_bitcast_fusion.1
  532.4 2.6 convolution_bitcast_fusion.2
  535.2 49.2 %reduce-scatter.10.cloned.1.call-done = f32[384,48]{0,1:T(8,128)} async-done(((f32[384,768]{0,1:T(8,128)}), f32[384,48]{0,1:T(8,128)}) %reduce-scatter.10.cloned.1.call-update) | async-done | bytes 73744 | tf_op jit(solution)/shard_map/reduce_scatter | solution.py:383
  584.4 1.6 add_subtract_fusion
  586.1 57.7 %all-reduce = (f32[2,384]{1,0:T(2,128)S(1)}, f32[1536]{0:T(1024)S(1)}) all-reduce(f32[2,384]{1,0:T(2,128)S(1)} %convert_reduce_fusion.4, f32[1536]{0:T(1024)S(1)} %copy-done.72), channel_id=1, replica_groups=mesh['ctx'=16,'tp'=2] {'ctx'}, use_global_device_ids=true, to_apply=%region_26.27 | all-reduce | flops 2304 | bytes 18432 | tf_op jit(solution)/shard_map/psum | solution.py:387
  646.5 74.8 %reduce-scatter.12.cloned.1.call-done = f32[48,1536]{1,0:T(8,128)} async-done(((f32[768,1536]{1,0:T(8,128)}), f32[48,1536]{1,0:T(8,128)}) %reduce-scatter.12.cloned.1.call-update) | async-done | bytes 294928 | tf_op jit(solution)/shard_map/reduce_scatter | solution.py:382
  721.3 2.0 multiply_subtract_fusion.1
  723.3 68.8 %reduce-scatter.8.cloned.1.call-done = f32[48,3,384]{2,0,1:T(8,128)} async-done(((f32[768,3,384]{2,0,1:T(8,128)}), f32[48,3,384]{2,0,1:T(8,128)}) %reduce-scatter.8.cloned.1.call-update) | async-done | bytes 221200 | tf_op jit(solution)/shard_map/reduce_scatter | solution.py:381
  792.1 1.9 multiply_subtract_fusion.2
  (313 shorter events, 37.4 us)
Async XLA Ops:
  7.2 46.9 %all-gather.10.cloned.1.call-start = ((), (), s32[]{:S(2)}) async-start(), calls=%async_computation.5 | async-start | bytes 1880064 | tf_op jit(solution)/shard_map/all_gather | solution.py:232
  8.9 87.3 %all-gather.12.cloned.1.call-start = ((), (), s32[]{:S(2)}) async-start(), calls=%async_computation.6 | async-start | bytes 1671168 | tf_op jit(solution)/shard_map/all_gather | solution.py:266
  33.9 23.0 %copy-start.50 = (f32[768]{0:T(1024)}, f32[768]{0:T(1024)S(1)}, u32[]{:S(2)}) copy-start(f32[768]{0:T(1024)S(1)} %get-tuple-element.387) | copy-start | bytes 9220
  33.9 190.0 %copy-start.52 = (f32[768]{0:T(1024)}, f32[768]{0:T(1024)S(1)}, u32[]{:S(2)}) copy-start(f32[768]{0:T(1024)S(1)} %get-tuple-element.384) | copy-start | bytes 9220
  33.9 387.3 %copy-start.42 = (f32[768]{0:T(1024)}, f32[768]{0:T(1024)S(1)}, u32[]{:S(2)}) copy-start(f32[768]{0:T(1024)S(1)} %get-tuple-element.385) | copy-start | bytes 9220
  34.9 22.0 %copy-start.48 = (f32[2,64]{1,0:T(2,128)}, f32[2,64]{1,0:T(2,128)S(1)}, u32[]{:S(2)}) copy-start(f32[2,64]{1,0:T(2,128)S(1)} %broadcast_multiply_fusion.1) | copy-start | bytes 1540
  36.1 20.8 %copy-start.68 = (f32[2,64]{1,0:T(2,128)}, f32[2,64]{1,0:T(2,128)S(1)}, u32[]{:S(2)}) copy-start(f32[2,64]{1,0:T(2,128)S(1)} %fusion.64) | copy-start | bytes 1540
  36.1 20.8 %copy-start.56 = (f32[2,64]{1,0:T(2,128)}, f32[2,64]{1,0:T(2,128)S(1)}, u32[]{:S(2)}) copy-start(f32[2,64]{1,0:T(2,128)S(1)} %fusion.81) | copy-start | bytes 1540
  54.1 4.0 copy-start.36
  57.0 80.7 %all-gather.22.cloned.1.call-start = ((), (), s32[]{:S(2)}) async-start(), calls=%async_computation.17 | async-start | bytes 1671168 | tf_op jit(solution)/shard_map/all_gather | solution.py:265
  57.7 120.8 %all-reduce.6.cloned.1.call-start = ((), (), s32[]{:S(2)}) async-start(), calls=%async_computation.7 | async-start | bytes 786432 | tf_op jit(solution)/shard_map/psum | solution.py:280
  149.2 4.6 copy-start.24
  149.9 28.6 %copy-start.7 = (bf16[2,64,768]{2,1,0:T(8,128)(2,1)S(1)}, bf16[2,64,768]{2,1,0:T(8,128)(2,1)}, u32[]{:S(2)}) copy-start(bf16[2,64,768]{2,1,0:T(8,128)(2,1)} %param.30) | copy-start | bytes 589828
  151.5 27.0 %copy-start.26 = (bf16[2,64,384]{2,1,0:T(8,128)(2,1)}, bf16[2,64,384]{2,1,0:T(8,128)(2,1)S(1)}, u32[]{:S(2)}) copy-start(bf16[2,64,384]{2,1,0:T(8,128)(2,1)S(1)} %convert_element_type.159) | copy-start | bytes 294916
  151.5 72.3 %copy-start.44 = (f32[1536]{0:T(1024)S(1)}, f32[1536]{0:T(1024)}, u32[]{:S(2)}) copy-start(f32[1536]{0:T(1024)} %param.38) | copy-start | bytes 18436
  153.8 70.1 %all-gather.14.cloned.1.call-start = ((), (), s32[]{:S(2)}) async-start(), calls=%async_computation.8 | async-start | bytes 2506752 | tf_op jit(solution)/shard_map/all_gather | solution.py:233
  154.5 150.0 %reduce-scatter.14.cloned.1.call-start = ((), (), s32[]{:S(2)}) async-start(), calls=%async_computation.16 | async-start | bytes 5013504 | tf_op jit(solution)/shard_map/reduce_scatter | solution.py:384
  179.7 241.5 %copy-start = (f32[2,64,768]{2,1,0:T(8,128)}, f32[2,64,768]{2,1,0:T(8,128)S(1)}, u32[]{:S(2)}) copy-start(f32[2,64,768]{2,1,0:T(8,128)S(1)} %get-tuple-element.483) | copy-start | bytes 1179652
  179.7 241.5 %copy-start.54 = (f32[2,64]{1,0:T(2,128)}, f32[2,64]{1,0:T(2,128)S(1)}, u32[]{:S(2)}) copy-start(f32[2,64]{1,0:T(2,128)S(1)} %broadcast_multiply_fusion) | copy-start | bytes 1540
  179.9 241.3 %copy-start.58 = (f32[2,64]{1,0:T(2,128)}, f32[2,64]{1,0:T(2,128)S(1)}, u32[]{:S(2)}) copy-start(f32[2,64]{1,0:T(2,128)S(1)} %fusion.82) | copy-start | bytes 1540
  230.0 74.5 %copy-start.33 = (f32[1536,48]{0,1:T(8,128)S(1)}, f32[1536,48]{0,1:T(8,128)}, u32[]{:S(2)}) copy-start(f32[1536,48]{0,1:T(8,128)} %param.36) | copy-start | bytes 884740
  230.0 74.5 %copy-start.34 = (f32[1536,48]{0,1:T(8,128)S(1)}, f32[1536,48]{0,1:T(8,128)}, u32[]{:S(2)}) copy-start(f32[1536,48]{0,1:T(8,128)} %param.46) | copy-start | bytes 884740
  230.0 74.5 %copy-start.35 = (f32[1536,48]{0,1:T(8,128)S(1)}, f32[1536,48]{0,1:T(8,128)}, u32[]{:S(2)}) copy-start(f32[1536,48]{0,1:T(8,128)} %param.47) | copy-start | bytes 884740
  230.0 77.5 %copy-start.30 = (f32[2,64,1,384]{3,1,2,0:T(8,128)S(1)}, f32[2,64,1,384]{3,1,2,0:T(8,128)}, u32[]{:S(2)}) copy-start(f32[2,64,1,384]{3,1,2,0:T(8,128)} %get-tuple-element.494) | copy-start | bytes 589828
  230.0 118.8 %all-gather.16.cloned.1.call-start = ((), (), s32[]{:S(2)}) async-start(), calls=%async_computation.9 | async-start | bytes 2506752 | tf_op jit(solution)/shard_map/all_gather | solution.py:235
  306.6 85.8 %all-gather.18.cloned.1.call-start = ((), (), s32[]{:S(2)}) async-start(), calls=%async_computation.11 | async-start | bytes 1671168 | tf_op jit(solution)/shard_map/all_gather | solution.py:340
  307.3 112.0 %all-reduce.8.cloned.1.call-start = ((), (), s32[]{:S(2)}) async-start(), calls=%async_computation.10 | async-start | bytes 786432 | tf_op jit(solution)/shard_map/psum | solution.py:301
  307.6 45.4 %copy-start.9 = (bf16[768,1536]{1,0:T(8,128)(2,1)S(1)}, bf16[768,1536]{1,0:T(8,128)(2,1)}, u32[]{:S(2)}) copy-start(bf16[768,1536]{1,0:T(8,128)(2,1)} %all-gather.14.cloned.1.call-done) | copy-start | bytes 7077892
  354.7 112.0 %all-gather.20.cloned.1.call-start = ((), (), s32[]{:S(2)}) async-start(), calls=%async_computation.12 | async-start | bytes 1671168 | tf_op jit(solution)/shard_map/all_gather | solution.py:343
  398.4 24.9 %copy-start.17 = (bf16[2,64,768]{2,1,0:T(8,128)(2,1)S(1)}, bf16[2,64,768]{2,1,0:T(8,128)(2,1)}, u32[]{:S(2)}) copy-start(bf16[2,64,768]{2,1,0:T(8,128)(2,1)} %param.31) | copy-start | bytes 589828
  398.4 25.6 %copy-start.11 = (bf16[384,768]{0,1:T(8,128)(2,1)S(1)}, bf16[384,768]{0,1:T(8,128)(2,1)}, u32[]{:S(2)}) copy-start(bf16[384,768]{0,1:T(8,128)(2,1)} %all_gather.37) | copy-start | bytes 1769476
  424.9 97.8 %all-reduce.10.cloned.1.call-start = ((), (), s32[]{:S(2)}) async-start(), calls=%async_computation.19 | async-start | bytes 1572864 | tf_op jit(solution)/shard_map/psum | solution.py:292
  487.9 34.8 %copy-start.8 = (bf16[2,64,768]{2,1,0:T(8,128)(2,1)S(1)}, bf16[2,64,768]{2,1,0:T(8,128)(2,1)}, u32[]{:S(2)}) copy-start(bf16[2,64,768]{2,1,0:T(8,128)(2,1)} %param.30) | copy-start | bytes 589828
  487.9 34.8 %copy-start.49 = (f32[2,64]{1,0:T(2,128)S(1)}, f32[2,64]{1,0:T(2,128)}, u32[]{:S(2)}) copy-start(f32[2,64]{1,0:T(2,128)} %copy-done.48) | copy-start | bytes 1540
  488.0 36.0 %copy-start.69 = (f32[2,64]{1,0:T(2,128)S(1)}, f32[2,64]{1,0:T(2,128)}, u32[]{:S(2)}) copy-start(f32[2,64]{1,0:T(2,128)} %copy-done.68) | copy-start | bytes 1540
  488.0 36.0 %copy-start.57 = (f32[2,64]{1,0:T(2,128)S(1)}, f32[2,64]{1,0:T(2,128)}, u32[]{:S(2)}) copy-start(f32[2,64]{1,0:T(2,128)} %copy-done.56) | copy-start | bytes 1540
  488.0 96.3 %reduce-scatter.10.cloned.1.call-start = ((), (), s32[]{:S(2)}) async-start(), calls=%async_computation.14 | async-start | bytes 1253376 | tf_op jit(solution)/shard_map/reduce_scatter | solution.py:383
  489.5 35.8 %copy-start.1 = (f32[2,64,768]{2,1,0:T(8,128)S(1)}, f32[2,64,768]{2,1,0:T(8,128)}, u32[]{:S(2)}) copy-start(f32[2,64,768]{2,1,0:T(8,128)} %copy-done) | copy-start | bytes 1179652
  489.5 35.8 %copy-start.13 = (f32[2,64,768]{2,1,0:T(8,128)S(1)}, f32[2,64,768]{2,1,0:T(8,128)}, u32[]{:S(2)}) copy-start(f32[2,64,768]{2,1,0:T(8,128)} %copy-done.12) | copy-start | bytes 1179652
  489.5 35.8 %copy-start.18 = (bf16[2,64,768]{2,1,0:T(8,128)(2,1)S(1)}, bf16[2,64,768]{2,1,0:T(8,128)(2,1)}, u32[]{:S(2)}) copy-start(bf16[2,64,768]{2,1,0:T(8,128)(2,1)} %param.31) | copy-start | bytes 589828
  489.5 35.8 %copy-start.63 = (f32[768]{0:T(1024)S(1)}, f32[768]{0:T(1024)}, u32[]{:S(2)}) copy-start(f32[768]{0:T(1024)} %get-tuple-element.383) | copy-start | bytes 9220
  489.5 35.8 %copy-start.67 = (f32[2,64]{1,0:T(2,128)S(1)}, f32[2,64]{1,0:T(2,128)}, u32[]{:S(2)}) copy-start(f32[2,64]{1,0:T(2,128)} %copy-done.66) | copy-start | bytes 1540
  489.5 155.5 %reduce-scatter.16.cloned.1.call-start = ((), (), s32[]{:S(2)}) async-start(), calls=%async_computation.18 | async-start | bytes 417792
  528.6 192.7 %reduce-scatter.12.cloned.1.call-start = ((), (), s32[]{:S(2)}) async-start(), calls=%async_computation.15 | async-start | bytes 5013504 | tf_op jit(solution)/shard_map/reduce_scatter | solution.py:382
  531.8 260.3 %reduce-scatter.8.cloned.1.call-start = ((), (), s32[]{:S(2)}) async-start(), calls=%async_computation.13 | async-start | bytes 3760128 | tf_op jit(solution)/shard_map/reduce_scatter | solution.py:381
  535.0 49.4 %copy-start.37 = (f32[384,48]{0,1:T(8,128)S(1)}, f32[384,48]{0,1:T(8,128)}, u32[]{:S(2)}) copy-start(f32[384,48]{0,1:T(8,128)} %param.34) | copy-start | bytes 221188
  535.0 49.4 %copy-start.46 = (f32[384,48]{0,1:T(8,128)S(1)}, f32[384,48]{0,1:T(8,128)}, u32[]{:S(2)}) copy-start(f32[384,48]{0,1:T(8,128)} %param.42) | copy-start | bytes 221188
  535.0 49.4 %copy-start.47 = (f32[384,48]{0,1:T(8,128)S(1)}, f32[384,48]{0,1:T(8,128)}, u32[]{:S(2)}) copy-start(f32[384,48]{0,1:T(8,128)} %param.43) | copy-start | bytes 221188
  535.0 51.0 %copy-start.72 = (f32[1536]{0:T(1024)S(1)}, f32[1536]{0:T(1024)}, u32[]{:S(2)}) copy-start(f32[1536]{0:T(1024)} %get-tuple-element.501) | copy-start | bytes 18436
  535.0 108.8 %copy-start.65 = (f32[2,384]{1,0:T(2,128)S(1)}, f32[2,384]{1,0:T(2,128)}, u32[]{:S(2)}) copy-start(f32[2,384]{1,0:T(2,128)} %param.37) | copy-start | bytes 9220
  535.0 108.8 %copy-start.76 = (f32[2,384]{1,0:T(2,128)S(1)}, f32[2,384]{1,0:T(2,128)}, u32[]{:S(2)}) copy-start(f32[2,384]{1,0:T(2,128)} %param.48) | copy-start | bytes 9220
  535.0 108.8 %copy-start.77 = (f32[2,384]{1,0:T(2,128)S(1)}, f32[2,384]{1,0:T(2,128)}, u32[]{:S(2)}) copy-start(f32[2,384]{1,0:T(2,128)} %param.49) | copy-start | bytes 9220
  535.0 109.4 %copy-start.45 = (f32[1536]{0:T(1024)S(1)}, f32[1536]{0:T(1024)}, u32[]{:S(2)}) copy-start(f32[1536]{0:T(1024)} %param.38) | copy-start | bytes 18436
  535.1 109.4 %copy-start.70 = (f32[1536]{0:T(1024)S(1)}, f32[1536]{0:T(1024)}, u32[]{:S(2)}) copy-start(f32[1536]{0:T(1024)} %param.50) | copy-start | bytes 18436
  535.1 109.4 %copy-start.71 = (f32[1536]{0:T(1024)S(1)}, f32[1536]{0:T(1024)}, u32[]{:S(2)}) copy-start(f32[1536]{0:T(1024)} %param.51) | copy-start | bytes 18436
  535.1 110.8 %copy-start.64 = (f32[6,48]{1,0:T(8,128)S(1)}, f32[6,48]{1,0:T(8,128)}, u32[]{:S(2)}) copy-start(f32[6,48]{1,0:T(8,128)} %param.39) | copy-start | bytes 3460
  535.1 110.8 %copy-start.73 = (f32[6,48]{1,0:T(8,128)S(1)}, f32[6,48]{1,0:T(8,128)}, u32[]{:S(2)}) copy-start(f32[6,48]{1,0:T(8,128)} %param.52) | copy-start | bytes 3460
  535.1 110.8 %copy-start.74 = (f32[6,48]{1,0:T(8,128)S(1)}, f32[6,48]{1,0:T(8,128)}, u32[]{:S(2)}) copy-start(f32[6,48]{1,0:T(8,128)} %param.53) | copy-start | bytes 3460
  535.1 186.1 %copy-start.25 = (f32[48,1536]{1,0:T(8,128)S(1)}, f32[48,1536]{1,0:T(8,128)}, u32[]{:S(2)}) copy-start(f32[48,1536]{1,0:T(8,128)} %param.35) | copy-start | bytes 884740
  535.2 186.1 %copy-start.38 = (f32[48,1536]{1,0:T(8,128)S(1)}, f32[48,1536]{1,0:T(8,128)}, u32[]{:S(2)}) copy-start(f32[48,1536]{1,0:T(8,128)} %param.44) | copy-start | bytes 884740
  535.2 186.1 %copy-start.39 = (f32[48,1536]{1,0:T(8,128)S(1)}, f32[48,1536]{1,0:T(8,128)}, u32[]{:S(2)}) copy-start(f32[48,1536]{1,0:T(8,128)} %param.45) | copy-start | bytes 884740
  586.0 206.1 %copy-start.28 = (f32[48,3,384]{2,0,1:T(8,128)S(1)}, f32[48,3,384]{2,0,1:T(8,128)}, u32[]{:S(2)}) copy-start(f32[48,3,384]{2,0,1:T(8,128)} %param.33) | copy-start | bytes 663556
  586.0 206.1 %copy-start.40 = (f32[48,3,384]{2,0,1:T(8,128)S(1)}, f32[48,3,384]{2,0,1:T(8,128)}, u32[]{:S(2)}) copy-start(f32[48,3,384]{2,0,1:T(8,128)} %param.40) | copy-start | bytes 663556
  586.0 206.1 %copy-start.41 = (f32[48,3,384]{2,0,1:T(8,128)S(1)}, f32[48,3,384]{2,0,1:T(8,128)}, u32[]{:S(2)}) copy-start(f32[48,3,384]{2,0,1:T(8,128)} %param.41) | copy-start | bytes 663556
  (31 other events, 59.3 us)
Sparse Core Ops, SparseCore 0:
  10.9 43.1 all-gather.9
  57.1 39.0 all-gather.11
  99.1 38.5 all-gather.21
  153.9 24.6 all-reduce.5
  181.5 42.3 all-gather.13
  230.1 74.3 reduce-scatter.13
  307.4 41.3 all-gather.15
  351.7 40.7 all-gather.17
  394.7 24.6 all-reduce.7
  425.0 41.6 all-gather.19
  488.1 34.5 all-reduce.9
  526.2 58.0 reduce-scatter.9
  587.8 54.5 reduce-scatter.15
  646.6 74.5 reduce-scatter.11
  725.0 67.0 reduce-scatter.7
where the time goes:
time: 802 us; the launch traced here: 800 us
  waiting for transfers between devices  516 us (64%)
  blocking collectives  152 us (19%)
  matrix products  43.6 us (5%)
  local copies, waits for them, and re-layouts  43.5 us (5%)
  other arithmetic  29.8 us (4%)
  between operations  14.8 us (2%)
    reduce_scatter x1, waiting for transfers between devices, local(): lax.psum_scatter(grad_up, 'ctx', scatter_dimension=0, tiled=True)  74.8 us
    reduce_scatter x1, waiting for transfers between devices, local(): lax.psum_scatter(grad_down, 'ctx', scatter_dimension=1, tiled=True)  74.4 us
    reduce_scatter x1, waiting for transfers between devices, local(): lax.psum_scatter(grad_qkv, 'ctx', scatter_dimension=0, tiled=True)  68.8 us
    psum x1, blocking collectives, local(): sum_qbias, sum_upbias = lax.psum((grad_qbias, grad_upbias), 'ctx')  57.7 us
    reduce_scatter x1, waiting for transfers between devices, local(): lax.psum_scatter(grad_proj, 'ctx', scatter_dimension=1, tiled=True)  49.2 us
    all_gather x1, waiting for transfers between devices, local(): lax.all_gather(up_weight.astype(jnp.bfloat16), 'ctx', axis=0, tiled=True)  43.9 us
    all_gather x1, waiting for transfers between devices, local(): lax.all_gather(down_weight.astype(jnp.bfloat16), 'ctx', axis=1, tiled=True)  41.2 us
    all_gather x1, waiting for transfers between devices, local(): lax.all_gather(keys, 'ctx', axis=1, tiled=True)  38.9 us
  transfers between devices with their start and end apart: 15, of which 14 were waited for; matrix products, arithmetic and copies ran while one was open for 7% of the time, Pallas kernels for 0%

commit v1 on v0

--- a/solution.py
+++ b/solution.py
@@ -4,10 +4,15 @@
 import jax
 import jax.numpy as jnp
 from jax import lax
+from jax.experimental import pallas as pl
+from jax.experimental.pallas import tpu as pltpu
 from jax.sharding import PartitionSpec as P
 
 HD = 64
 STEP = 10
+WIDTH = 768
+MESH = pl.DeviceIdType.MESH
+VMEM_LIMIT = 48 * 1024 * 1024
 
 
 BETA_ONE = 0.9
@@ -419,9 +424,544 @@
     )
 
 
+def chip_at(place, chips):
+    half = chips // 2
+    back = place // half
+    return (1 - back) * 2 * place + back * (2 * (chips - 1 - place) + 1)
+
+
+class Ring:
+    def __init__(self, chips):
+        me = lax.axis_index("ctx")
+        self.chips, self.me = chips, me
+        self.core = me % 2
+        chip = me // 2
+        along, across = chip // 2, chip % 2
+        self.place = along + across * (chips - 1 - 2 * along)
+        self.right, self.left = self.slot(1), self.slot(-1)
+        self.mate = chip * 2 + 1 - self.core
+
+    def slot(self, ahead, other=False):
+        place = (self.place + ahead + 2 * self.chips) % self.chips
+        core = 1 - self.core if other else self.core
+        return chip_at(place, self.chips) * 2 + core
+
+    def greet(self):
+        barrier = pltpu.get_barrier_semaphore()
+        for device in (self.left, self.right, self.mate):
+            pl.semaphore_signal(barrier, inc=1, device_id={"ctx": device}, device_id_type=MESH)
+        pl.semaphore_wait(barrier, 3)
+
+
+def remote(src, dst, send, recv, device):
+    return pltpu.make_async_remote_copy(
+        src_ref=src,
+        dst_ref=dst,
+        send_sem=send,
+        recv_sem=recv,
+        device_id={"ctx": device},
+        device_id_type=MESH,
+    )
+
+
+class Gather:
+    def __init__(self, ring, ins, outs, sems):
+        self.ring, self.ins, self.outs = ring, ins, outs
+        self.ring_send, self.ring_recv, self.mate_send, self.mate_recv, self.own = sems
+        self.far_right = ring.chips // 2
+        self.far_left = ring.chips - 1 - self.far_right
+        self.sent = []
+
+    def hop(self, at, src, slot, index, device):
+        copy = remote(
+            src, self.outs[at].at[slot], self.ring_send.at[at, index],
+            self.ring_recv.at[at, index], device,
+        )
+        return copy
+
+    def pass_on(self, at, src, slot, index):
+        copy = remote(
+            src, self.outs[at].at[slot], self.mate_send.at[at, index],
+            self.mate_recv.at[at, index], self.ring.mate,
+        )
+        return copy
+
+    def go(self, copy):
+        copy.start()
+        self.sent.append(copy)
+
+    def start(self):
+        ring = self.ring
+        for at, block in enumerate(self.ins):
+            self.go(self.hop(at, block, ring.me, 0, ring.right))
+            self.go(self.hop(at, block, ring.me, self.far_right, ring.left))
+            self.go(self.pass_on(at, block, ring.me, 0))
+            pltpu.make_async_copy(block, self.outs[at].at[ring.me], self.own.at[at]).start()
+
+    def step(self, step):
+        ring = self.ring
+        for at in range(len(self.ins)):
+            for sign, far, base, device in (
+                (-1, self.far_right, 0, ring.right),
+                (1, self.far_left, self.far_right, ring.left),
+            ):
+                if step >= far:
+                    continue
+                slot = ring.slot(sign * (step + 1))
+                block = self.outs[at].at[slot]
+                self.hop(at, block, slot, base + step, device).wait_recv()
+                if step + 1 < far:
+                    self.go(self.hop(at, block, slot, base + step + 1, device))
+                self.go(self.pass_on(at, block, slot, 1 + base + step))
+
+    def finish(self):
+        ring = self.ring
+        for at in range(len(self.ins)):
+            order = [0] + [-(s + 1) for s in range(self.far_right)]
+            order += [s + 1 for s in range(self.far_left)]
+            for index, ahead in enumerate(order):
+                slot = ring.slot(ahead, other=True)
+                self.pass_on(at, self.outs[at].at[slot], slot, index).wait_recv()
+            pltpu.make_async_copy(
+                self.ins[at], self.outs[at].at[ring.me], self.own.at[at]
+            ).wait()
+        for copy in self.sent:
+            copy.wait_send()
+
+
+def gather_sems(count, chips):
+    return [pltpu.SemaphoreType.DMA((count, chips))] * 4 + [pltpu.SemaphoreType.DMA((count,))]
+
+
+def gather_kernel(chips, count, *refs):
+    ins, outs, sems = refs[:count], refs[count : 2 * count], refs[2 * count :]
+    ring = Ring(chips)
+    ring.greet()
+    gather = Gather(ring, ins, outs, sems)
+    gather.start()
+    for step in range(gather.far_right):
+        gather.step(step)
+    gather.finish()
+
+
+def ring_gather(arrays, groups, collective):
+    count, chips = len(arrays), groups // 2
+    return pl.pallas_call(
+        partial(gather_kernel, chips, count),
+        out_shape=[jax.ShapeDtypeStruct((groups,) + a.shape, a.dtype) for a in arrays],
+        in_specs=[pl.BlockSpec(memory_space=pl.ANY)] * count,
+        out_specs=[pl.BlockSpec(memory_space=pl.ANY)] * count,
+        scratch_shapes=gather_sems(count, chips),
+        compiler_params=pltpu.CompilerParams(collective_id=collective, has_side_effects=True),
+    )(*arrays)
+
+
+def scatter_kernel(chips, pieces, *refs):
+    grads, small = refs[0:4], refs[4]
+    outs, small_out = refs[5:9], refs[9]
+    mates, lands = refs[10:14], refs[14 : 14 + len(pieces)]
+    rest = refs[14 + len(pieces) :]
+    mate_send, mate_recv, ring_send, ring_recv = rest[:4]
+    ring = Ring(chips)
+    ring.greet()
+    order = []
+    for far in range(1, chips // 2):
+        order += [-far, far]
+    order += [chips // 2, 0]
+    sent = []
+
+    def to_mate(index, at):
+        ahead = order[index]
+        return remote(
+            grads[at].at[ring.slot(ahead, other=True)], mates[at].at[index],
+            mate_send.at[at, index], mate_recv.at[at, index], ring.mate,
+        )
+
+    arrived = set()
+
+    def own_part(ahead, at, columns):
+        ahead = (ahead + chips // 2 - 1) % chips - (chips // 2 - 1)
+        index = order.index(ahead)
+        if (index, at) not in arrived:
+            arrived.add((index, at))
+            to_mate(index, at).wait_recv()
+        mine = grads[at][ring.slot(ahead), :, columns].astype(jnp.float32)
+        return mine + mates[at][index, :, columns].astype(jnp.float32)
+
+    for index in range(chips):
+        for at in range(4):
+            copy = to_mate(index, at)
+            copy.start()
+            sent.append(copy)
+    gather = Gather(ring, [small], [small_out], rest[4:])
+    gather.start()
+
+    def hop(which, step, src):
+        device = ring.right if pieces[which][3] > 0 else ring.left
+        return remote(
+            src, lands[which].at[step], ring_send.at[which, step],
+            ring_recv.at[which, step], device,
+        )
+
+    for step in range(chips):
+        for which, (at, first, count, sign) in enumerate(pieces):
+            columns = slice(first, first + count)
+            part = own_part(-sign * (step + 1), at, columns)
+            if step > 0:
+                hop(which, step - 1, lands[which].at[step]).wait_recv()
+                part = part + lands[which][step - 1].astype(jnp.float32)
+            if step < chips - 1:
+                hold = lands[which].at[chips - 1 + step]
+                hold[...] = part.astype(jnp.bfloat16)
+                copy = hop(which, step, hold)
+                copy.start()
+                sent.append(copy)
+            else:
+                outs[at][:, columns] = part
+        if step < gather.far_right:
+            gather.step(step)
+    gather.finish()
+    for copy in sent:
+        copy.wait_send()
+
+
+def ring_scatter(grads, small, groups, collective):
+    chips = groups // 2
+    blocks = [g.reshape(groups, g.shape[0] // groups, g.shape[1]) for g in grads]
+    rows = blocks[0].shape[1]
+    qkv, proj, up, down = [b.shape[2] for b in blocks]
+    right_up = up * 3 // 4 // 128 * 128
+    pieces = (
+        (0, 0, qkv, 1),
+        (3, 0, down, -1),
+        (2, 0, right_up, 1),
+        (1, 0, proj, -1),
+        (2, right_up, up - right_up, -1),
+    )
+    vmem = pl.BlockSpec(memory_space=pltpu.VMEM)
+    hbm = pl.BlockSpec(memory_space=pl.ANY)
+    dma = pltpu.SemaphoreType.DMA
+    return pl.pallas_call(
+        partial(scatter_kernel, chips, pieces),
+        out_shape=[jax.ShapeDtypeStruct(b.shape[1:], jnp.float32) for b in blocks]
+        + [jax.ShapeDtypeStruct((groups,) + small.shape, small.dtype)],
+        in_specs=[vmem] * 4 + [hbm],
+        out_specs=[vmem] * 4 + [hbm],
+        scratch_shapes=[pltpu.VMEM((chips, rows, b.shape[2]), jnp.bfloat16) for b in blocks]
+        + [pltpu.VMEM((2 * chips - 2, rows, p[2]), jnp.bfloat16) for p in pieces]
+        + [dma((4, chips)), dma((4, chips))]
+        + [dma((len(pieces), chips)), dma((len(pieces), chips))]
+        + gather_sems(1, chips),
+        compiler_params=pltpu.CompilerParams(
+            collective_id=collective, has_side_effects=True, vmem_limit_bytes=VMEM_LIMIT
+        ),
+    )(*blocks, small)
+
+
+def pair_kernel(count, *refs):
+    ins, outs = refs[:count], refs[count : 2 * count]
+    holds, lands = refs[2 * count : 3 * count], refs[3 * count : 4 * count]
+    send, recv = refs[4 * count :]
+    other = 1 - lax.axis_index("tp")
+    barrier = pltpu.get_barrier_semaphore()
+    pl.semaphore_signal(barrier, inc=1, device_id={"tp": other}, device_id_type=MESH)
+    for at in range(count):
+        holds[at][...] = ins[at][...].astype(jnp.bfloat16)
+    pl.semaphore_wait(barrier, 1)
+    copies = []
+    for at in range(count):
+        copy = pltpu.make_async_remote_copy(
+            src_ref=holds[at], dst_ref=lands[at], send_sem=send.at[at], recv_sem=recv.at[at],
+            device_id={"tp": other}, device_id_type=MESH,
+        )
+        copy.start()
+        copies.append(copy)
+    for at in range(count):
+        copies[at].wait()
+        outs[at][...] = holds[at][...].astype(jnp.float32) + lands[at][...].astype(jnp.float32)
+
+
+def pair_sum(arrays, collective):
+    count = len(arrays)
+    vmem = pl.BlockSpec(memory_space=pltpu.VMEM)
+    return pl.pallas_call(
+        partial(pair_kernel, count),
+        out_shape=[jax.ShapeDtypeStruct(a.shape, jnp.float32) for a in arrays],
+        in_specs=[vmem] * count,
+        out_specs=[vmem] * count,
+        scratch_shapes=[pltpu.VMEM(a.shape, jnp.bfloat16) for a in arrays] * 2
+        + [pltpu.SemaphoreType.DMA((count,))] * 2,
+        compiler_params=pltpu.CompilerParams(
+            collective_id=collective, has_side_effects=True, vmem_limit_bytes=VMEM_LIMIT
+        ),
+    )(*arrays)
+
+
+NT = (((1,), (1,)), ((), ()))
+NN = (((1,), (0,)), ((), ()))
+
+
+def mul(left, right, dims):
+    return lax.dot_general(left, right, dims, preferred_element_type=jnp.float32)
+
+
+def attend_kernel(heads, q_ref, kv_ref, own_ref, all_ref, context_ref, log_ref):
+    seqs = own_ref.shape[0]
+    rows = q_ref.shape[0] // seqs
+    width = heads * HD
+    lanes = lax.broadcasted_iota(jnp.int32, (rows, 128), 1)
+    for seq in range(seqs):
+        here = slice(seq * rows, (seq + 1) * rows)
+        allowed = own_ref[seq] >= all_ref[seq]
+        logs = jnp.zeros((rows, 128), jnp.float32)
+        for head in range(heads):
+            at = slice(head * HD, (head + 1) * HD)
+            past = slice(width + head * HD, width + (head + 1) * HD)
+            keys = kv_ref[:, here, at].reshape(-1, HD)
+            values = kv_ref[:, here, past].reshape(-1, HD)
+            scores = mul(q_ref[here, at], keys, NT) * 0.125
+            scores = jnp.where(allowed, scores, -1000000000.0)
+            top = jnp.max(scores, axis=-1, keepdims=True)
+            shares = jnp.exp(scores - top)
+            total = jnp.sum(shares, axis=-1, keepdims=True)
+            mixed = mul(shares.astype(jnp.bfloat16), values, NN)
+            context_ref[here, at] = mixed / total
+            logs = jnp.where(lanes == head, top + jnp.log(total), logs)
+        log_ref[here, :] = logs
+
+
+def attend(queries, pairs, own_pos, all_pos, heads):
+    vmem = pl.BlockSpec(memory_space=pltpu.VMEM)
+    return pl.pallas_call(
+        partial(attend_kernel, heads),
+        out_shape=[
+            jax.ShapeDtypeStruct(queries.shape, jnp.float32),
+            jax.ShapeDtypeStruct((queries.shape[0], 128), jnp.float32),
+        ],
+        in_specs=[vmem] * 4,
+        out_specs=[vmem] * 2,
+        compiler_params=pltpu.CompilerParams(vmem_limit_bytes=VMEM_LIMIT),
+    )(queries, pairs, own_pos, all_pos)
+
+
+def attend_back_kernel(
+    heads, qg_ref, stat_ref, kv_ref, qgs_ref, stats_ref, own_ref, all_ref, out_ref
+):
+    seqs = own_ref.shape[0]
+    rows = qg_ref.shape[0] // seqs
+    width = heads * HD
+    me = lax.axis_index("ctx")
+    for seq in range(seqs):
+        here = slice(seq * rows, (seq + 1) * rows)
+        allowed = own_ref[seq] >= all_ref[seq]
+        allowed_back = own_ref[seq] <= all_ref[seq]
+        turned = stats_ref[:, here, :].reshape(-1, 128).T
+        for head in range(heads):
+            at = slice(head * HD, (head + 1) * HD)
+            past = slice(width + head * HD, width + (head + 1) * HD)
+            keys = kv_ref[:, here, at].reshape(-1, HD)
+            values = kv_ref[:, here, past].reshape(-1, HD)
+            scores = jnp.where(allowed, mul(qg_ref[here, at], keys, NT) * 0.125, -1000000000.0)
+            shares = jnp.exp(scores - stat_ref[here, head : head + 1])
+            grad_share = mul(qg_ref[here, past], values, NT)
+            delta = stat_ref[here, heads + head : heads + head + 1]
+            grad_score = (shares * (grad_share - delta)).astype(jnp.bfloat16)
+            out_ref[here, at] = (mul(grad_score, keys, NN) * 0.125).astype(jnp.bfloat16)
+            queries = qgs_ref[:, here, at].reshape(-1, HD)
+            grads = qgs_ref[:, here, past].reshape(-1, HD)
+            key, value = kv_ref[me, here, at], kv_ref[me, here, past]
+            scores = jnp.where(allowed_back, mul(key, queries, NT) * 0.125, -1000000000.0)
+            shares = jnp.exp(scores - turned[head : head + 1])
+            grad_value = mul(shares.astype(jnp.bfloat16), grads, NN)
+            grad_share = mul(value, grads, NT)
+            grad_score = shares * (grad_share - turned[heads + head : heads + head + 1])
+            grad_key = mul(grad_score.astype(jnp.bfloat16), queries, NN) * 0.125
+            out_ref[here, past] = grad_key.astype(jnp.bfloat16)
+            last = slice(2 * width + head * HD, 2 * width + (head + 1) * HD)
+            out_ref[here, last] = grad_value.astype(jnp.bfloat16)
+
+
+def attend_back(own, stats, pairs, all_own, all_stats, own_pos, all_pos, heads):
+    vmem = pl.BlockSpec(memory_space=pltpu.VMEM)
+    return pl.pallas_call(
+        partial(attend_back_kernel, heads),
+        out_shape=jax.ShapeDtypeStruct((own.shape[0], 3 * heads * HD), jnp.bfloat16),
+        in_specs=[vmem] * 7,
+        out_specs=vmem,
+        compiler_params=pltpu.CompilerParams(vmem_limit_bytes=VMEM_LIMIT),
+    )(own, stats, pairs, all_own, all_stats, own_pos, all_pos)
+
+
+def three_parts(array):
+    high = lax.reduce_precision(array, 8, 7)
+    rest = array - high
+    middle = lax.reduce_precision(rest, 8, 7)
+    return [part.astype(jnp.bfloat16) for part in (high, middle, rest - middle)]
+
+
+def ring_local(
+    tokens,
+    out_grad,
+    block_order,
+    qkv_weight,
+    proj_weight,
+    up_weight,
+    down_weight,
+    qkv_bias,
+    up_bias,
+    layer_vectors,
+    qkv_first,
+    qkv_second,
+    proj_first,
+    proj_second,
+    up_first,
+    up_second,
+    down_first,
+    down_second,
+    qbias_first,
+    qbias_second,
+    ubias_first,
+    ubias_second,
+    vector_first,
+    vector_second,
+):
+    device = lax.axis_index("ctx")
+    groups = lax.axis_size("ctx")
+    seqs, rows, width = tokens.shape
+    blk = rows // 2
+    share = qkv_weight.shape[0]
+    inner = qkv_weight.shape[2]
+    heads = inner // HD
+    many = seqs * rows
+    own_pos = block_positions(block_order, device * rows, rows, blk)[:, :, None]
+    all_pos = block_positions(block_order, 0, rows * groups, blk)[:, None, :]
+    low = jnp.bfloat16
+    vector_parts = jnp.concatenate(three_parts(layer_vectors.T), axis=1)
+    packed = jnp.concatenate(
+        [
+            qkv_weight.astype(low).reshape(share, 3 * inner),
+            jnp.pad(vector_parts, ((0, 0), (0, 128 - vector_parts.shape[1]))),
+        ],
+        axis=1,
+    )
+    packed_full, proj_full, up_full, down_full = ring_gather(
+        [packed, proj_weight.astype(low).T, up_weight.astype(low), down_weight.astype(low).T],
+        groups,
+        1,
+    )
+    packed_full = packed_full.reshape(width, -1)
+    qkv_full = packed_full[:, : 3 * inner]
+    vectors = packed_full[:, 3 * inner : 3 * inner + 18].astype(jnp.float32).T
+    vectors = (vectors[0:6] + vectors[6:12]) + vectors[12:18]
+    proj_full = proj_full.reshape(width, -1)
+    up_full = up_full.reshape(width, -1)
+    down_full = down_full.reshape(width, -1)
+    inputs = tokens.reshape(many, width).astype(jnp.float32)
+    grad_low = out_grad.reshape(many, width)
+    first_normalized, norm_one_back = jax.vjp(layer_norm, inputs, vectors[0], vectors[1])
+    normed_low = first_normalized.astype(low)
+    projected = mul(normed_low, qkv_full, NN)
+    bias = jnp.concatenate([qkv_bias[0], jnp.zeros_like(qkv_bias[0]), qkv_bias[1]])
+    projected = (projected + bias).astype(low)
+    queries = projected[:, :inner]
+    (pairs,) = ring_gather([projected[:, inner:]], groups, 2)
+    context, logs = attend(queries, pairs, own_pos, all_pos, heads)
+    context_low = context.astype(low)
+    (attn,) = pair_sum([mul(context_low, proj_full, NT)], 3)
+    middle = inputs + (attn + vectors[4])
+    second_normalized, norm_two_back = jax.vjp(layer_norm, middle, vectors[2], vectors[3])
+    normed_mid = second_normalized.astype(low)
+    hidden_preactivation = mul(normed_mid, up_full, NN) + up_bias
+    hidden_activation, gelu_back = jax.vjp(gelu_tanh, hidden_preactivation)
+    hidden_low = hidden_activation.astype(low)
+    grad_hidden = mul(grad_low, down_full, NN)
+    grad_pre = gelu_back(grad_hidden)[0].astype(low)
+    mlp, grad_normed_two = pair_sum(
+        [mul(hidden_low, down_full, NT), mul(grad_pre, up_full, NT)], 4
+    )
+    block_output = (middle + (mlp + vectors[5])).astype(low)
+    grad_out = grad_low.astype(jnp.float32)
+    grad_mid_norm, grad_gain_two, grad_shift_two = norm_two_back(grad_normed_two)
+    grad_middle = grad_out + grad_mid_norm
+    grad_attn = grad_middle.astype(low)
+    grad_context = mul(grad_attn, proj_full, NN).astype(low)
+    lanes = jnp.arange(128)[None, :]
+    choose = (lanes == heads + jnp.arange(inner)[:, None] // HD).astype(jnp.float32)
+    delta = jnp.dot(
+        grad_context.astype(jnp.float32) * context, choose, precision=lax.Precision.HIGHEST
+    )
+    stats = logs + delta
+    own = jnp.concatenate([queries, grad_context], axis=1)
+    all_own, all_stats = ring_gather([own, stats], groups, 5)
+    grad_low_qkv = attend_back(own, stats, pairs, all_own, all_stats, own_pos, all_pos, heads)
+    (grad_normed_one,) = pair_sum([mul(grad_low_qkv, qkv_full, NT)], 6)
+    grad_in_norm, grad_gain_one, grad_shift_one = norm_one_back(grad_normed_one)
+    input_grad = grad_middle + grad_in_norm
+
+    def turned(left, right):
+        return lax.dot_general(
+            left, right, (((0,), (0,)), ((), ())), preferred_element_type=jnp.float32
+        ).astype(low)
+
+    grad_qbias = jnp.sum(grad_low_qkv.astype(jnp.float32), axis=0)
+    small = jnp.concatenate(
+        [
+            grad_gain_one,
+            grad_shift_one,
+            grad_gain_two,
+            grad_shift_two,
+            jnp.sum(grad_attn.astype(jnp.float32), axis=0),
+            jnp.sum(grad_out, axis=0),
+            grad_qbias[:inner],
+            grad_qbias[2 * inner :],
+            jnp.sum(grad_pre.astype(jnp.float32), axis=0),
+        ]
+    ).reshape(-1, 128)
+    sum_qkv, sum_proj, sum_up, sum_down, all_small = ring_scatter(
+        [
+            turned(normed_low, grad_low_qkv),
+            turned(grad_attn, context_low),
+            turned(normed_mid, grad_pre),
+            turned(grad_low, hidden_low),
+        ],
+        small,
+        groups,
+        7,
+    )
+    sums = jnp.sum(all_small, axis=0).reshape(-1)
+    ends = 6 * width
+    sum_vectors = lax.dynamic_slice_in_dim(
+        sums[:ends].reshape(6, width), device * share, share, 1
+    )
+    sum_qbias = sums[ends : ends + 2 * inner].reshape(2, inner)
+    sum_upbias = sums[ends + 2 * inner :]
+    qkv_new = adamw(
+        qkv_weight, sum_qkv.reshape(share, 3, inner), qkv_first, qkv_second, 0.1, 0.1
+    )
+    proj_new = adamw(proj_weight, sum_proj.T, proj_first, proj_second, 1.0, 0.1)
+    up_new = adamw(up_weight, sum_up, up_first, up_second, 0.1, 0.1)
+    down_new = adamw(down_weight, sum_down.T, down_first, down_second, 0.05, 0.1)
+    qbias_new = adamw(qkv_bias, sum_qbias, qbias_first, qbias_second, 1.0, 0.0)
+    ubias_new = adamw(up_bias, sum_upbias, ubias_first, ubias_second, 1.0, 0.0)
+    vector_new = adamw(layer_vectors, sum_vectors, vector_first, vector_second, 1.0, 0.0)
+    return (
+        block_output.reshape(seqs, rows, width),
+        input_grad.reshape(seqs, rows, width),
+        *qkv_new,
+        *proj_new,
+        *up_new,
+        *down_new,
+        *qbias_new,
+        *ubias_new,
+        *vector_new,
+    )
+
+
 def solution(mesh):
+    groups = mesh.shape["ctx"]
+    tiled = groups % 4 == 0 and WIDTH % (groups * 16) == 0
     return jax.shard_map(
-        local,
+        ring_local if tiled else local,
         mesh=mesh,
         in_specs=(
             P(None, "ctx", None),

time: 802 us -> 228 us (0.28)
  waiting for transfers between devices: 516 us -> 0 us
  Pallas kernels: 0 us -> 186 us
  blocking collectives: 152 us -> 0 us
  local copies, waits for them, and re-layouts: 43.5 us -> 10.4 us
  matrix products: 43.6 us -> 12.1 us
  between operations: 14.8 us -> 1.73 us
  other arithmetic: 29.8 us -> 17.4 us
    reduce_scatter x4 -> x0, waiting for transfers between devices: 267 us -> none  [the longest x1 74.8 us: local(): lax.psum_scatter(grad_up, 'ctx', scatter_dimension=0, tiled=True)]
    pallas_call x0 -> x9, Pallas kernels: none -> 186 us  [the longest x3 101 us: ring_gather(): pl.pallas_call(partial(gather_kernel, chips, count), out_shape=[jax.Shape...]
    all_gather x7 -> x0, waiting for transfers between devices: 170 us -> none  [the longest x1 43.9 us: local(): lax.all_gather(up_weight.astype(jnp.bfloat16), 'ctx', axis=0, tiled=True)]
    all_gather x4 -> x0, blocking collectives: 93.9 us -> none  [the longest x1 25 us: local(): lax.all_gather(row_delta, 'ctx', axis=1, tiled=True)]
    psum x3 -> x0, waiting for transfers between devices: 78 us -> none  [the longest x1 33.1 us: local(): mlp_total = lax.psum(mlp_part, 'tp') + layer_vector_rows[5]]
    psum x1 -> x0, blocking collectives: 57.7 us -> none  [local(): sum_qbias, sum_upbias = lax.psum((grad_qbias, grad_upbias), 'ctx')]
    dot_general x26 -> x13, matrix products: 43.6 us -> 12.1 us  [the longest x8 6.98 us: mul(): lax.dot_general(left, right, dims, preferred_element_type=jnp.float32)]
    reshape x5 -> x3, local copies, waits for them, and re-layouts: 10.7 us -> 0.03 us  [the longest x1 0.01 us: ring_local(): qkv_weight.astype(low).reshape(share, 3 * inner)]
  transfers between devices with their start and end apart: 15 -> 0, of which waited for: 14 -> 0; matrix products, arithmetic and copies ran while one was open for 7% -> 0% of each run, Pallas kernels for 0% -> 0%
where the time goes in v1:
time: 228 us; the launch traced here: 227 us
  Pallas kernels  186 us (82%)
  other arithmetic  17.4 us (8%)
  matrix products  12.1 us (5%)
  local copies, waits for them, and re-layouts  10.4 us (5%)
    pallas_call x3, Pallas kernels, ring_gather(): pl.pallas_call(partial(gather_kernel, chips, count), out_shape=[jax.Shape...  101 us
    pallas_call x1, Pallas kernels, ring_scatter(): pl.pallas_call(partial(scatter_kernel, chips, pieces), out_shape=[jax.Sha...  43.4 us
    pallas_call x3, Pallas kernels, pair_sum(): pl.pallas_call(partial(pair_kernel, count), out_shape=[jax.ShapeDtypeStru...  25.4 us
    pallas_call x1, Pallas kernels, attend_back(): pl.pallas_call(partial(attend_back_kernel, heads), out_shape=jax.ShapeDty...  11.7 us
    unnamed x132, local copies, waits for them, and re-layouts  7.97 us
    dot_general x8, matrix products, mul(): lax.dot_general(left, right, dims, preferred_element_type=jnp.float32)  6.98 us
    sub x7, other arithmetic, adamw(): weight - rate * (first_hat / (jnp.sqrt(second_hat) + EPSILON) + decay * w...  5.67 us

profile of v1, /device:TPU:0, one launch (start us, length us, event | category | flops | bytes accessed | tf_op | source)
XLA Modules:
  0.0 227.3 jit_solution(4310525070366709246)
XLA Ops:
  0.7 0.8 dynamic-slice_multiply_fusion
  1.6 0.1 add.366
  1.7 0.1 add.301
  1.9 0.8 copy.65
  2.7 0.1 fusion.40
  2.8 0.9 convert_bitcast_fusion.1
  3.7 0.7 pad_maximum_fusion.1.refs_0_
  4.4 1.6 convert_bitcast_fusion.refs_3_
  6.0 1.6 convert_element_type.103.refs_2_
  7.7 1.5 convert_bitcast_fusion.3.refs_1_
  9.2 46.7 %shard_map.407 = (bf16[16,48,1280]{2,1,0:T(8,128)(2,1)}, bf16[16,48,384]{2,1,0:T(8,128)(2,1)}, bf16[16,48,1536]{2,1,0:T(8,128)(2,1)}, bf16[16,48,1536]{2,1,0:T(8,128)(2,1)}) custom-call(bf16[48,1280]{1,0:T(8,128)(2,1)} %pad_maximum_fusion.1.refs_0_, bf16[48,384]{1,0:T(8,128)(2,1)} %convert_bitcast_fusion.3.refs_1_, ...), custom_call_target="tpu_custom_call" | custom-call | tf_op jit(solution)/shard_map/pallas_call | solution.py:549
  55.9 0.9 slice.86
  56.9 0.1 copy.71
  57.1 0.1 convert_reduce_fusion.2
  57.2 0.2 fusion.20
  57.4 0.1 add.289
  57.5 0.1 div.160
  57.6 0.4 copy-done.49
  58.0 0.2 fusion.16
  58.3 1.9 fusion
  60.2 0.7 slice.94.refs_0_
  60.9 26.9 %shard_map.408.kv_ref = bf16[16,128,768]{2,1,0:T(8,128)(2,1)} custom-call(bf16[128,768]{1,0:T(8,128)(2,1)} %slice.94.refs_0_), custom_call_target="tpu_custom_call" | custom-call | tf_op jit(solution)/shard_map/pallas_call | solution.py:549
  87.9 0.1 add.305
  88.1 1.9 copy-done
  90.0 4.4 %shard_map.409 = (f32[128,384]{1,0:T(8,128)S(1)}, f32[128,128]{1,0:T(8,128)S(1)}) custom-call(bf16[128,384]{1,0:T(8,128)(2,1)S(1)} %slice.93.q_ref, bf16[16,128,768]{2,1,0:T(8,128)(2,1)S(1)} %copy-done, s32[2,64,1]{2,1,0:T(8,128)S(1)} %broadcast_add_fusion.own_ref, s32[2,1,1024]{2,1,0:T(1,128)S(1)} %broadcast_add_fusion.1.all_ref), custom_call_target="tpu_custom_call" | custom-call | tf_op jit(solution)/shard_map/pallas_call | solution.py:735
  94.5 0.3 fusion.33.refs_0_
  94.8 7.3 %shard_map.410 = f32[128,768]{1,0:T(8,128)S(1)} custom-call(f32[128,768]{1,0:T(8,128)S(1)} %fusion.33.refs_0_), custom_call_target="tpu_custom_call" | custom-call | tf_op jit(solution)/shard_map/pallas_call | solution.py:687
  102.1 0.1 fusion.64
  102.3 0.2 multiply_reduce_fusion.2
  102.5 0.5 convolution_add_fusion.1
  103.1 1.0 copy-done.58
  104.0 1.6 convert_reduce_fusion
  105.6 0.9 fusion.65.refs_1_
  106.5 0.9 fusion.50.refs_0_
  107.4 10.8 %shard_map.411 = (f32[128,768]{1,0:T(8,128)S(1)}, f32[128,768]{1,0:T(8,128)S(1)}) custom-call(f32[128,768]{1,0:T(8,128)S(1)} %fusion.50.refs_0_, f32[128,768]{1,0:T(8,128)S(1)} %fusion.65.refs_1_), custom_call_target="tpu_custom_call" | custom-call | tf_op jit(solution)/shard_map/pallas_call | solution.py:687
  118.2 0.2 multiply_reduce_fusion
  118.5 0.8 fusion.63
  119.3 0.1 convert_reduce_fusion.4
  119.4 0.4 copy-done.56
  119.8 0.3 convolution_convert_fusion.4
  120.1 1.0 convolution_add_fusion.2.refs_1_.stat_ref
  121.1 0.7 pad_maximum_fusion.refs_0_.qg_ref
  121.8 27.1 %shard_map.412 = (bf16[16,128,768]{2,1,0:T(8,128)(2,1)}, f32[16,128,128]{2,1,0:T(8,128)}) custom-call(bf16[128,768]{1,0:T(8,128)(2,1)} %pad_maximum_fusion.refs_0_.qg_ref, f32[128,128]{1,0:T(8,128)} %convolution_add_fusion.2.refs_1_.stat_ref), custom_call_target="tpu_custom_call" | custom-call | tf_op jit(solution)/shard_map/pallas_call | solution.py:549
  148.9 0.9 copy-done.4
  149.8 1.2 copy-done.5
  151.1 0.8 copy-done.6
  151.9 11.7 %shard_map.413 = bf16[128,1152]{1,0:T(8,128)(2,1)S(1)} custom-call(bf16[128,768]{1,0:T(8,128)(2,1)S(1)} %copy-done.4, f32[128,128]{1,0:T(8,128)S(1)} %copy-done.6, bf16[16,128,768]{2,1,0:T(8,128)(2,1)S(1)} %copy-done.1, bf16[16,128,768]{2,1,0:T(8,128)(2,1)} %get-tuple-element.46.qgs_ref, f32[16,128,128]{2,1,0:T(8,128)S(1)} %copy-done.5, ...), custom_call_target="tpu_custom_call" | custom-call | tf_op jit(solution)/shard_map/pallas_call | solution.py:786
  163.7 0.6 fusion.1.refs_0_
  164.3 7.3 %shard_map.414 = f32[128,768]{1,0:T(8,128)S(1)} custom-call(f32[128,768]{1,0:T(8,128)S(1)} %fusion.1.refs_0_), custom_call_target="tpu_custom_call" | custom-call | tf_op jit(solution)/shard_map/pallas_call | solution.py:687
  171.7 0.2 fusion.51
  172.0 0.3 fusion.17
  172.5 0.9 convolution_convert_fusion.1
  173.5 0.3 convolution_convert_fusion.3
  173.8 0.7 convolution_convert_fusion.2
  174.6 2.3 convolution_convert_fusion
  176.9 43.4 %shard_map.415 = (f32[48,1152]{1,0:T(8,128)S(1)}, f32[48,384]{1,0:T(8,128)S(1)}, f32[48,1536]{1,0:T(8,128)S(1)}, f32[48,1536]{1,0:T(8,128)S(1)}, f32[16,54,128]{2,1,0:T(8,128)S(1)}) custom-call(bf16[16,48,1152]{2,1,0:T(8,128)(2,1)S(1)} %bitcast.112, bf16[16,48,384]{2,1,0:T(8,128)(2,1)S(1)} %bitcast.113, bf16[16,48,1536]{2,1,0:T(8,128)(2,1)S(1)} %bitcast.111, ...), custom_call_target="tpu_custom_call" | custom-call | tf_op jit(solution)/shard_map/pallas_call | solution.py:644
  220.3 1.0 multiply_subtract_fusion
  221.5 1.0 multiply_subtract_fusion.1
  222.6 0.9 multiply_subtract_fusion.2
  223.5 0.7 add_subtract_fusion
  224.3 0.7 add_subtract_fusion.2
  225.0 0.6 add_subtract_fusion.1
  225.7 0.6 add_subtract_fusion.3
  226.3 1.0 add_add_fusion.2
  (159 shorter events, 1.1 us)
Async XLA Ops:
  0.7 56.4 %copy-start.9 = (bf16[2,64,768]{2,1,0:T(8,128)(2,1)S(1)}, bf16[2,64,768]{2,1,0:T(8,128)(2,1)}, u32[]{:S(2)}) copy-start(bf16[2,64,768]{2,1,0:T(8,128)(2,1)} %param.24) | copy-start | bytes 589828
  0.7 57.5 %copy-start.41 = (f32[2,384]{1,0:T(2,128)S(1)}, f32[2,384]{1,0:T(2,128)}, u32[]{:S(2)}) copy-start(f32[2,384]{1,0:T(2,128)} %param.31) | copy-start | bytes 9220
  57.5 0.7 copy-start.59
  57.5 0.5 copy-start.49
  58.0 29.8 %copy-start.42 = (f32[128]{0:T(128)}, f32[128]{0:T(128)S(1)}, u32[]{:S(2)}) copy-start(f32[128]{0:T(128)S(1)} %div.160) | copy-start | bytes 1540
  58.2 2.0 copy-start.27
  60.2 27.6 %copy-start.53 = (s32[2,32]{1,0:T(2,128)S(1)}, s32[2,32]{1,0:T(2,128)}, u32[]{:S(2)}) copy-start(s32[2,32]{1,0:T(2,128)} %param.26) | copy-start | bytes 772
  60.9 33.5 %copy-start.18 = (bf16[16,48,384]{2,1,0:T(8,128)(2,1)S(1)}, bf16[16,48,384]{2,1,0:T(8,128)(2,1)}, u32[]{:S(2)}) copy-start(bf16[16,48,384]{2,1,0:T(8,128)(2,1)} %get-tuple-element.40) | copy-start | bytes 1769476
  88.1 1.9 copy-start
  94.4 25.7 %copy-start.2 = (f32[128,384]{1,0:T(8,128)}, f32[128,384]{1,0:T(8,128)S(1)}, u32[]{:S(2)}) copy-start(f32[128,384]{1,0:T(8,128)S(1)} %get-tuple-element.39) | copy-start | bytes 589828
  94.4 8.1 %copy-start.11 = (bf16[16,48,1536]{2,1,0:T(8,128)(2,1)S(1)}, bf16[16,48,1536]{2,1,0:T(8,128)(2,1)}, u32[]{:S(2)}) copy-start(bf16[16,48,1536]{2,1,0:T(8,128)(2,1)} %get-tuple-element.41) | copy-start | bytes 7077892
  94.4 8.1 %copy-start.38 = (f32[1536]{0:T(1024)S(1)}, f32[1536]{0:T(1024)}, u32[]{:S(2)}) copy-start(f32[1536]{0:T(1024)} %param.32) | copy-start | bytes 18436
  102.1 1.0 copy-start.14
  102.1 1.9 copy-start.58
  102.3 16.2 %copy-start.7 = (f32[128,768]{1,0:T(8,128)}, f32[128,768]{1,0:T(8,128)S(1)}, u32[]{:S(2)}) copy-start(f32[128,768]{1,0:T(8,128)S(1)} %get-tuple-element.117) | copy-start | bytes 1179652
  102.5 16.0 %copy-start.47 = (f32[128]{0:T(128)}, f32[128]{0:T(128)S(1)}, u32[]{:S(2)}) copy-start(f32[128]{0:T(128)S(1)} %fusion.48) | copy-start | bytes 1540
  103.1 3.4 %copy-start.16 = (f32[128,1536]{1,0:T(8,128)}, f32[128,1536]{1,0:T(8,128)S(1)}, u32[]{:S(2)}) copy-start(f32[128,1536]{1,0:T(8,128)S(1)} %convolution_add_fusion.1) | copy-start | bytes 2359300
  105.6 1.8 copy-start.22
  107.4 12.4 %copy-start.19 = (bf16[16,48,384]{2,1,0:T(8,128)(2,1)S(1)}, bf16[16,48,384]{2,1,0:T(8,128)(2,1)}, u32[]{:S(2)}) copy-start(bf16[16,48,384]{2,1,0:T(8,128)(2,1)} %get-tuple-element.40) | copy-start | bytes 1769476
  118.4 30.5 %copy-start.1 = (bf16[16,128,768]{2,1,0:T(8,128)(2,1)S(1)}, bf16[16,128,768]{2,1,0:T(8,128)(2,1)}, u32[]{:S(2)}) copy-start(bf16[16,128,768]{2,1,0:T(8,128)(2,1)} %shard_map.408.kv_ref) | copy-start | bytes 9437188
  119.3 1.8 copy-start.12
  119.3 0.5 copy-start.56
  119.8 29.0 %copy-start.20 = (bf16[128,768]{1,0:T(8,128)(2,1)}, bf16[128,768]{1,0:T(8,128)(2,1)S(1)}, u32[]{:S(2)}) copy-start(bf16[128,768]{1,0:T(8,128)(2,1)S(1)} %get-tuple-element.113) | copy-start | bytes 589828
  148.9 0.9 copy-start.4
  149.8 1.2 copy-start.5
  151.1 0.8 copy-start.6
  151.9 11.7 %copy-start.39 = (bf16[16,48,1280]{2,1,0:T(8,128)(2,1)S(1)}, bf16[16,48,1280]{2,1,0:T(8,128)(2,1)}, u32[]{:S(2)}) copy-start(bf16[16,48,1280]{2,1,0:T(8,128)(2,1)} %get-tuple-element.38) | copy-start | bytes 5898244
  163.6 8.1 %copy-start.10 = (bf16[2,64,768]{2,1,0:T(8,128)(2,1)S(1)}, bf16[2,64,768]{2,1,0:T(8,128)(2,1)}, u32[]{:S(2)}) copy-start(bf16[2,64,768]{2,1,0:T(8,128)(2,1)} %param.24) | copy-start | bytes 589828
  163.6 8.1 %copy-start.43 = (f32[128]{0:T(128)S(1)}, f32[128]{0:T(128)}, u32[]{:S(2)}) copy-start(f32[128]{0:T(128)} %copy-done.42) | copy-start | bytes 1540
  163.6 8.3 %copy-start.60 = (f32[128]{0:T(128)S(1)}, f32[128]{0:T(128)}, u32[]{:S(2)}) copy-start(f32[128]{0:T(128)} %copy-done.59) | copy-start | bytes 1540
  163.6 8.3 %copy-start.50 = (f32[128]{0:T(128)S(1)}, f32[128]{0:T(128)}, u32[]{:S(2)}) copy-start(f32[128]{0:T(128)} %copy-done.49) | copy-start | bytes 1540
  163.6 8.7 %copy-start.15 = (bf16[2,64,768]{2,1,0:T(8,128)(2,1)S(1)}, bf16[2,64,768]{2,1,0:T(8,128)(2,1)}, u32[]{:S(2)}) copy-start(bf16[2,64,768]{2,1,0:T(8,128)(2,1)} %param.25) | copy-start | bytes 589828
  163.7 8.8 %copy-start.46 = (f32[1536]{0:T(1024)S(1)}, f32[1536]{0:T(1024)}, u32[]{:S(2)}) copy-start(f32[1536]{0:T(1024)} %get-tuple-element.122) | copy-start | bytes 18436
  163.7 8.8 %copy-start.8 = (f32[128,768]{1,0:T(8,128)S(1)}, f32[128,768]{1,0:T(8,128)}, u32[]{:S(2)}) copy-start(f32[128,768]{1,0:T(8,128)} %copy-done.7) | copy-start | bytes 1179652
  163.7 8.8 %copy-start.23 = (bf16[128,1536]{1,0:T(8,128)(2,1)S(1)}, bf16[128,1536]{1,0:T(8,128)(2,1)}, u32[]{:S(2)}) copy-start(bf16[128,1536]{1,0:T(8,128)(2,1)} %copy-done.22) | copy-start | bytes 1179652
  163.7 8.8 %copy-start.48 = (f32[128]{0:T(128)S(1)}, f32[128]{0:T(128)}, u32[]{:S(2)}) copy-start(f32[128]{0:T(128)} %copy-done.47) | copy-start | bytes 1540
  171.7 1.7 copy-start.3
  171.7 1.7 copy-start.21
  172.3 1.6 copy-start.28
  173.4 1.1 copy-start.17
  176.8 43.5 %copy-start.24 = (f32[1536,48]{0,1:T(8,128)S(1)}, f32[1536,48]{0,1:T(8,128)}, u32[]{:S(2)}) copy-start(f32[1536,48]{0,1:T(8,128)} %param.30) | copy-start | bytes 884740
  176.8 43.5 %copy-start.30 = (f32[1536,48]{0,1:T(8,128)S(1)}, f32[1536,48]{0,1:T(8,128)}, u32[]{:S(2)}) copy-start(f32[1536,48]{0,1:T(8,128)} %param.40) | copy-start | bytes 884740
  176.8 43.5 %copy-start.31 = (f32[1536,48]{0,1:T(8,128)S(1)}, f32[1536,48]{0,1:T(8,128)}, u32[]{:S(2)}) copy-start(f32[1536,48]{0,1:T(8,128)} %param.41) | copy-start | bytes 884740
  176.8 44.6 %copy-start.25 = (f32[48,1536]{1,0:T(8,128)S(1)}, f32[48,1536]{1,0:T(8,128)}, u32[]{:S(2)}) copy-start(f32[48,1536]{1,0:T(8,128)} %param.29) | copy-start | bytes 884740
  176.8 44.6 %copy-start.32 = (f32[48,1536]{1,0:T(8,128)S(1)}, f32[48,1536]{1,0:T(8,128)}, u32[]{:S(2)}) copy-start(f32[48,1536]{1,0:T(8,128)} %param.38) | copy-start | bytes 884740
  176.8 44.6 %copy-start.33 = (f32[48,1536]{1,0:T(8,128)S(1)}, f32[48,1536]{1,0:T(8,128)}, u32[]{:S(2)}) copy-start(f32[48,1536]{1,0:T(8,128)} %param.39) | copy-start | bytes 884740
  220.2 2.3 %copy-start.26 = (f32[48,3,384]{2,0,1:T(8,128)S(1)}, f32[48,3,384]{2,0,1:T(8,128)}, u32[]{:S(2)}) copy-start(f32[48,3,384]{2,0,1:T(8,128)} %param.27) | copy-start | bytes 663556
  220.2 2.3 %copy-start.34 = (f32[48,3,384]{2,0,1:T(8,128)S(1)}, f32[48,3,384]{2,0,1:T(8,128)}, u32[]{:S(2)}) copy-start(f32[48,3,384]{2,0,1:T(8,128)} %param.34) | copy-start | bytes 663556
  220.3 2.3 %copy-start.35 = (f32[48,3,384]{2,0,1:T(8,128)S(1)}, f32[48,3,384]{2,0,1:T(8,128)}, u32[]{:S(2)}) copy-start(f32[48,3,384]{2,0,1:T(8,128)} %param.35) | copy-start | bytes 663556
  220.3 3.2 %copy-start.29 = (f32[384,48]{0,1:T(8,128)S(1)}, f32[384,48]{0,1:T(8,128)}, u32[]{:S(2)}) copy-start(f32[384,48]{0,1:T(8,128)} %param.28) | copy-start | bytes 221188
  220.3 3.2 %copy-start.36 = (f32[384,48]{0,1:T(8,128)S(1)}, f32[384,48]{0,1:T(8,128)}, u32[]{:S(2)}) copy-start(f32[384,48]{0,1:T(8,128)} %param.36) | copy-start | bytes 221188
  220.3 3.2 %copy-start.37 = (f32[384,48]{0,1:T(8,128)S(1)}, f32[384,48]{0,1:T(8,128)}, u32[]{:S(2)}) copy-start(f32[384,48]{0,1:T(8,128)} %param.37) | copy-start | bytes 221188
  221.4 2.9 %copy-start.40 = (f32[6,48]{1,0:T(8,128)S(1)}, f32[6,48]{1,0:T(8,128)}, u32[]{:S(2)}) copy-start(f32[6,48]{1,0:T(8,128)} %param.33) | copy-start | bytes 3460
  221.4 2.9 %copy-start.51 = (f32[6,48]{1,0:T(8,128)S(1)}, f32[6,48]{1,0:T(8,128)}, u32[]{:S(2)}) copy-start(f32[6,48]{1,0:T(8,128)} %param.46) | copy-start | bytes 3460
  221.4 2.9 %copy-start.52 = (f32[6,48]{1,0:T(8,128)S(1)}, f32[6,48]{1,0:T(8,128)}, u32[]{:S(2)}) copy-start(f32[6,48]{1,0:T(8,128)} %param.47) | copy-start | bytes 3460
  221.4 3.6 %copy-start.44 = (f32[1536]{0:T(1024)S(1)}, f32[1536]{0:T(1024)}, u32[]{:S(2)}) copy-start(f32[1536]{0:T(1024)} %param.44) | copy-start | bytes 18436
  221.4 3.6 %copy-start.45 = (f32[1536]{0:T(1024)S(1)}, f32[1536]{0:T(1024)}, u32[]{:S(2)}) copy-start(f32[1536]{0:T(1024)} %param.45) | copy-start | bytes 18436
  221.5 4.2 %copy-start.54 = (f32[2,384]{1,0:T(2,128)S(1)}, f32[2,384]{1,0:T(2,128)}, u32[]{:S(2)}) copy-start(f32[2,384]{1,0:T(2,128)} %param.42) | copy-start | bytes 9220
  221.5 4.2 %copy-start.55 = (f32[2,384]{1,0:T(2,128)S(1)}, f32[2,384]{1,0:T(2,128)}, u32[]{:S(2)}) copy-start(f32[2,384]{1,0:T(2,128)} %param.43) | copy-start | bytes 9220
  221.5 4.8 %copy-start.13 = (f32[128,768]{1,0:T(8,128)S(1)}, f32[128,768]{1,0:T(8,128)}, u32[]{:S(2)}) copy-start(f32[128,768]{1,0:T(8,128)} %copy-done.12) | copy-start | bytes 1179652
  221.5 4.8 %copy-start.57 = (f32[128]{0:T(128)S(1)}, f32[128]{0:T(128)}, u32[]{:S(2)}) copy-start(f32[128]{0:T(128)} %copy-done.56) | copy-start | bytes 1540

commit v2 on v1

--- a/solution.py
+++ b/solution.py
@@ -446,11 +446,11 @@
         core = 1 - self.core if other else self.core
         return chip_at(place, self.chips) * 2 + core
 
-    def greet(self):
+    def greet(self, count=3):
         barrier = pltpu.get_barrier_semaphore()
         for device in (self.left, self.right, self.mate):
             pl.semaphore_signal(barrier, inc=1, device_id={"ctx": device}, device_id_type=MESH)
-        pl.semaphore_wait(barrier, 3)
+        pl.semaphore_wait(barrier, count)
 
 
 def remote(src, dst, send, recv, device):
@@ -533,129 +533,150 @@
     return [pltpu.SemaphoreType.DMA((count, chips))] * 4 + [pltpu.SemaphoreType.DMA((count,))]
 
 
-def gather_kernel(chips, count, *refs):
-    ins, outs, sems = refs[:count], refs[count : 2 * count], refs[2 * count :]
+class Scatter:
+    def __init__(self, ring, pieces, grads, mates, lands, outs, sems):
+        self.ring, self.pieces = ring, pieces
+        self.grads, self.mates, self.lands, self.outs = grads, mates, lands, outs
+        self.mate_send, self.mate_recv, self.ring_send, self.ring_recv = sems
+        self.order = []
+        for far in range(1, ring.chips // 2):
+            self.order += [-far, far]
+        self.order += [ring.chips // 2, 0]
+        self.arrived = set()
+        self.sent = []
+
+    def to_mate(self, index, at):
+        ring = self.ring
+        return remote(
+            self.grads[at].at[ring.slot(self.order[index], other=True)],
+            self.mates[at].at[index],
+            self.mate_send.at[at, index], self.mate_recv.at[at, index], ring.mate,
+        )
+
+    def start(self):
+        for index in range(self.ring.chips):
+            for at in range(len(self.grads)):
+                copy = self.to_mate(index, at)
+                copy.start()
+                self.sent.append(copy)
+
+    def own_part(self, ahead, at, columns):
+        half = self.ring.chips // 2 - 1
+        ahead = (ahead + half) % self.ring.chips - half
+        index = self.order.index(ahead)
+        if (index, at) not in self.arrived:
+            self.arrived.add((index, at))
+            self.to_mate(index, at).wait_recv()
+        mine = self.grads[at][self.ring.slot(ahead), :, columns].astype(jnp.float32)
+        return mine + self.mates[at][index, :, columns].astype(jnp.float32)
+
+    def hop(self, which, step, src):
+        device = self.ring.right if self.pieces[which][3] > 0 else self.ring.left
+        return remote(
+            src, self.lands[which].at[step], self.ring_send.at[which, step],
+            self.ring_recv.at[which, step], device,
+        )
+
+    def step(self, step):
+        chips = self.ring.chips
+        for which, (at, first, count, sign) in enumerate(self.pieces):
+            columns = slice(first, first + count)
+            land = self.lands[which]
+            part = self.own_part(-sign * (step + 1), at, columns)
+            if step > 0:
+                self.hop(which, step - 1, land.at[step - 1]).wait_recv()
+                part = part + land[step - 1].astype(jnp.float32)
+            if step < chips - 1:
+                hold = land.at[chips - 1 + step]
+                hold[...] = part.astype(jnp.bfloat16)
+                copy = self.hop(which, step, hold)
+                copy.start()
+                self.sent.append(copy)
+            else:
+                self.outs[at][:, columns] = part
+
+    def finish(self):
+        for copy in self.sent:
+            copy.wait_send()
+
+
+def scatter_scratch(blocks, pieces, chips):
+    rows, dma = blocks[0].shape[1], pltpu.SemaphoreType.DMA
+    return (
+        [pltpu.VMEM((chips, rows, b.shape[2]), jnp.bfloat16) for b in blocks]
+        + [pltpu.VMEM((2 * chips - 2, rows, p[2]), jnp.bfloat16) for p in pieces]
+        + [dma((len(blocks), chips))] * 2
+        + [dma((len(pieces), chips))] * 2
+    )
+
+
+def row_split(array, groups):
+    return array.reshape(groups, array.shape[0] // groups, array.shape[1])
+
+
+def tail_kernel(chips, pieces, *refs):
+    grad, part, normal, small_in = refs[0:4]
+    out, total, small_out = refs[4:7]
+    hold, land, small, mate = refs[7:11]
+    lands, sems = refs[11 : 11 + len(pieces)], refs[11 + len(pieces) :]
+    pair_send, pair_recv = sems[4:6]
+    other = 1 - lax.axis_index("tp")
     ring = Ring(chips)
-    ring.greet()
-    gather = Gather(ring, ins, outs, sems)
+    barrier = pltpu.get_barrier_semaphore()
+    pl.semaphore_signal(barrier, inc=1, device_id={"tp": other}, device_id_type=MESH)
+    ring.greet(4)
+    scatter = Scatter(ring, pieces, [grad], [mate], lands, [out], sems[:4])
+    scatter.start()
+    hold[...] = part[...].astype(jnp.bfloat16)
+    pair = pltpu.make_async_remote_copy(
+        src_ref=hold, dst_ref=land, send_sem=pair_send.at[0], recv_sem=pair_recv.at[0],
+        device_id={"tp": other}, device_id_type=MESH,
+    )
+    pair.start()
+    gather = Gather(ring, [small], [small_out], sems[6:])
+    scatter.step(0)
+    scatter.step(1)
+    small[...] = small_in[...]
+    pair.wait()
+    summed = hold[...].astype(jnp.float32) + land[...].astype(jnp.float32)
+    total[...] = summed
+    small[0:1, :] = jnp.sum(summed * normal[...], axis=0, keepdims=True)
+    small[1:2, :] = jnp.sum(summed, axis=0, keepdims=True)
     gather.start()
-    for step in range(gather.far_right):
-        gather.step(step)
+    for step in range(2, chips):
+        scatter.step(step)
+        if step - 2 < gather.far_right:
+            gather.step(step - 2)
     gather.finish()
-
-
-def ring_gather(arrays, groups, collective):
-    count, chips = len(arrays), groups // 2
-    return pl.pallas_call(
-        partial(gather_kernel, chips, count),
-        out_shape=[jax.ShapeDtypeStruct((groups,) + a.shape, a.dtype) for a in arrays],
-        in_specs=[pl.BlockSpec(memory_space=pl.ANY)] * count,
-        out_specs=[pl.BlockSpec(memory_space=pl.ANY)] * count,
-        scratch_shapes=gather_sems(count, chips),
-        compiler_params=pltpu.CompilerParams(collective_id=collective, has_side_effects=True),
-    )(*arrays)
-
-
-def scatter_kernel(chips, pieces, *refs):
-    grads, small = refs[0:4], refs[4]
-    outs, small_out = refs[5:9], refs[9]
-    mates, lands = refs[10:14], refs[14 : 14 + len(pieces)]
-    rest = refs[14 + len(pieces) :]
-    mate_send, mate_recv, ring_send, ring_recv = rest[:4]
-    ring = Ring(chips)
-    ring.greet()
-    order = []
-    for far in range(1, chips // 2):
-        order += [-far, far]
-    order += [chips // 2, 0]
-    sent = []
-
-    def to_mate(index, at):
-        ahead = order[index]
-        return remote(
-            grads[at].at[ring.slot(ahead, other=True)], mates[at].at[index],
-            mate_send.at[at, index], mate_recv.at[at, index], ring.mate,
-        )
-
-    arrived = set()
-
-    def own_part(ahead, at, columns):
-        ahead = (ahead + chips // 2 - 1) % chips - (chips // 2 - 1)
-        index = order.index(ahead)
-        if (index, at) not in arrived:
-            arrived.add((index, at))
-            to_mate(index, at).wait_recv()
-        mine = grads[at][ring.slot(ahead), :, columns].astype(jnp.float32)
-        return mine + mates[at][index, :, columns].astype(jnp.float32)
-
-    for index in range(chips):
-        for at in range(4):
-            copy = to_mate(index, at)
-            copy.start()
-            sent.append(copy)
-    gather = Gather(ring, [small], [small_out], rest[4:])
-    gather.start()
-
-    def hop(which, step, src):
-        device = ring.right if pieces[which][3] > 0 else ring.left
-        return remote(
-            src, lands[which].at[step], ring_send.at[which, step],
-            ring_recv.at[which, step], device,
-        )
-
-    for step in range(chips):
-        for which, (at, first, count, sign) in enumerate(pieces):
-            columns = slice(first, first + count)
-            part = own_part(-sign * (step + 1), at, columns)
-            if step > 0:
-                hop(which, step - 1, lands[which].at[step]).wait_recv()
-                part = part + lands[which][step - 1].astype(jnp.float32)
-            if step < chips - 1:
-                hold = lands[which].at[chips - 1 + step]
-                hold[...] = part.astype(jnp.bfloat16)
-                copy = hop(which, step, hold)
-                copy.start()
-                sent.append(copy)
-            else:
-                outs[at][:, columns] = part
-        if step < gather.far_right:
-            gather.step(step)
-    gather.finish()
-    for copy in sent:
-        copy.wait_send()
-
-
-def ring_scatter(grads, small, groups, collective):
+    scatter.finish()
+
+
+def tail(grad, part, normal, small, groups, collective):
     chips = groups // 2
-    blocks = [g.reshape(groups, g.shape[0] // groups, g.shape[1]) for g in grads]
-    rows = blocks[0].shape[1]
-    qkv, proj, up, down = [b.shape[2] for b in blocks]
-    right_up = up * 3 // 4 // 128 * 128
-    pieces = (
-        (0, 0, qkv, 1),
-        (3, 0, down, -1),
-        (2, 0, right_up, 1),
-        (1, 0, proj, -1),
-        (2, right_up, up - right_up, -1),
-    )
+    block = row_split(grad, groups)
+    columns = block.shape[2]
+    right = columns // 256 * 128
+    pieces = ((0, 0, right, 1), (0, right, columns - right, -1))
     vmem = pl.BlockSpec(memory_space=pltpu.VMEM)
-    hbm = pl.BlockSpec(memory_space=pl.ANY)
     dma = pltpu.SemaphoreType.DMA
     return pl.pallas_call(
-        partial(scatter_kernel, chips, pieces),
-        out_shape=[jax.ShapeDtypeStruct(b.shape[1:], jnp.float32) for b in blocks]
-        + [jax.ShapeDtypeStruct((groups,) + small.shape, small.dtype)],
-        in_specs=[vmem] * 4 + [hbm],
-        out_specs=[vmem] * 4 + [hbm],
-        scratch_shapes=[pltpu.VMEM((chips, rows, b.shape[2]), jnp.bfloat16) for b in blocks]
-        + [pltpu.VMEM((2 * chips - 2, rows, p[2]), jnp.bfloat16) for p in pieces]
-        + [dma((4, chips)), dma((4, chips))]
-        + [dma((len(pieces), chips)), dma((len(pieces), chips))]
+        partial(tail_kernel, chips, pieces),
+        out_shape=[
+            jax.ShapeDtypeStruct(block.shape[1:], jnp.float32),
+            jax.ShapeDtypeStruct(part.shape, jnp.float32),
+            jax.ShapeDtypeStruct((groups,) + small.shape, jnp.float32),
+        ],
+        in_specs=[vmem] * 4,
+        out_specs=[vmem] * 3,
+        scratch_shapes=[pltpu.VMEM(part.shape, jnp.bfloat16)] * 2
+        + [pltpu.VMEM(small.shape, jnp.float32)]
+        + scatter_scratch([block], pieces, chips)
+        + [dma((1,)), dma((1,))]
         + gather_sems(1, chips),
         compiler_params=pltpu.CompilerParams(
             collective_id=collective, has_side_effects=True, vmem_limit_bytes=VMEM_LIMIT
         ),
-    )(*blocks, small)
+    )(block, part, normal, small)
 
 
 def pair_kernel(count, *refs):
@@ -705,91 +726,180 @@
     return lax.dot_general(left, right, dims, preferred_element_type=jnp.float32)
 
 
-def attend_kernel(heads, q_ref, kv_ref, own_ref, all_ref, context_ref, log_ref):
-    seqs = own_ref.shape[0]
-    rows = q_ref.shape[0] // seqs
+def attend_unit(heads, seq, head, rows, allowed, own, every, context_ref):
     width = heads * HD
+    here = slice(seq * rows, (seq + 1) * rows)
+    at = slice(head * HD, (head + 1) * HD)
+    keys = every[:, here, width + head * HD : width + (head + 1) * HD].reshape(-1, HD)
+    values = every[:, here, 2 * width + head * HD : 2 * width + (head + 1) * HD].reshape(-1, HD)
+    scores = mul(own(here, at), keys, NT) * 0.125
+    scores = jnp.where(allowed, scores, -1000000000.0)
+    top = jnp.max(scores, axis=-1, keepdims=True)
+    shares = jnp.exp(scores - top)
+    total = jnp.sum(shares, axis=-1, keepdims=True)
+    mixed = mul(shares.astype(jnp.bfloat16), values, NN)
+    context_ref[here, at] = mixed / total
+    return top + jnp.log(total)
+
+
+def front_kernel(chips, heads, *refs):
+    ins, (bias, own_pos, all_pos) = refs[0:5], refs[5:8]
+    outs, vectors_ref, every, context_ref, log_ref = refs[8:13], *refs[13:17]
+    tokens_all, sems = outs[1], refs[17:]
+    width = heads * HD
+    groups = 2 * chips
+    seqs = own_pos.shape[0]
+    rows = tokens_all.shape[1] // seqs
+    ring = Ring(chips)
+    ring.greet()
+    first = Gather(ring, ins[0:2], outs[0:2], sems[0:5])
+    second = Gather(ring, ins[2:5], outs[2:5], sems[5:10])
+    first.start()
+    for step in range(first.far_right - 1):
+        first.step(step)
+    second.start()
+    first.step(first.far_right - 1)
+    first.finish()
+    packed = outs[0]
+    extra = packed[:, :, 3 * width :].reshape(-1, 128).astype(jnp.float32).T
+    vectors = (extra[0:6] + extra[6:12]) + extra[12:18]
+    vectors_ref[0:6, :] = vectors
+    gain, shift = vectors[0:1], vectors[1:2]
+
+    def project(at, carry):
+        values = tokens_all[pl.ds(2 * at, 2)].reshape(-1, tokens_all.shape[2])
+        normed = layer_norm(values.astype(jnp.float32), gain, shift).astype(jnp.bfloat16)
+        weights = packed[:, :, : 3 * width].reshape(-1, 3 * width)
+        result = (mul(normed, weights, NN) + bias[...]).astype(jnp.bfloat16)
+        every[pl.ds(2 * at, 2)] = result.reshape(2, -1, 3 * width)
+        return carry
+
+    lax.fori_loop(0, groups // 4, project, 0)
+    second.step(0)
+    lax.fori_loop(groups // 4, groups // 2, project, 0)
+    second.step(1)
+
+    def own(here, at):
+        return every[ring.me, here, at]
+
     lanes = lax.broadcasted_iota(jnp.int32, (rows, 128), 1)
     for seq in range(seqs):
+        allowed = own_pos[seq] >= all_pos[seq]
+        logs = jnp.zeros((rows, 128), jnp.float32)
+        for head in range(heads):
+            log = attend_unit(heads, seq, head, rows, allowed, own, every, context_ref)
+            logs = jnp.where(lanes == head, log, logs)
+        log_ref[seq * rows : (seq + 1) * rows, :] = logs
+        if seq + 2 < second.far_right:
+            second.step(seq + 2)
+    for step in range(seqs + 2, second.far_right):
+        second.step(step)
+    second.finish()
+
+
+def front(arrays, bias, own_pos, all_pos, heads, groups, collective):
+    vmem = pl.BlockSpec(memory_space=pltpu.VMEM)
+    hbm = pl.BlockSpec(memory_space=pl.ANY)
+    many, width = arrays[1].shape
+    chips = groups // 2
+    return pl.pallas_call(
+        partial(front_kernel, chips, heads),
+        out_shape=[jax.ShapeDtypeStruct((groups,) + a.shape, a.dtype) for a in arrays]
+        + [
+            jax.ShapeDtypeStruct((8, width), jnp.float32),
+            jax.ShapeDtypeStruct((groups, many, 3 * heads * HD), jnp.bfloat16),
+            jax.ShapeDtypeStruct((many, heads * HD), jnp.float32),
+            jax.ShapeDtypeStruct((many, 128), jnp.float32),
+        ],
+        in_specs=[vmem] * 2 + [hbm] * 3 + [vmem] * 3,
+        out_specs=[vmem] * 2 + [hbm] * 3 + [vmem] * 4,
+        scratch_shapes=gather_sems(2, chips) + gather_sems(3, chips),
+        compiler_params=pltpu.CompilerParams(
+            collective_id=collective, has_side_effects=True, vmem_limit_bytes=VMEM_LIMIT
+        ),
+    )(*arrays, bias, own_pos, all_pos)
+
+
+def back_kernel(chips, heads, pieces, *refs):
+    own, every, own_pos, all_pos = refs[0:4]
+    grads, out_ref, sums = refs[4:7], refs[7], refs[8:11]
+    gathered, mates, lands = refs[11], refs[12:15], refs[15 : 15 + len(pieces)]
+    sems = refs[15 + len(pieces) :]
+    seqs = own_pos.shape[0]
+    rows = own.shape[0] // seqs
+    width = heads * HD
+    ring = Ring(chips)
+    me = ring.me
+    ring.greet()
+    gather = Gather(ring, [own], [gathered], sems[4:])
+    scatter = Scatter(ring, pieces, grads, mates, lands, sums, sems[:4])
+    gather.start()
+    scatter.start()
+    for step in range(gather.far_right - 1):
+        gather.step(step)
+    scatter.step(0)
+    gather.step(gather.far_right - 1)
+    gather.finish()
+    done = 1
+    for seq in range(seqs):
         here = slice(seq * rows, (seq + 1) * rows)
-        allowed = own_ref[seq] >= all_ref[seq]
-        logs = jnp.zeros((rows, 128), jnp.float32)
+        allowed = own_pos[seq] >= all_pos[seq]
+        allowed_back = own_pos[seq] <= all_pos[seq]
+        stats = gathered[:, here, width:].reshape(-1, 128).astype(jnp.float32).T
+        turned = (stats[0:16] + stats[16:32]) + stats[32:48]
+        parts = own[here, width:].astype(jnp.float32)
+        stat = (parts[:, 0:16] + parts[:, 16:32]) + parts[:, 32:48]
         for head in range(heads):
             at = slice(head * HD, (head + 1) * HD)
             past = slice(width + head * HD, width + (head + 1) * HD)
-            keys = kv_ref[:, here, at].reshape(-1, HD)
-            values = kv_ref[:, here, past].reshape(-1, HD)
-            scores = mul(q_ref[here, at], keys, NT) * 0.125
-            scores = jnp.where(allowed, scores, -1000000000.0)
-            top = jnp.max(scores, axis=-1, keepdims=True)
-            shares = jnp.exp(scores - top)
-            total = jnp.sum(shares, axis=-1, keepdims=True)
-            mixed = mul(shares.astype(jnp.bfloat16), values, NN)
-            context_ref[here, at] = mixed / total
-            logs = jnp.where(lanes == head, top + jnp.log(total), logs)
-        log_ref[here, :] = logs
-
-
-def attend(queries, pairs, own_pos, all_pos, heads):
-    vmem = pl.BlockSpec(memory_space=pltpu.VMEM)
-    return pl.pallas_call(
-        partial(attend_kernel, heads),
-        out_shape=[
-            jax.ShapeDtypeStruct(queries.shape, jnp.float32),
-            jax.ShapeDtypeStruct((queries.shape[0], 128), jnp.float32),
-        ],
-        in_specs=[vmem] * 4,
-        out_specs=[vmem] * 2,
-        compiler_params=pltpu.CompilerParams(vmem_limit_bytes=VMEM_LIMIT),
-    )(queries, pairs, own_pos, all_pos)
-
-
-def attend_back_kernel(
-    heads, qg_ref, stat_ref, kv_ref, qgs_ref, stats_ref, own_ref, all_ref, out_ref
-):
-    seqs = own_ref.shape[0]
-    rows = qg_ref.shape[0] // seqs
-    width = heads * HD
-    me = lax.axis_index("ctx")
-    for seq in range(seqs):
-        here = slice(seq * rows, (seq + 1) * rows)
-        allowed = own_ref[seq] >= all_ref[seq]
-        allowed_back = own_ref[seq] <= all_ref[seq]
-        turned = stats_ref[:, here, :].reshape(-1, 128).T
-        for head in range(heads):
-            at = slice(head * HD, (head + 1) * HD)
-            past = slice(width + head * HD, width + (head + 1) * HD)
-            keys = kv_ref[:, here, at].reshape(-1, HD)
-            values = kv_ref[:, here, past].reshape(-1, HD)
-            scores = jnp.where(allowed, mul(qg_ref[here, at], keys, NT) * 0.125, -1000000000.0)
-            shares = jnp.exp(scores - stat_ref[here, head : head + 1])
-            grad_share = mul(qg_ref[here, past], values, NT)
-            delta = stat_ref[here, heads + head : heads + head + 1]
+            last = slice(2 * width + head * HD, 2 * width + (head + 1) * HD)
+            queries = every[:, here, at].reshape(-1, HD)
+            keys = every[:, here, past].reshape(-1, HD)
+            values = every[:, here, last].reshape(-1, HD)
+            grad_all = gathered[:, here, at].reshape(-1, HD)
+            query, key, value = every[me, here, at], every[me, here, past], every[me, here, last]
+            scores = jnp.where(allowed, mul(query, keys, NT) * 0.125, -1000000000.0)
+            shares = jnp.exp(scores - stat[:, head : head + 1])
+            grad_share = mul(own[here, at], values, NT)
+            delta = stat[:, heads + head : heads + head + 1]
             grad_score = (shares * (grad_share - delta)).astype(jnp.bfloat16)
             out_ref[here, at] = (mul(grad_score, keys, NN) * 0.125).astype(jnp.bfloat16)
-            queries = qgs_ref[:, here, at].reshape(-1, HD)
-            grads = qgs_ref[:, here, past].reshape(-1, HD)
-            key, value = kv_ref[me, here, at], kv_ref[me, here, past]
             scores = jnp.where(allowed_back, mul(key, queries, NT) * 0.125, -1000000000.0)
             shares = jnp.exp(scores - turned[head : head + 1])
-            grad_value = mul(shares.astype(jnp.bfloat16), grads, NN)
-            grad_share = mul(value, grads, NT)
+            grad_value = mul(shares.astype(jnp.bfloat16), grad_all, NN)
+            grad_share = mul(value, grad_all, NT)
             grad_score = shares * (grad_share - turned[heads + head : heads + head + 1])
             grad_key = mul(grad_score.astype(jnp.bfloat16), queries, NN) * 0.125
             out_ref[here, past] = grad_key.astype(jnp.bfloat16)
-            last = slice(2 * width + head * HD, 2 * width + (head + 1) * HD)
             out_ref[here, last] = grad_value.astype(jnp.bfloat16)
-
-
-def attend_back(own, stats, pairs, all_own, all_stats, own_pos, all_pos, heads):
+            if head % 2 == 1 and done < chips - 1:
+                scatter.step(done)
+                done += 1
+    for step in range(done, chips):
+        scatter.step(step)
+    scatter.finish()
+
+
+def back(own, every, own_pos, all_pos, grads, heads, groups, collective):
     vmem = pl.BlockSpec(memory_space=pltpu.VMEM)
+    chips = groups // 2
+    blocks = [row_split(g, groups) for g in grads]
+    proj, up, down = [b.shape[2] for b in blocks]
+    cut = proj * 2 // 3 // 128 * 128
+    pieces = ((1, 0, up, 1), (2, 0, down, -1), (0, 0, cut, 1), (0, cut, proj - cut, -1))
     return pl.pallas_call(
-        partial(attend_back_kernel, heads),
-        out_shape=jax.ShapeDtypeStruct((own.shape[0], 3 * heads * HD), jnp.bfloat16),
+        partial(back_kernel, chips, heads, pieces),
+        out_shape=[jax.ShapeDtypeStruct((own.shape[0], 3 * heads * HD), jnp.bfloat16)]
+        + [jax.ShapeDtypeStruct(b.shape[1:], jnp.float32) for b in blocks],
         in_specs=[vmem] * 7,
-        out_specs=vmem,
-        compiler_params=pltpu.CompilerParams(vmem_limit_bytes=VMEM_LIMIT),
-    )(own, stats, pairs, all_own, all_stats, own_pos, all_pos)
+        out_specs=[vmem] * 4,
+        scratch_shapes=[pltpu.VMEM((groups,) + own.shape, own.dtype)]
+        + scatter_scratch(blocks, pieces, chips)
+        + gather_sems(1, chips),
+        compiler_params=pltpu.CompilerParams(
+            collective_id=collective, has_side_effects=True, vmem_limit_bytes=VMEM_LIMIT
+        ),
+    )(own, every, own_pos, all_pos, *blocks)
 
 
 def three_parts(array):
@@ -844,28 +954,33 @@
         ],
         axis=1,
     )
-    packed_full, proj_full, up_full, down_full = ring_gather(
-        [packed, proj_weight.astype(low).T, up_weight.astype(low), down_weight.astype(low).T],
+    bias = jnp.concatenate([qkv_bias[0], jnp.zeros_like(qkv_bias[0]), qkv_bias[1]])[None]
+    grad_low = out_grad.reshape(many, width)
+    packed_full, _, proj_full, up_full, down_full, vectors, every, context, logs = front(
+        [
+            packed,
+            tokens.reshape(many, width),
+            proj_weight.astype(low).T,
+            up_weight.astype(low),
+            down_weight.astype(low).T,
+        ],
+        bias,
+        own_pos,
+        all_pos,
+        heads,
         groups,
         1,
     )
     packed_full = packed_full.reshape(width, -1)
     qkv_full = packed_full[:, : 3 * inner]
-    vectors = packed_full[:, 3 * inner : 3 * inner + 18].astype(jnp.float32).T
-    vectors = (vectors[0:6] + vectors[6:12]) + vectors[12:18]
     proj_full = proj_full.reshape(width, -1)
     up_full = up_full.reshape(width, -1)
     down_full = down_full.reshape(width, -1)
     inputs = tokens.reshape(many, width).astype(jnp.float32)
-    grad_low = out_grad.reshape(many, width)
     first_normalized, norm_one_back = jax.vjp(layer_norm, inputs, vectors[0], vectors[1])
     normed_low = first_normalized.astype(low)
-    projected = mul(normed_low, qkv_full, NN)
-    bias = jnp.concatenate([qkv_bias[0], jnp.zeros_like(qkv_bias[0]), qkv_bias[1]])
-    projected = (projected + bias).astype(low)
-    queries = projected[:, :inner]
-    (pairs,) = ring_gather([projected[:, inner:]], groups, 2)
-    context, logs = attend(queries, pairs, own_pos, all_pos, heads)
+    center = inputs - jnp.mean(inputs, axis=-1, keepdims=True)
+    normal = center * lax.rsqrt(jnp.mean(center * center, axis=-1, keepdims=True) + 1e-05)
     context_low = context.astype(low)
     (attn,) = pair_sum([mul(context_low, proj_full, NT)], 3)
     middle = inputs + (attn + vectors[4])
@@ -890,24 +1005,32 @@
     delta = jnp.dot(
         grad_context.astype(jnp.float32) * context, choose, precision=lax.Precision.HIGHEST
     )
-    stats = logs + delta
-    own = jnp.concatenate([queries, grad_context], axis=1)
-    all_own, all_stats = ring_gather([own, stats], groups, 5)
-    grad_low_qkv = attend_back(own, stats, pairs, all_own, all_stats, own_pos, all_pos, heads)
-    (grad_normed_one,) = pair_sum([mul(grad_low_qkv, qkv_full, NT)], 6)
-    grad_in_norm, grad_gain_one, grad_shift_one = norm_one_back(grad_normed_one)
-    input_grad = grad_middle + grad_in_norm
+    stats = three_parts((logs + delta)[:, :16])
+    own = jnp.concatenate([grad_context] + stats + [jnp.zeros((many, 80), low)], axis=1)
 
     def turned(left, right):
         return lax.dot_general(
             left, right, (((0,), (0,)), ((), ())), preferred_element_type=jnp.float32
         ).astype(low)
 
+    grad_low_qkv, sum_proj, sum_up, sum_down = back(
+        own,
+        every,
+        own_pos,
+        all_pos,
+        [
+            turned(grad_attn, context_low),
+            turned(normed_mid, grad_pre),
+            turned(grad_low, hidden_low),
+        ],
+        heads,
+        groups,
+        5,
+    )
     grad_qbias = jnp.sum(grad_low_qkv.astype(jnp.float32), axis=0)
     small = jnp.concatenate(
         [
-            grad_gain_one,
-            grad_shift_one,
+            jnp.zeros((2 * width,), jnp.float32),
             grad_gain_two,
             grad_shift_two,
             jnp.sum(grad_attn.astype(jnp.float32), axis=0),
@@ -916,25 +1039,26 @@
             grad_qbias[2 * inner :],
             jnp.sum(grad_pre.astype(jnp.float32), axis=0),
         ]
-    ).reshape(-1, 128)
-    sum_qkv, sum_proj, sum_up, sum_down, all_small = ring_scatter(
-        [
-            turned(normed_low, grad_low_qkv),
-            turned(grad_attn, context_low),
-            turned(normed_mid, grad_pre),
-            turned(grad_low, hidden_low),
-        ],
+    )
+    used = small.shape[0]
+    small = jnp.pad(small, (0, -used % (8 * width))).reshape(-1, width)
+    sum_qkv, grad_normed_one, all_small = tail(
+        turned(normed_low, grad_low_qkv),
+        mul(grad_low_qkv, qkv_full, NT),
+        normal,
         small,
         groups,
-        7,
-    )
+        6,
+    )
+    grad_in_norm = norm_one_back(grad_normed_one)[0]
+    input_grad = grad_middle + grad_in_norm
     sums = jnp.sum(all_small, axis=0).reshape(-1)
     ends = 6 * width
     sum_vectors = lax.dynamic_slice_in_dim(
         sums[:ends].reshape(6, width), device * share, share, 1
     )
     sum_qbias = sums[ends : ends + 2 * inner].reshape(2, inner)
-    sum_upbias = sums[ends + 2 * inner :]
+    sum_upbias = sums[ends + 2 * inner : used]
     qkv_new = adamw(
         qkv_weight, sum_qkv.reshape(share, 3, inner), qkv_first, qkv_second, 0.1, 0.1
     )

time: 228 us -> 228 us (level)
  Pallas kernels: 186 us -> 171 us
  local copies, waits for them, and re-layouts: 10.4 us -> 23 us
    unnamed x132 -> x138, local copies, waits for them, and re-layouts: 7.97 us -> 15.5 us
    pallas_call x3 -> x2, Pallas kernels: 25.4 us -> 18.1 us  [pair_sum(): pl.pallas_call(partial(pair_kernel, count), out_shape=[jax.ShapeDtypeStru...]
    pallas_call x6 -> x3, Pallas kernels: 160 us -> 153 us  [the longest x1 69 us: front(): pl.pallas_call(partial(front_kernel, chips, heads), out_shape=[jax.ShapeD...]
    concatenate x1 -> x2, local copies, waits for them, and re-layouts: 0.01 us -> 3 us  [the longest x1 1.7 us: ring_local(): jnp.concatenate([grad_context] + stats + [jnp.zeros((many, 80), low)], ax...]
    dot_general x4, matrix products: 4.14 us -> 6.46 us  [turned(): lax.dot_general(left, right, (((0,), (0,)), ((), ())), preferred_element_...]
    dot_general x8 -> x7, matrix products: 6.98 us -> 7.36 us  [mul(): lax.dot_general(left, right, dims, preferred_element_type=jnp.float32)]
where the time goes in v2:
time: 228 us; the launch traced here: 227 us
  Pallas kernels  171 us (75%)
  local copies, waits for them, and re-layouts  23 us (10%)
  other arithmetic  17.2 us (8%)
  matrix products  14.1 us (6%)
    pallas_call x1, Pallas kernels, front(): pl.pallas_call(partial(front_kernel, chips, heads), out_shape=[jax.ShapeD...  69 us
    pallas_call x1, Pallas kernels, back(): pl.pallas_call(partial(back_kernel, chips, heads, pieces), out_shape=[jax...  58.1 us
    pallas_call x1, Pallas kernels, tail(): pl.pallas_call(partial(tail_kernel, chips, pieces), out_shape=[jax.ShapeD...  26 us
    pallas_call x2, Pallas kernels, pair_sum(): pl.pallas_call(partial(pair_kernel, count), out_shape=[jax.ShapeDtypeStru...  18.1 us
    unnamed x138, local copies, waits for them, and re-layouts  15.5 us
    dot_general x7, matrix products, mul(): lax.dot_general(left, right, dims, preferred_element_type=jnp.float32)  7.36 us
    dot_general x4, matrix products, turned(): lax.dot_general(left, right, (((0,), (0,)), ((), ())), preferred_element_...  6.46 us
    sub x7, other arithmetic, adamw(): weight - rate * (first_hat / (jnp.sqrt(second_hat) + EPSILON) + decay * w...  5.65 us

profile of v2, /device:TPU:0, one launch (start us, length us, event | category | flops | bytes accessed | tf_op | source)
XLA Modules:
  0.0 227.2 jit_solution(7505165715276851821)
XLA Ops:
  0.7 0.8 dynamic-slice_multiply_fusion
  1.6 0.1 add.351
  1.9 0.8 copy.66
  2.7 0.9 convert_bitcast_fusion.1
  3.7 0.8 slice_reduce_fusion.8
  4.5 0.7 broadcast_multiply_fusion.1
  5.5 1.0 convert_bitcast_fusion.refs_4_
  6.5 1.0 convert_element_type.105.refs_3_
  7.5 0.9 convert_bitcast_fusion.2.refs_2_
  8.4 69.0 %shard_map.407 = (bf16[16,48,1280]{2,1,0:T(8,128)(2,1)S(1)}, bf16[16,128,768]{2,1,0:T(8,128)(2,1)}, bf16[16,48,384]{2,1,0:T(8,128)(2,1)S(1)}, bf16[16,48,1536]{2...) custom-call(bf16[48,1280]{1,0:T(8,128)(2,1)S(1)} %pad_maximum_fusion, ...), custom_call_target="tpu_custom_call" | custom-call | tf_op jit(solution)/shard_map/pallas_call | solution.py:805
  77.4 1.3 copy-done.18
  78.7 0.8 copy-done.1
  79.6 0.3 fusion.30.refs_0_
  79.9 7.3 %shard_map.408 = f32[128,768]{1,0:T(8,128)S(1)} custom-call(f32[128,768]{1,0:T(8,128)S(1)} %fusion.30.refs_0_), custom_call_target="tpu_custom_call" | custom-call | tf_op jit(solution)/shard_map/pallas_call | solution.py:708
  87.3 0.6 slice_reduce_fusion.2
  87.9 0.1 convert_reduce_fusion.2
  88.0 0.2 fusion.13
  88.3 0.5 rsqrt.22
  88.9 0.6 div.170
  89.5 1.0 fusion.60
  90.5 0.2 multiply_reduce_fusion.2
  90.7 1.3 convolution_add_fusion
  92.0 1.6 convert_reduce_fusion
  93.6 0.8 copy-done.26
  94.4 0.9 fusion.61.refs_1_
  95.3 0.9 fusion.47.refs_0_
  96.2 10.8 %shard_map.409 = (f32[128,768]{1,0:T(8,128)S(1)}, f32[128,768]{1,0:T(8,128)S(1)}) custom-call(f32[128,768]{1,0:T(8,128)S(1)} %fusion.47.refs_0_, f32[128,768]{1,0:T(8,128)S(1)} %fusion.61.refs_1_), custom_call_target="tpu_custom_call" | custom-call | tf_op jit(solution)/shard_map/pallas_call | solution.py:708
  107.0 0.3 multiply_reduce_fusion
  107.3 1.4 constant_dynamic-update-slice_fusion.7
  108.6 1.3 constant_dynamic-update-slice_fusion.6
  109.9 1.3 constant_dynamic-update-slice_fusion.5
  111.3 1.9 fusion.59
  113.2 0.1 convert_reduce_fusion.4
  113.3 1.4 constant_dynamic-update-slice_fusion.4
  114.8 1.3 constant_dynamic-update-slice_fusion.3
  116.1 1.9 convolution_convert_fusion.2
  118.0 0.3 convolution_convert_fusion.3
  118.4 0.3 convolution_convert_fusion.4
  118.7 0.3 fusion.20
  119.0 0.7 fusion.28
  119.7 0.6 broadcast_in_dim.18
  120.3 1.7 concatenate.18.refs_0_
  122.0 3.5 %convolution_convert_fusion.1 = bf16[1536,768]{0,1:T(8,128)(2,1)} fusion(bf16[128,768]{1,0:T(8,128)(2,1)} %bitcast.91, f32[128,1536]{1,0:T(8,128)} %copy-done.25), kind=kOutput, calls=%fused_computation.1 | convolution fusion | flops 304939008 | bytes 3342336 | tf_op jit(solution)/shard_map/dot_general | solution.py:1012
  125.6 58.1 %shard_map.410 = (bf16[128,1152]{1,0:T(8,128)(2,1)S(1)}, f32[48,384]{1,0:T(8,128)S(1)}, f32[48,1536]{1,0:T(8,128)S(1)}, f32[48,1536]{1,0:T(8,128)S(1)}) custom-call(bf16[128,512]{1,0:T(8,128)(2,1)S(1)} %copy-done.9, bf16[16,128,1152]{2,1,0:T(8,128)(2,1)} %get-tuple-element.48.refs_1_, s32[2,64,1]{2,1,0:T(8,128)S(1)} %copy-done.8, ...), custom_call_target="tpu_custom_call" | custom-call | tf_op jit(solution)/shard_map/pallas_call | solution.py:890
  183.7 0.7 copy-done.12
  184.4 0.6 copy-done.14
  185.0 0.7 copy-done.5
  185.8 1.3 constant_dynamic-update-slice_fusion.2
  187.1 1.3 constant_dynamic-update-slice_fusion.1
  188.4 1.3 constant_dynamic-update-slice_fusion
  189.7 0.8 pad.9
  190.5 2.2 fusion.refs_1_
  192.8 0.7 convolution_convert_fusion
  193.5 26.0 %shard_map.411 = (f32[48,1152]{1,0:T(8,128)S(1)}, f32[128,768]{1,0:T(8,128)S(1)}, f32[16,16,768]{2,1,0:T(8,128)S(1)}) custom-call(bf16[16,48,1152]{2,1,0:T(8,128)(2,1)S(1)} %bitcast.84, f32[128,768]{1,0:T(8,128)S(1)} %fusion.refs_1_, f32[128,768]{1,0:T(8,128)S(1)} %get-tuple-element.119.refs_2_, f32[16,768]{1,0:T(8,128)S(1)} %reshape.300.refs_3_), custom_call_target="tpu_custom_call" | custom-call | tf_op jit(solution)/shard_map/pallas_call | solution.py:662
  219.7 0.9 multiply_subtract_fusion.2
  220.7 0.2 fusion.11
  220.9 0.2 fusion.46
  221.2 1.0 add_add_fusion.2
  222.3 0.7 add_subtract_fusion.2
  223.1 0.6 add_subtract_fusion.1
  223.8 0.6 add_subtract_fusion.3
  224.4 1.0 multiply_subtract_fusion
  225.5 1.0 multiply_subtract_fusion.1
  226.5 0.7 add_subtract_fusion
  (160 shorter events, 1.4 us)
Async XLA Ops:
  0.7 7.7 %copy-start = (bf16[2,64,768]{2,1,0:T(8,128)(2,1)S(1)}, bf16[2,64,768]{2,1,0:T(8,128)(2,1)}, u32[]{:S(2)}) copy-start(bf16[2,64,768]{2,1,0:T(8,128)(2,1)} %param.24) | copy-start | bytes 589828
  1.9 85.4 %copy-start.7 = (s32[2,64,1]{2,1,0:T(8,128)}, s32[2,64,1]{2,1,0:T(8,128)S(1)}, u32[]{:S(2)}) copy-start(s32[2,64,1]{2,1,0:T(8,128)S(1)} %broadcast_add_fusion.refs_6_.refs_2_) | copy-start | bytes 1540
  77.4 1.3 copy-start.18
  78.7 0.8 copy-start.1
  78.7 0.9 copy-start.3
  78.7 10.1 %copy-start.16 = (f32[128,128]{1,0:T(8,128)}, f32[128,128]{1,0:T(8,128)S(1)}, u32[]{:S(2)}) copy-start(f32[128,128]{1,0:T(8,128)S(1)} %get-tuple-element.47) | copy-start | bytes 196612
  89.5 2.5 %copy-start.23 = (bf16[2,64,768]{2,1,0:T(8,128)(2,1)S(1)}, bf16[2,64,768]{2,1,0:T(8,128)(2,1)}, u32[]{:S(2)}) copy-start(bf16[2,64,768]{2,1,0:T(8,128)(2,1)} %param.25) | copy-start | bytes 589828
  89.5 2.5 %copy-start.62 = (bf16[16,48,1536]{2,1,0:T(8,128)(2,1)S(1)}, bf16[16,48,1536]{2,1,0:T(8,128)(2,1)}, u32[]{:S(2)}) copy-start(bf16[16,48,1536]{2,1,0:T(8,128)(2,1)} %get-tuple-element.44) | copy-start | bytes 7077892
  90.5 16.5 %copy-start.19 = (f32[128,768]{1,0:T(8,128)}, f32[128,768]{1,0:T(8,128)S(1)}, u32[]{:S(2)}) copy-start(f32[128,768]{1,0:T(8,128)S(1)} %get-tuple-element.117) | copy-start | bytes 1179652
  90.5 16.5 %copy-start.44 = (f32[128]{0:T(128)}, f32[128]{0:T(128)S(1)}, u32[]{:S(2)}) copy-start(f32[128]{0:T(128)S(1)} %broadcast_multiply_fusion.2) | copy-start | bytes 1540
  90.7 2.9 %copy-start.60 = (f32[128]{0:T(128)}, f32[128]{0:T(128)S(1)}, u32[]{:S(2)}) copy-start(f32[128]{0:T(128)S(1)} %multiply_reduce_fusion.2) | copy-start | bytes 1540
  90.7 16.3 %copy-start.51 = (f32[128]{0:T(128)}, f32[128]{0:T(128)S(1)}, u32[]{:S(2)}) copy-start(f32[128]{0:T(128)S(1)} %fusion.45) | copy-start | bytes 1540
  92.0 3.3 %copy-start.25 = (f32[128,1536]{1,0:T(8,128)}, f32[128,1536]{1,0:T(8,128)S(1)}, u32[]{:S(2)}) copy-start(f32[128,1536]{1,0:T(8,128)S(1)} %convolution_add_fusion) | copy-start | bytes 2359300
  93.6 0.8 copy-start.26
  95.3 16.0 %copy-start.61 = (f32[128]{0:T(128)S(1)}, f32[128]{0:T(128)}, u32[]{:S(2)}) copy-start(f32[128]{0:T(128)} %copy-done.60) | copy-start | bytes 1540
  95.3 16.0 %copy-start.42 = (f32[768]{0:T(1024)S(1)}, f32[768]{0:T(1024)}, u32[]{:S(2)}) copy-start(f32[768]{0:T(1024)} %get-tuple-element.85) | copy-start | bytes 9220
  107.2 8.8 %copy-start.20 = (f32[128,768]{1,0:T(8,128)S(1)}, f32[128,768]{1,0:T(8,128)}, u32[]{:S(2)}) copy-start(f32[128,768]{1,0:T(8,128)} %copy-done.19) | copy-start | bytes 1179652
  107.3 8.8 %copy-start.45 = (f32[128]{0:T(128)S(1)}, f32[128]{0:T(128)}, u32[]{:S(2)}) copy-start(f32[128]{0:T(128)} %copy-done.44) | copy-start | bytes 1540
  107.3 8.8 %copy-start.52 = (f32[128]{0:T(128)S(1)}, f32[128]{0:T(128)}, u32[]{:S(2)}) copy-start(f32[128]{0:T(128)} %copy-done.51) | copy-start | bytes 1540
  113.1 1.6 copy-start.21
  113.1 4.9 %copy-start.4 = (f32[128,384]{1,0:T(8,128)S(1)}, f32[128,384]{1,0:T(8,128)}, u32[]{:S(2)}) copy-start(f32[128,384]{1,0:T(8,128)} %copy-done.3) | copy-start | bytes 589828
  113.1 1.6 copy-start.58
  113.3 5.1 %copy-start.2 = (bf16[16,48,384]{2,1,0:T(8,128)(2,1)S(1)}, bf16[16,48,384]{2,1,0:T(8,128)(2,1)}, u32[]{:S(2)}) copy-start(bf16[16,48,384]{2,1,0:T(8,128)(2,1)} %copy-done.1) | copy-start | bytes 1769476
  116.1 3.0 %copy-start.17 = (f32[128,128]{1,0:T(8,128)S(1)}, f32[128,128]{1,0:T(8,128)}, u32[]{:S(2)}) copy-start(f32[128,128]{1,0:T(8,128)} %copy-done.16) | copy-start | bytes 196612
  118.7 1.0 copy-start.30
  122.0 3.5 %copy-start.8 = (s32[2,64,1]{2,1,0:T(8,128)S(1)}, s32[2,64,1]{2,1,0:T(8,128)}, u32[]{:S(2)}) copy-start(s32[2,64,1]{2,1,0:T(8,128)} %copy-done.7) | copy-start | bytes 1540
  122.0 3.5 %copy-start.9 = (bf16[128,512]{1,0:T(8,128)(2,1)S(1)}, bf16[128,512]{1,0:T(8,128)(2,1)}, u32[]{:S(2)}) copy-start(bf16[128,512]{1,0:T(8,128)(2,1)} %concatenate.18.refs_0_) | copy-start | bytes 393220
  125.5 62.9 %copy-start.50 = (f32[1536]{0:T(1024)S(1)}, f32[1536]{0:T(1024)}, u32[]{:S(2)}) copy-start(f32[1536]{0:T(1024)} %get-tuple-element.126) | copy-start | bytes 18436
  183.6 0.7 copy-start.12
  184.4 0.6 copy-start.14
  185.0 0.7 copy-start.5
  185.0 0.8 copy-start.10
  185.0 7.7 %copy-start.41 = (f32[768]{0:T(1024)S(1)}, f32[768]{0:T(1024)}, u32[]{:S(2)}) copy-start(f32[768]{0:T(1024)} %get-tuple-element.84) | copy-start | bytes 9220
  185.8 7.0 %copy-start.6 = (bf16[128,1152]{1,0:T(8,128)(2,1)S(1)}, bf16[128,1152]{1,0:T(8,128)(2,1)}, u32[]{:S(2)}) copy-start(bf16[128,1152]{1,0:T(8,128)(2,1)} %copy-done.5) | copy-start | bytes 884740
  192.8 26.8 %copy-start.29 = (f32[48,3,384]{2,0,1:T(8,128)S(1)}, f32[48,3,384]{2,0,1:T(8,128)}, u32[]{:S(2)}) copy-start(f32[48,3,384]{2,0,1:T(8,128)} %param.27) | copy-start | bytes 663556
  192.8 26.8 %copy-start.36 = (f32[48,3,384]{2,0,1:T(8,128)S(1)}, f32[48,3,384]{2,0,1:T(8,128)}, u32[]{:S(2)}) copy-start(f32[48,3,384]{2,0,1:T(8,128)} %param.34) | copy-start | bytes 663556
  192.8 26.8 %copy-start.37 = (f32[48,3,384]{2,0,1:T(8,128)S(1)}, f32[48,3,384]{2,0,1:T(8,128)}, u32[]{:S(2)}) copy-start(f32[48,3,384]{2,0,1:T(8,128)} %param.35) | copy-start | bytes 663556
  193.5 27.2 %copy-start.47 = (f32[128]{0:T(128)S(1)}, f32[128]{0:T(128)}, u32[]{:S(2)}) copy-start(f32[128]{0:T(128)} %div.170) | copy-start | bytes 1540
  193.5 27.4 %copy-start.64 = (f32[128]{0:T(128)S(1)}, f32[128]{0:T(128)}, u32[]{:S(2)}) copy-start(f32[128]{0:T(128)} %copy-done.63) | copy-start | bytes 1540
  193.5 27.4 %copy-start.53 = (f32[128]{0:T(128)S(1)}, f32[128]{0:T(128)}, u32[]{:S(2)}) copy-start(f32[128]{0:T(128)} %rsqrt.22) | copy-start | bytes 1540
  193.5 27.7 %copy-start.22 = (f32[128,768]{1,0:T(8,128)S(1)}, f32[128,768]{1,0:T(8,128)}, u32[]{:S(2)}) copy-start(f32[128,768]{1,0:T(8,128)} %copy-done.21) | copy-start | bytes 1179652
  193.5 27.7 %copy-start.24 = (bf16[2,64,768]{2,1,0:T(8,128)(2,1)S(1)}, bf16[2,64,768]{2,1,0:T(8,128)(2,1)}, u32[]{:S(2)}) copy-start(bf16[2,64,768]{2,1,0:T(8,128)(2,1)} %param.25) | copy-start | bytes 589828
  193.5 27.7 %copy-start.59 = (f32[128]{0:T(128)S(1)}, f32[128]{0:T(128)}, u32[]{:S(2)}) copy-start(f32[128]{0:T(128)} %copy-done.58) | copy-start | bytes 1540
  219.6 2.7 %copy-start.43 = (f32[6,48]{1,0:T(8,128)S(1)}, f32[6,48]{1,0:T(8,128)}, u32[]{:S(2)}) copy-start(f32[6,48]{1,0:T(8,128)} %param.33) | copy-start | bytes 3460
  219.6 2.7 %copy-start.54 = (f32[6,48]{1,0:T(8,128)S(1)}, f32[6,48]{1,0:T(8,128)}, u32[]{:S(2)}) copy-start(f32[6,48]{1,0:T(8,128)} %param.46) | copy-start | bytes 3460
  219.6 2.7 %copy-start.55 = (f32[6,48]{1,0:T(8,128)S(1)}, f32[6,48]{1,0:T(8,128)}, u32[]{:S(2)}) copy-start(f32[6,48]{1,0:T(8,128)} %param.47) | copy-start | bytes 3460
  219.6 3.5 %copy-start.40 = (f32[1536]{0:T(1024)S(1)}, f32[1536]{0:T(1024)}, u32[]{:S(2)}) copy-start(f32[1536]{0:T(1024)} %param.32) | copy-start | bytes 18436
  219.6 3.4 %copy-start.48 = (f32[1536]{0:T(1024)S(1)}, f32[1536]{0:T(1024)}, u32[]{:S(2)}) copy-start(f32[1536]{0:T(1024)} %param.44) | copy-start | bytes 18436
  219.6 3.4 %copy-start.49 = (f32[1536]{0:T(1024)S(1)}, f32[1536]{0:T(1024)}, u32[]{:S(2)}) copy-start(f32[1536]{0:T(1024)} %param.45) | copy-start | bytes 18436
  219.6 4.1 %copy-start.46 = (f32[2,384]{1,0:T(2,128)S(1)}, f32[2,384]{1,0:T(2,128)}, u32[]{:S(2)}) copy-start(f32[2,384]{1,0:T(2,128)} %param.31) | copy-start | bytes 9220
  219.7 4.1 %copy-start.56 = (f32[2,384]{1,0:T(2,128)S(1)}, f32[2,384]{1,0:T(2,128)}, u32[]{:S(2)}) copy-start(f32[2,384]{1,0:T(2,128)} %param.42) | copy-start | bytes 9220
  219.7 4.1 %copy-start.57 = (f32[2,384]{1,0:T(2,128)S(1)}, f32[2,384]{1,0:T(2,128)}, u32[]{:S(2)}) copy-start(f32[2,384]{1,0:T(2,128)} %param.43) | copy-start | bytes 9220
  219.7 4.7 %copy-start.13 = (f32[48,1536]{1,0:T(8,128)S(1)}, f32[48,1536]{1,0:T(8,128)}, u32[]{:S(2)}) copy-start(f32[48,1536]{1,0:T(8,128)} %copy-done.12) | copy-start | bytes 884740
  219.7 4.7 %copy-start.27 = (f32[1536,48]{0,1:T(8,128)S(1)}, f32[1536,48]{0,1:T(8,128)}, u32[]{:S(2)}) copy-start(f32[1536,48]{0,1:T(8,128)} %param.30) | copy-start | bytes 884740
  219.7 4.7 %copy-start.32 = (f32[1536,48]{0,1:T(8,128)S(1)}, f32[1536,48]{0,1:T(8,128)}, u32[]{:S(2)}) copy-start(f32[1536,48]{0,1:T(8,128)} %param.40) | copy-start | bytes 884740
  219.7 4.7 %copy-start.33 = (f32[1536,48]{0,1:T(8,128)S(1)}, f32[1536,48]{0,1:T(8,128)}, u32[]{:S(2)}) copy-start(f32[1536,48]{0,1:T(8,128)} %param.41) | copy-start | bytes 884740
  221.1 4.3 %copy-start.11 = (f32[48,1536]{1,0:T(8,128)S(1)}, f32[48,1536]{1,0:T(8,128)}, u32[]{:S(2)}) copy-start(f32[48,1536]{1,0:T(8,128)} %copy-done.10) | copy-start | bytes 884740
  221.1 4.3 %copy-start.28 = (f32[48,1536]{1,0:T(8,128)S(1)}, f32[48,1536]{1,0:T(8,128)}, u32[]{:S(2)}) copy-start(f32[48,1536]{1,0:T(8,128)} %param.29) | copy-start | bytes 884740
  221.1 4.3 %copy-start.34 = (f32[48,1536]{1,0:T(8,128)S(1)}, f32[48,1536]{1,0:T(8,128)}, u32[]{:S(2)}) copy-start(f32[48,1536]{1,0:T(8,128)} %param.38) | copy-start | bytes 884740
  221.2 4.3 %copy-start.35 = (f32[48,1536]{1,0:T(8,128)S(1)}, f32[48,1536]{1,0:T(8,128)}, u32[]{:S(2)}) copy-start(f32[48,1536]{1,0:T(8,128)} %param.39) | copy-start | bytes 884740
  222.2 4.3 %copy-start.15 = (f32[48,384]{1,0:T(8,128)S(1)}, f32[48,384]{1,0:T(8,128)}, u32[]{:S(2)}) copy-start(f32[48,384]{1,0:T(8,128)} %copy-done.14) | copy-start | bytes 221188
  222.3 4.2 %copy-start.31 = (f32[384,48]{0,1:T(8,128)S(1)}, f32[384,48]{0,1:T(8,128)}, u32[]{:S(2)}) copy-start(f32[384,48]{0,1:T(8,128)} %param.28) | copy-start | bytes 221188
  222.3 4.2 %copy-start.38 = (f32[384,48]{0,1:T(8,128)S(1)}, f32[384,48]{0,1:T(8,128)}, u32[]{:S(2)}) copy-start(f32[384,48]{0,1:T(8,128)} %param.36) | copy-start | bytes 221188
  222.3 4.2 %copy-start.39 = (f32[384,48]{0,1:T(8,128)S(1)}, f32[384,48]{0,1:T(8,128)}, u32[]{:S(2)}) copy-start(f32[384,48]{0,1:T(8,128)} %param.37) | copy-start | bytes 221188
  (1 other events, 0.5 us)

commit v3 on v2

--- a/solution.py
+++ b/solution.py
@@ -472,12 +472,19 @@
         self.far_left = ring.chips - 1 - self.far_right
         self.sent = []
 
-    def hop(self, at, src, slot, index, device):
-        copy = remote(
-            src, self.outs[at].at[slot], self.ring_send.at[at, index],
-            self.ring_recv.at[at, index], device,
-        )
-        return copy
+    def hop(self, at, src, slot, step, sign):
+        columns, last = slice(None), step == self.far_right - 1
+        if last:
+            width = src.shape[-1]
+            cut = (width + 128) // 256 * 128
+            columns = slice(0, cut) if sign > 0 else slice(cut, width)
+        index = step if sign > 0 else self.far_right + step
+        return remote(
+            src.at[:, columns] if last else src,
+            self.outs[at].at[slot, :, columns] if last else self.outs[at].at[slot],
+            self.ring_send.at[at, index], self.ring_recv.at[at, index],
+            self.ring.right if sign > 0 else self.ring.left,
+        )
 
     def pass_on(self, at, src, slot, index):
         copy = remote(
@@ -493,26 +500,24 @@
     def start(self):
         ring = self.ring
         for at, block in enumerate(self.ins):
-            self.go(self.hop(at, block, ring.me, 0, ring.right))
-            self.go(self.hop(at, block, ring.me, self.far_right, ring.left))
+            self.go(self.hop(at, block, ring.me, 0, 1))
+            self.go(self.hop(at, block, ring.me, 0, -1))
             self.go(self.pass_on(at, block, ring.me, 0))
             pltpu.make_async_copy(block, self.outs[at].at[ring.me], self.own.at[at]).start()
 
     def step(self, step):
         ring = self.ring
+        last = step == self.far_right - 1
         for at in range(len(self.ins)):
-            for sign, far, base, device in (
-                (-1, self.far_right, 0, ring.right),
-                (1, self.far_left, self.far_right, ring.left),
-            ):
-                if step >= far:
-                    continue
-                slot = ring.slot(sign * (step + 1))
+            for sign in (1, -1):
+                slot = ring.slot(-sign * (step + 1))
                 block = self.outs[at].at[slot]
-                self.hop(at, block, slot, base + step, device).wait_recv()
-                if step + 1 < far:
-                    self.go(self.hop(at, block, slot, base + step + 1, device))
-                self.go(self.pass_on(at, block, slot, 1 + base + step))
+                self.hop(at, block, slot, step, sign).wait_recv()
+                if not last:
+                    self.go(self.hop(at, block, slot, step + 1, sign))
+                if not last or sign < 0:
+                    index = 1 + step if last or sign > 0 else 1 + self.far_right + step
+                    self.go(self.pass_on(at, block, slot, index))
 
     def finish(self):
         ring = self.ring
@@ -614,71 +619,6 @@
     return array.reshape(groups, array.shape[0] // groups, array.shape[1])
 
 
-def tail_kernel(chips, pieces, *refs):
-    grad, part, normal, small_in = refs[0:4]
-    out, total, small_out = refs[4:7]
-    hold, land, small, mate = refs[7:11]
-    lands, sems = refs[11 : 11 + len(pieces)], refs[11 + len(pieces) :]
-    pair_send, pair_recv = sems[4:6]
-    other = 1 - lax.axis_index("tp")
-    ring = Ring(chips)
-    barrier = pltpu.get_barrier_semaphore()
-    pl.semaphore_signal(barrier, inc=1, device_id={"tp": other}, device_id_type=MESH)
-    ring.greet(4)
-    scatter = Scatter(ring, pieces, [grad], [mate], lands, [out], sems[:4])
-    scatter.start()
-    hold[...] = part[...].astype(jnp.bfloat16)
-    pair = pltpu.make_async_remote_copy(
-        src_ref=hold, dst_ref=land, send_sem=pair_send.at[0], recv_sem=pair_recv.at[0],
-        device_id={"tp": other}, device_id_type=MESH,
-    )
-    pair.start()
-    gather = Gather(ring, [small], [small_out], sems[6:])
-    scatter.step(0)
-    scatter.step(1)
-    small[...] = small_in[...]
-    pair.wait()
-    summed = hold[...].astype(jnp.float32) + land[...].astype(jnp.float32)
-    total[...] = summed
-    small[0:1, :] = jnp.sum(summed * normal[...], axis=0, keepdims=True)
-    small[1:2, :] = jnp.sum(summed, axis=0, keepdims=True)
-    gather.start()
-    for step in range(2, chips):
-        scatter.step(step)
-        if step - 2 < gather.far_right:
-            gather.step(step - 2)
-    gather.finish()
-    scatter.finish()
-
-
-def tail(grad, part, normal, small, groups, collective):
-    chips = groups // 2
-    block = row_split(grad, groups)
-    columns = block.shape[2]
-    right = columns // 256 * 128
-    pieces = ((0, 0, right, 1), (0, right, columns - right, -1))
-    vmem = pl.BlockSpec(memory_space=pltpu.VMEM)
-    dma = pltpu.SemaphoreType.DMA
-    return pl.pallas_call(
-        partial(tail_kernel, chips, pieces),
-        out_shape=[
-            jax.ShapeDtypeStruct(block.shape[1:], jnp.float32),
-            jax.ShapeDtypeStruct(part.shape, jnp.float32),
-            jax.ShapeDtypeStruct((groups,) + small.shape, jnp.float32),
-        ],
-        in_specs=[vmem] * 4,
-        out_specs=[vmem] * 3,
-        scratch_shapes=[pltpu.VMEM(part.shape, jnp.bfloat16)] * 2
-        + [pltpu.VMEM(small.shape, jnp.float32)]
-        + scatter_scratch([block], pieces, chips)
-        + [dma((1,)), dma((1,))]
-        + gather_sems(1, chips),
-        compiler_params=pltpu.CompilerParams(
-            collective_id=collective, has_side_effects=True, vmem_limit_bytes=VMEM_LIMIT
-        ),
-    )(block, part, normal, small)
-
-
 def pair_kernel(count, *refs):
     ins, outs = refs[:count], refs[count : 2 * count]
     holds, lands = refs[2 * count : 3 * count], refs[3 * count : 4 * count]
@@ -745,7 +685,7 @@
 def front_kernel(chips, heads, *refs):
     ins, (bias, own_pos, all_pos) = refs[0:5], refs[5:8]
     outs, vectors_ref, every, context_ref, log_ref = refs[8:13], *refs[13:17]
-    tokens_all, sems = outs[1], refs[17:]
+    tokens_all, lows, sems = outs[1], refs[17:20], refs[20:]
     width = heads * HD
     groups = 2 * chips
     seqs = own_pos.shape[0]
@@ -753,8 +693,10 @@
     ring = Ring(chips)
     ring.greet()
     first = Gather(ring, ins[0:2], outs[0:2], sems[0:5])
-    second = Gather(ring, ins[2:5], outs[2:5], sems[5:10])
+    second = Gather(ring, lows, outs[2:5], sems[5:10])
     first.start()
+    for low, weight in zip(lows, ins[2:5]):
+        low[...] = weight[...].astype(jnp.bfloat16)
     for step in range(first.far_right - 1):
         first.step(step)
     second.start()
@@ -804,38 +746,74 @@
     chips = groups // 2
     return pl.pallas_call(
         partial(front_kernel, chips, heads),
-        out_shape=[jax.ShapeDtypeStruct((groups,) + a.shape, a.dtype) for a in arrays]
+        out_shape=[jax.ShapeDtypeStruct((groups,) + a.shape, jnp.bfloat16) for a in arrays]
         + [
             jax.ShapeDtypeStruct((8, width), jnp.float32),
             jax.ShapeDtypeStruct((groups, many, 3 * heads * HD), jnp.bfloat16),
             jax.ShapeDtypeStruct((many, heads * HD), jnp.float32),
             jax.ShapeDtypeStruct((many, 128), jnp.float32),
         ],
-        in_specs=[vmem] * 2 + [hbm] * 3 + [vmem] * 3,
+        in_specs=[vmem] * 8,
         out_specs=[vmem] * 2 + [hbm] * 3 + [vmem] * 4,
-        scratch_shapes=gather_sems(2, chips) + gather_sems(3, chips),
+        scratch_shapes=[pltpu.VMEM(a.shape, jnp.bfloat16) for a in arrays[2:5]]
+        + gather_sems(2, chips)
+        + gather_sems(3, chips),
         compiler_params=pltpu.CompilerParams(
             collective_id=collective, has_side_effects=True, vmem_limit_bytes=VMEM_LIMIT
         ),
     )(*arrays, bias, own_pos, all_pos)
 
 
-def back_kernel(chips, heads, pieces, *refs):
+def token_sum(array):
+    return jnp.sum(array.astype(jnp.float32), axis=0, keepdims=True)
+
+
+def back_kernel(chips, heads, pieces, lone, *refs):
     own, every, own_pos, all_pos = refs[0:4]
-    grads, out_ref, sums = refs[4:7], refs[7], refs[8:11]
-    gathered, mates, lands = refs[11], refs[12:15], refs[15 : 15 + len(pieces)]
-    sems = refs[15 + len(pieces) :]
+    grad_attn, context, normed_mid, grad_pre, grad_low, hidden = refs[4:10]
+    normed, packed, normal, grad_two, normal_two = refs[10:15]
+    total, sums, small_out = refs[15], refs[16:20], refs[20]
+    out_ref, hold, land, small, gathered = refs[21:26]
+    grads, rest = refs[26:30], refs[30:]
+    many = len(pieces)
+    mates, lands, sems, rest = rest[0:3], rest[3 : 3 + many], rest[3 + many : 7 + many], rest[7 + many :]
+    alone = len(lone)
+    mate, lone_lands, lone_sems = rest[0:1], rest[1 : 1 + alone], rest[1 + alone : 5 + alone]
+    pair_send, pair_recv = rest[5 + alone : 7 + alone]
+    gather_one, gather_two = rest[7 + alone : 12 + alone], rest[12 + alone : 17 + alone]
     seqs = own_pos.shape[0]
     rows = own.shape[0] // seqs
     width = heads * HD
+    other = 1 - lax.axis_index("tp")
     ring = Ring(chips)
     me = ring.me
-    ring.greet()
-    gather = Gather(ring, [own], [gathered], sems[4:])
-    scatter = Scatter(ring, pieces, grads, mates, lands, sums, sems[:4])
+    barrier = pltpu.get_barrier_semaphore()
+    pl.semaphore_signal(barrier, inc=1, device_id={"tp": other}, device_id_type=MESH)
+    ring.greet(4)
+    gather = Gather(ring, [own], [gathered], gather_one)
+    scatter = Scatter(ring, pieces, grads[0:3], mates, lands, sums[0:3], sems)
+    lone_scatter = Scatter(ring, lone, grads[3:4], mate, lone_lands, sums[3:4], lone_sems)
+
+    def product(into, left, right):
+        blocks = into.shape[0] // 2
+        high = blocks * into.shape[1]
+        for half in range(2):
+            result = lax.dot_general(
+                left[:, half * high : (half + 1) * high], right[...],
+                (((0,), (0,)), ((), ())), preferred_element_type=jnp.float32,
+            )
+            into[half * blocks : (half + 1) * blocks] = result.astype(jnp.bfloat16).reshape(
+                (blocks,) + into.shape[1:]
+            )
+
     gather.start()
+    product(grads[2], grad_low, hidden)
+    gather.step(0)
+    product(grads[1], normed_mid, grad_pre)
+    gather.step(1)
+    product(grads[0], grad_attn, context)
     scatter.start()
-    for step in range(gather.far_right - 1):
+    for step in range(2, gather.far_right - 1):
         gather.step(step)
     scatter.step(0)
     gather.step(gather.far_right - 1)
@@ -872,34 +850,94 @@
             grad_key = mul(grad_score.astype(jnp.bfloat16), queries, NN) * 0.125
             out_ref[here, past] = grad_key.astype(jnp.bfloat16)
             out_ref[here, last] = grad_value.astype(jnp.bfloat16)
-            if head % 2 == 1 and done < chips - 1:
+            if head % 3 == 2 and done < chips - 1:
                 scatter.step(done)
                 done += 1
-    for step in range(done, chips):
-        scatter.step(step)
+    weights = packed[:, :, : 3 * width].reshape(-1, 3 * width)
+    hold[...] = mul(out_ref[...], weights, NT).astype(jnp.bfloat16)
+    pair = pltpu.make_async_remote_copy(
+        src_ref=hold, dst_ref=land, send_sem=pair_send.at[0], recv_sem=pair_recv.at[0],
+        device_id={"tp": other}, device_id_type=MESH,
+    )
+    pair.start()
+    product(grads[3], normed, out_ref)
+    lone_scatter.start()
+    if done < chips:
+        scatter.step(done)
+    lone_scatter.step(0)
+    small[...] = jnp.zeros_like(small)
+    small[2:3, :] = jnp.sum(grad_two[...] * normal_two[...], axis=0, keepdims=True)
+    small[3:4, :] = token_sum(grad_two[...])
+    small[4:5, :] = token_sum(grad_attn[...])
+    small[5:6, :] = token_sum(grad_low[...])
+    small[6:7, 0:width] = token_sum(out_ref[:, 0:width])
+    small[7:8, 0:width] = token_sum(out_ref[:, 2 * width : 3 * width])
+    span = small.shape[1]
+    for at in range(grad_pre.shape[1] // span):
+        small[8 + at : 9 + at, :] = token_sum(grad_pre[:, at * span : (at + 1) * span])
+    pair.wait()
+    summed = hold[...].astype(jnp.float32) + land[...].astype(jnp.float32)
+    total[...] = summed
+    small[0:1, :] = jnp.sum(summed * normal[...], axis=0, keepdims=True)
+    small[1:2, :] = token_sum(summed)
+    last = Gather(ring, [small], [small_out], gather_two)
+    last.start()
+    for step in range(1, chips):
+        if done + step < chips:
+            scatter.step(done + step)
+        lone_scatter.step(step)
+        if step - 1 < last.far_right:
+            last.step(step - 1)
+    for step in range(chips - 1, last.far_right):
+        last.step(step)
+    last.finish()
     scatter.finish()
-
-
-def back(own, every, own_pos, all_pos, grads, heads, groups, collective):
+    lone_scatter.finish()
+
+
+def back(arrays, widths, heads, groups, collective):
     vmem = pl.BlockSpec(memory_space=pltpu.VMEM)
+    dma = pltpu.SemaphoreType.DMA
     chips = groups // 2
-    blocks = [row_split(g, groups) for g in grads]
-    proj, up, down = [b.shape[2] for b in blocks]
+    own = arrays[0]
+    many, width = arrays[4].shape
+    blocks = [jax.ShapeDtypeStruct((groups, width // groups, w), jnp.bfloat16) for w in widths]
+    proj, up, down, qkv = widths
     cut = proj * 2 // 3 // 128 * 128
     pieces = ((1, 0, up, 1), (2, 0, down, -1), (0, 0, cut, 1), (0, cut, proj - cut, -1))
+    right = qkv // 256 * 128
+    lone = ((0, 0, right, 1), (0, right, qkv - right, -1))
+    small = (8 + -(-up // width) + 7) // 8 * 8, width
     return pl.pallas_call(
-        partial(back_kernel, chips, heads, pieces),
-        out_shape=[jax.ShapeDtypeStruct((own.shape[0], 3 * heads * HD), jnp.bfloat16)]
-        + [jax.ShapeDtypeStruct(b.shape[1:], jnp.float32) for b in blocks],
-        in_specs=[vmem] * 7,
-        out_specs=[vmem] * 4,
-        scratch_shapes=[pltpu.VMEM((groups,) + own.shape, own.dtype)]
-        + scatter_scratch(blocks, pieces, chips)
+        partial(back_kernel, chips, heads, pieces, lone),
+        out_shape=[jax.ShapeDtypeStruct((many, width), jnp.float32)]
+        + [jax.ShapeDtypeStruct(b.shape[1:], jnp.float32) for b in blocks]
+        + [jax.ShapeDtypeStruct((groups,) + small, jnp.float32)],
+        in_specs=[vmem] * 15,
+        out_specs=[vmem] * 6,
+        scratch_shapes=[
+            pltpu.VMEM((many, qkv), jnp.bfloat16),
+            pltpu.VMEM((many, width), jnp.bfloat16),
+            pltpu.VMEM((many, width), jnp.bfloat16),
+            pltpu.VMEM(small, jnp.float32),
+            pltpu.VMEM((groups,) + own.shape, own.dtype),
+        ]
+        + [pltpu.VMEM(b.shape, b.dtype) for b in blocks]
+        + scatter_scratch(blocks[0:3], pieces, chips)
+        + scatter_scratch(blocks[3:4], lone, chips)
+        + [dma((1,)), dma((1,))]
+        + gather_sems(1, chips)
         + gather_sems(1, chips),
         compiler_params=pltpu.CompilerParams(
             collective_id=collective, has_side_effects=True, vmem_limit_bytes=VMEM_LIMIT
         ),
-    )(own, every, own_pos, all_pos, *blocks)
+    )(*arrays)
+
+
+def standard(values):
+    center = values - jnp.mean(values, axis=-1, keepdims=True)
+    spread = jnp.mean(center * center, axis=-1, keepdims=True)
+    return center * lax.rsqrt(spread + 1e-05)
 
 
 def three_parts(array):
@@ -960,9 +998,9 @@
         [
             packed,
             tokens.reshape(many, width),
-            proj_weight.astype(low).T,
-            up_weight.astype(low),
-            down_weight.astype(low).T,
+            proj_weight.T,
+            up_weight,
+            down_weight.T,
         ],
         bias,
         own_pos,
@@ -971,21 +1009,19 @@
         groups,
         1,
     )
-    packed_full = packed_full.reshape(width, -1)
-    qkv_full = packed_full[:, : 3 * inner]
     proj_full = proj_full.reshape(width, -1)
     up_full = up_full.reshape(width, -1)
     down_full = down_full.reshape(width, -1)
     inputs = tokens.reshape(many, width).astype(jnp.float32)
     first_normalized, norm_one_back = jax.vjp(layer_norm, inputs, vectors[0], vectors[1])
     normed_low = first_normalized.astype(low)
-    center = inputs - jnp.mean(inputs, axis=-1, keepdims=True)
-    normal = center * lax.rsqrt(jnp.mean(center * center, axis=-1, keepdims=True) + 1e-05)
+    normal = standard(inputs)
     context_low = context.astype(low)
     (attn,) = pair_sum([mul(context_low, proj_full, NT)], 3)
     middle = inputs + (attn + vectors[4])
     second_normalized, norm_two_back = jax.vjp(layer_norm, middle, vectors[2], vectors[3])
     normed_mid = second_normalized.astype(low)
+    normal_two = standard(middle)
     hidden_preactivation = mul(normed_mid, up_full, NN) + up_bias
     hidden_activation, gelu_back = jax.vjp(gelu_tanh, hidden_preactivation)
     hidden_low = hidden_activation.astype(low)
@@ -996,7 +1032,7 @@
     )
     block_output = (middle + (mlp + vectors[5])).astype(low)
     grad_out = grad_low.astype(jnp.float32)
-    grad_mid_norm, grad_gain_two, grad_shift_two = norm_two_back(grad_normed_two)
+    grad_mid_norm = norm_two_back(grad_normed_two)[0]
     grad_middle = grad_out + grad_mid_norm
     grad_attn = grad_middle.astype(low)
     grad_context = mul(grad_attn, proj_full, NN).astype(low)
@@ -1008,57 +1044,23 @@
     stats = three_parts((logs + delta)[:, :16])
     own = jnp.concatenate([grad_context] + stats + [jnp.zeros((many, 80), low)], axis=1)
 
-    def turned(left, right):
-        return lax.dot_general(
-            left, right, (((0,), (0,)), ((), ())), preferred_element_type=jnp.float32
-        ).astype(low)
-
-    grad_low_qkv, sum_proj, sum_up, sum_down = back(
-        own,
-        every,
-        own_pos,
-        all_pos,
+    grad_normed_one, sum_proj, sum_up, sum_down, sum_qkv, all_small = back(
         [
-            turned(grad_attn, context_low),
-            turned(normed_mid, grad_pre),
-            turned(grad_low, hidden_low),
+            own, every, own_pos, all_pos,
+            grad_attn, context_low, normed_mid, grad_pre, grad_low, hidden_low,
+            normed_low, packed_full, normal, grad_normed_two, normal_two,
         ],
+        (inner, up_full.shape[1], down_full.shape[1], 3 * inner),
         heads,
         groups,
         5,
     )
-    grad_qbias = jnp.sum(grad_low_qkv.astype(jnp.float32), axis=0)
-    small = jnp.concatenate(
-        [
-            jnp.zeros((2 * width,), jnp.float32),
-            grad_gain_two,
-            grad_shift_two,
-            jnp.sum(grad_attn.astype(jnp.float32), axis=0),
-            jnp.sum(grad_out, axis=0),
-            grad_qbias[:inner],
-            grad_qbias[2 * inner :],
-            jnp.sum(grad_pre.astype(jnp.float32), axis=0),
-        ]
-    )
-    used = small.shape[0]
-    small = jnp.pad(small, (0, -used % (8 * width))).reshape(-1, width)
-    sum_qkv, grad_normed_one, all_small = tail(
-        turned(normed_low, grad_low_qkv),
-        mul(grad_low_qkv, qkv_full, NT),
-        normal,
-        small,
-        groups,
-        6,
-    )
     grad_in_norm = norm_one_back(grad_normed_one)[0]
     input_grad = grad_middle + grad_in_norm
-    sums = jnp.sum(all_small, axis=0).reshape(-1)
-    ends = 6 * width
-    sum_vectors = lax.dynamic_slice_in_dim(
-        sums[:ends].reshape(6, width), device * share, share, 1
-    )
-    sum_qbias = sums[ends : ends + 2 * inner].reshape(2, inner)
-    sum_upbias = sums[ends + 2 * inner : used]
+    sums = jnp.sum(all_small, axis=0)
+    sum_vectors = lax.dynamic_slice_in_dim(sums[0:6], device * share, share, 1)
+    sum_qbias = sums[6:8, :inner]
+    sum_upbias = sums[8:].reshape(-1)[: up_bias.shape[0]]
     qkv_new = adamw(
         qkv_weight, sum_qkv.reshape(share, 3, inner), qkv_first, qkv_second, 0.1, 0.1
     )
@@ -1083,7 +1085,7 @@
 
 def solution(mesh):
     groups = mesh.shape["ctx"]
-    tiled = groups % 4 == 0 and WIDTH % (groups * 16) == 0
+    tiled = groups >= 16 and groups % 4 == 0 and WIDTH % (groups * 16) == 0
     return jax.shard_map(
         ring_local if tiled else local,
         mesh=mesh,

time: 228 us -> 189 us (0.83)
  Pallas kernels: 171 us -> 159 us
  local copies, waits for them, and re-layouts: 23 us -> 11.8 us
  matrix products: 14.1 us -> 4.21 us
  other arithmetic: 17.2 us -> 12.5 us
    pallas_call x2 -> x1, Pallas kernels: 84.1 us -> 77.4 us  [back(): pl.pallas_call(partial(back_kernel, chips, heads, pieces, lone), out_shap...]
    dot_general x4 -> x0, matrix products: 6.46 us -> none  [turned(): lax.dot_general(left, right, (((0,), (0,)), ((), ())), preferred_element_...]
    unnamed x138 -> x81, local copies, waits for them, and re-layouts: 15.5 us -> 9.22 us
    pallas_call x1, Pallas kernels: 69 us -> 63.1 us  [front(): pl.pallas_call(partial(front_kernel, chips, heads), out_shape=[jax.ShapeD...]
    dot_general x7 -> x6, matrix products: 7.36 us -> 3.88 us  [mul(): lax.dot_general(left, right, dims, preferred_element_type=jnp.float32)]
where the time goes in v3:
time: 189 us; the launch traced here: 188 us
  Pallas kernels  159 us (84%)
  other arithmetic  12.5 us (7%)
  local copies, waits for them, and re-layouts  11.8 us (6%)
  matrix products  4.21 us (2%)
    pallas_call x1, Pallas kernels, back(): pl.pallas_call(partial(back_kernel, chips, heads, pieces, lone), out_shap...  77.4 us
    pallas_call x1, Pallas kernels, front(): pl.pallas_call(partial(front_kernel, chips, heads), out_shape=[jax.ShapeD...  63.1 us
    pallas_call x2, Pallas kernels, pair_sum(): pl.pallas_call(partial(pair_kernel, count), out_shape=[jax.ShapeDtypeStru...  18.1 us
    unnamed x81, local copies, waits for them, and re-layouts  9.22 us
    sub x7, other arithmetic, adamw(): weight - rate * (first_hat / (jnp.sqrt(second_hat) + EPSILON) + decay * w...  5.66 us
    dot_general x6, matrix products, mul(): lax.dot_general(left, right, dims, preferred_element_type=jnp.float32)  3.88 us

profile of v3, /device:TPU:0, one launch (start us, length us, event | category | flops | bytes accessed | tf_op | source)
XLA Modules:
  0.0 188.5 jit_solution(8246527430779875083)
XLA Ops:
  0.7 0.8 dynamic-slice_multiply_fusion
  1.5 0.1 add.277
  1.6 0.1 add.350
  1.7 0.1 add.280
  1.8 0.1 broadcast_add_fusion.refs_6_.refs_2_
  1.9 0.8 copy.68
  2.6 0.1 fusion.30
  2.7 0.9 convert_bitcast_fusion
  3.7 0.8 slice_reduce_fusion.7
  4.5 0.7 broadcast_multiply_fusion.1
  5.2 0.1 add.283
  5.3 0.1 add.284
  5.4 0.1 add.286
  5.5 0.9 copy-done
  6.4 1.0 copy-done.4
  7.4 1.0 copy-done.6
  8.3 0.9 copy-done.13
  9.2 63.1 %shard_map.407 = (bf16[16,48,1280]{2,1,0:T(8,128)(2,1)S(1)}, bf16[16,128,768]{2,1,0:T(8,128)(2,1)}, bf16[16,48,384]{2,1,0:T(8,128)(2,1)S(1)}, bf16[16,48,1536]{2...) custom-call(bf16[48,1280]{1,0:T(8,128)(2,1)S(1)} %pad_maximum_fusion, ...), custom_call_target="tpu_custom_call" | custom-call | tf_op jit(solution)/shard_map/pallas_call | solution.py:747
  72.4 1.3 copy-done.2
  73.7 0.3 fusion.52.refs_0_
  74.1 0.0 copy-start.33
  74.1 7.3 %shard_map.408 = f32[128,768]{1,0:T(8,128)S(1)} custom-call(f32[128,768]{1,0:T(8,128)S(1)} %fusion.52.refs_0_), custom_call_target="tpu_custom_call" | custom-call | tf_op jit(solution)/shard_map/pallas_call | solution.py:648
  81.4 0.1 slice_reduce_fusion.1
  81.5 0.1 convert_reduce_fusion
  81.6 0.2 fusion.11
  81.8 0.1 add.309
  81.9 0.1 div.174
  82.0 0.8 fusion.8
  82.9 0.2 multiply_reduce_fusion.1
  83.1 0.0 copy-start.3
  83.1 0.1 add_convert_fusion.2
  83.2 0.5 copy-done.20
  83.7 0.6 multiply_convert_fusion
  84.4 0.6 copy-done.19
  85.0 0.9 fusion.3.refs_7_
  86.0 0.9 fusion.54.refs_1_
  86.9 0.9 fusion.53.refs_0_
  87.7 10.8 %shard_map.409 = (f32[128,768]{1,0:T(8,128)S(1)}, f32[128,768]{1,0:T(8,128)S(1)}) custom-call(f32[128,768]{1,0:T(8,128)S(1)} %fusion.53.refs_0_, f32[128,768]{1,0:T(8,128)S(1)} %fusion.54.refs_1_), custom_call_target="tpu_custom_call" | custom-call | tf_op jit(solution)/shard_map/pallas_call | solution.py:648
  98.5 0.0 copy-start.16
  98.5 0.2 multiply_reduce_fusion
  98.7 0.8 fusion.50
  99.6 0.1 fusion.15.refs_4_
  99.7 0.3 convolution_convert_fusion
  100.0 0.0 copy-start.22
  100.0 0.3 fusion.18
  100.4 0.2 copy-done.22
  100.6 1.0 concatenate.15.refs_0_
  101.7 0.9 copy-done.10
  102.6 0.9 copy-done.12
  103.5 0.0 copy-start.25
  103.5 0.0 copy-start.26
  103.5 77.4 %shard_map.410 = (f32[128,768]{1,0:T(8,128)S(1)}, f32[48,384]{1,0:T(8,128)S(1)}, f32[48,1536]{1,0:T(8,128)S(1)}, f32[48,1536]{1,0:T(8,128)S(1)}, f32[48,1152]{1,0:T(8,128)S(1)}, /*index=5*/f32[16,16,768]{2,1,0:T(8,128)S(1)}) custom-call(bf16[128,512]{1,0:T(8,128)(2,1)S(1)} %concatenate.15.refs_0_, bf16[16,128,1152]{2,1,0:T(8,128)(2,1)} %get-tuple-element.47.refs_1_, ...), custom_call_target="tpu_custom_call" | custom-call | tf_op jit(solution)/shard_map/pallas_call | solution.py:911
  181.0 0.0 copy-start.27
  181.0 0.0 copy-start.28
  181.0 1.0 multiply_subtract_fusion.1
  182.1 1.0 multiply_subtract_fusion
  183.2 0.9 multiply_subtract_fusion.2
  184.2 0.2 fusion.9
  184.4 0.2 fusion.39
  184.7 1.0 add_add_fusion.2
  185.7 0.7 add_subtract_fusion
  186.5 0.7 add_subtract_fusion.2
  187.2 0.6 add_subtract_fusion.1
  187.8 0.6 add_subtract_fusion.3
  (88 shorter events, 0.4 us)
Async XLA Ops:
  0.7 80.8 %copy-start.1 = (bf16[2,64,768]{2,1,0:T(8,128)(2,1)S(1)}, bf16[2,64,768]{2,1,0:T(8,128)(2,1)}, u32[]{:S(2)}) copy-start(bf16[2,64,768]{2,1,0:T(8,128)(2,1)} %param.24) | copy-start | bytes 589828
  5.5 0.9 copy-start
  6.4 1.0 copy-start.4
  7.4 1.0 copy-start.6
  8.3 0.9 copy-start.13
  72.4 1.3 copy-start.2
  73.7 7.7 %copy-start.15 = (f32[128,128]{1,0:T(8,128)}, f32[128,128]{1,0:T(8,128)S(1)}, u32[]{:S(2)}) copy-start(f32[128,128]{1,0:T(8,128)S(1)} %get-tuple-element.46) | copy-start | bytes 196612
  74.1 9.2 %copy-start.33 = (f32[1536]{0:T(1024)S(1)}, f32[1536]{0:T(1024)}, u32[]{:S(2)}) copy-start(f32[1536]{0:T(1024)} %param.32) | copy-start | bytes 18436
  82.0 1.7 copy-start.20
  83.1 1.3 copy-start.3
  83.1 2.0 %copy-start.19 = (bf16[16,48,1536]{2,1,0:T(8,128)(2,1)S(1)}, bf16[16,48,1536]{2,1,0:T(8,128)(2,1)}, u32[]{:S(2)}) copy-start(bf16[16,48,1536]{2,1,0:T(8,128)(2,1)} %get-tuple-element.43) | copy-start | bytes 7077892
  83.2 2.8 %copy-start.11 = (bf16[128,768]{1,0:T(8,128)(2,1)}, bf16[128,768]{1,0:T(8,128)(2,1)S(1)}, u32[]{:S(2)}) copy-start(bf16[128,768]{1,0:T(8,128)(2,1)S(1)} %get-tuple-element.109.refs_6_) | copy-start | bytes 589828
  98.5 1.8 copy-start.16
  99.6 0.8 copy-start.17
  100.0 0.6 copy-start.22
  101.6 0.9 copy-start.10
  102.6 0.9 copy-start.12
  103.5 77.5 %copy-start.5 = (f32[48,1536]{1,0:T(8,128)S(1)}, f32[48,1536]{1,0:T(8,128)}, u32[]{:S(2)}) copy-start(f32[48,1536]{1,0:T(8,128)} %refs_3_.1) | copy-start | bytes 884740
  103.5 77.5 %copy-start.23 = (f32[48,1536]{1,0:T(8,128)S(1)}, f32[48,1536]{1,0:T(8,128)}, u32[]{:S(2)}) copy-start(f32[48,1536]{1,0:T(8,128)} %param.38) | copy-start | bytes 884740
  103.5 77.5 %copy-start.24 = (f32[48,1536]{1,0:T(8,128)S(1)}, f32[48,1536]{1,0:T(8,128)}, u32[]{:S(2)}) copy-start(f32[48,1536]{1,0:T(8,128)} %param.39) | copy-start | bytes 884740
  103.5 78.6 %copy-start.7 = (f32[1536,48]{0,1:T(8,128)S(1)}, f32[1536,48]{0,1:T(8,128)}, u32[]{:S(2)}) copy-start(f32[1536,48]{0,1:T(8,128)} %param.30) | copy-start | bytes 884740
  103.5 78.6 %copy-start.25 = (f32[1536,48]{0,1:T(8,128)S(1)}, f32[1536,48]{0,1:T(8,128)}, u32[]{:S(2)}) copy-start(f32[1536,48]{0,1:T(8,128)} %param.40) | copy-start | bytes 884740
  103.5 78.6 %copy-start.26 = (f32[1536,48]{0,1:T(8,128)S(1)}, f32[1536,48]{0,1:T(8,128)}, u32[]{:S(2)}) copy-start(f32[1536,48]{0,1:T(8,128)} %param.41) | copy-start | bytes 884740
  181.0 3.2 %copy-start.8 = (f32[16,16,768]{2,1,0:T(8,128)}, f32[16,16,768]{2,1,0:T(8,128)S(1)}, u32[]{:S(2)}) copy-start(f32[16,16,768]{2,1,0:T(8,128)S(1)} %get-tuple-element.54) | copy-start | bytes 2359300
  181.0 2.2 %copy-start.21 = (f32[48,3,384]{2,0,1:T(8,128)S(1)}, f32[48,3,384]{2,0,1:T(8,128)}, u32[]{:S(2)}) copy-start(f32[48,3,384]{2,0,1:T(8,128)} %param.27) | copy-start | bytes 663556
  181.0 2.2 %copy-start.27 = (f32[48,3,384]{2,0,1:T(8,128)S(1)}, f32[48,3,384]{2,0,1:T(8,128)}, u32[]{:S(2)}) copy-start(f32[48,3,384]{2,0,1:T(8,128)} %param.34) | copy-start | bytes 663556
  181.0 2.2 %copy-start.28 = (f32[48,3,384]{2,0,1:T(8,128)S(1)}, f32[48,3,384]{2,0,1:T(8,128)}, u32[]{:S(2)}) copy-start(f32[48,3,384]{2,0,1:T(8,128)} %param.35) | copy-start | bytes 663556
  182.1 2.6 %copy-start.18 = (f32[128,768]{1,0:T(8,128)S(1)}, f32[128,768]{1,0:T(8,128)}, u32[]{:S(2)}) copy-start(f32[128,768]{1,0:T(8,128)} %copy-done.17) | copy-start | bytes 1179652
  183.1 2.5 %copy-start.14 = (f32[384,48]{0,1:T(8,128)S(1)}, f32[384,48]{0,1:T(8,128)}, u32[]{:S(2)}) copy-start(f32[384,48]{0,1:T(8,128)} %param.28) | copy-start | bytes 221188
  183.2 2.5 %copy-start.29 = (f32[384,48]{0,1:T(8,128)S(1)}, f32[384,48]{0,1:T(8,128)}, u32[]{:S(2)}) copy-start(f32[384,48]{0,1:T(8,128)} %param.36) | copy-start | bytes 221188
  183.2 2.5 %copy-start.30 = (f32[384,48]{0,1:T(8,128)S(1)}, f32[384,48]{0,1:T(8,128)}, u32[]{:S(2)}) copy-start(f32[384,48]{0,1:T(8,128)} %param.37) | copy-start | bytes 221188
  184.1 2.3 %copy-start.31 = (f32[6,48]{1,0:T(8,128)S(1)}, f32[6,48]{1,0:T(8,128)}, u32[]{:S(2)}) copy-start(f32[6,48]{1,0:T(8,128)} %param.33) | copy-start | bytes 3460
  184.1 2.3 %copy-start.36 = (f32[6,48]{1,0:T(8,128)S(1)}, f32[6,48]{1,0:T(8,128)}, u32[]{:S(2)}) copy-start(f32[6,48]{1,0:T(8,128)} %param.46) | copy-start | bytes 3460
  184.1 2.3 %copy-start.37 = (f32[6,48]{1,0:T(8,128)S(1)}, f32[6,48]{1,0:T(8,128)}, u32[]{:S(2)}) copy-start(f32[6,48]{1,0:T(8,128)} %param.47) | copy-start | bytes 3460
  184.1 3.1 %copy-start.34 = (f32[1536]{0:T(1024)S(1)}, f32[1536]{0:T(1024)}, u32[]{:S(2)}) copy-start(f32[1536]{0:T(1024)} %param.44) | copy-start | bytes 18436
  184.1 3.1 %copy-start.35 = (f32[1536]{0:T(1024)S(1)}, f32[1536]{0:T(1024)}, u32[]{:S(2)}) copy-start(f32[1536]{0:T(1024)} %param.45) | copy-start | bytes 18436
  184.2 3.7 %copy-start.32 = (f32[2,384]{1,0:T(2,128)S(1)}, f32[2,384]{1,0:T(2,128)}, u32[]{:S(2)}) copy-start(f32[2,384]{1,0:T(2,128)} %param.31) | copy-start | bytes 9220
  184.2 3.7 %copy-start.38 = (f32[2,384]{1,0:T(2,128)S(1)}, f32[2,384]{1,0:T(2,128)}, u32[]{:S(2)}) copy-start(f32[2,384]{1,0:T(2,128)} %param.42) | copy-start | bytes 9220
  184.2 3.7 %copy-start.39 = (f32[2,384]{1,0:T(2,128)S(1)}, f32[2,384]{1,0:T(2,128)}, u32[]{:S(2)}) copy-start(f32[2,384]{1,0:T(2,128)} %param.43) | copy-start | bytes 9220
  184.2 2.2 %copy-start.9 = (f32[16,16,768]{2,1,0:T(8,128)S(1)}, f32[16,16,768]{2,1,0:T(8,128)}, u32[]{:S(2)}) copy-start(f32[16,16,768]{2,1,0:T(8,128)} %copy-done.8) | copy-start | bytes 2359300

commit v4 on v3

--- a/solution.py
+++ b/solution.py
@@ -850,7 +850,7 @@
             grad_key = mul(grad_score.astype(jnp.bfloat16), queries, NN) * 0.125
             out_ref[here, past] = grad_key.astype(jnp.bfloat16)
             out_ref[here, last] = grad_value.astype(jnp.bfloat16)
-            if head % 3 == 2 and done < chips - 1:
+            if head % 2 == 1 and done < chips - 1:
                 scatter.step(done)
                 done += 1
     weights = packed[:, :, : 3 * width].reshape(-1, 3 * width)

time: 189 us -> 193 us (1.021)
  Pallas kernels: 159 us -> 162 us
    pallas_call x1, Pallas kernels: 77.4 us -> 81.1 us  [back(): pl.pallas_call(partial(back_kernel, chips, heads, pieces, lone), out_shap...]
where the time goes in v4:
time: 193 us; the launch traced here: 192 us
  Pallas kernels  162 us (84%)
  other arithmetic  12.5 us (6%)
  local copies, waits for them, and re-layouts  11.8 us (6%)
  matrix products  4.21 us (2%)
    pallas_call x1, Pallas kernels, back(): pl.pallas_call(partial(back_kernel, chips, heads, pieces, lone), out_shap...  81.1 us
    pallas_call x1, Pallas kernels, front(): pl.pallas_call(partial(front_kernel, chips, heads), out_shape=[jax.ShapeD...  63.1 us
    pallas_call x2, Pallas kernels, pair_sum(): pl.pallas_call(partial(pair_kernel, count), out_shape=[jax.ShapeDtypeStru...  18.1 us
    unnamed x81, local copies, waits for them, and re-layouts  9.22 us
    sub x7, other arithmetic, adamw(): weight - rate * (first_hat / (jnp.sqrt(second_hat) + EPSILON) + decay * w...  5.66 us
    dot_general x6, matrix products, mul(): lax.dot_general(left, right, dims, preferred_element_type=jnp.float32)  3.88 us

profile of v4, /device:TPU:0, one launch (start us, length us, event | category | flops | bytes accessed | tf_op | source)
XLA Modules:
  0.0 192.1 jit_solution(10270891255604738639)
XLA Ops:
  0.7 0.0 copy-start.1
  0.7 0.8 dynamic-slice_multiply_fusion
  1.5 0.1 add.277
  1.6 0.1 add.350
  1.7 0.1 add.280
  1.8 0.1 broadcast_add_fusion.refs_6_.refs_2_
  1.9 0.8 copy.68
  2.6 0.1 fusion.30
  2.7 0.9 convert_bitcast_fusion
  3.7 0.8 slice_reduce_fusion.7
  4.5 0.7 broadcast_multiply_fusion.1
  5.2 0.1 add.283
  5.3 0.1 add.284
  5.4 0.1 add.286
  5.5 0.0 copy-start
  5.5 0.9 copy-done
  6.4 1.0 copy-done.4
  7.4 1.0 copy-done.6
  8.3 0.9 copy-done.13
  9.2 63.1 %shard_map.407 = (bf16[16,48,1280]{2,1,0:T(8,128)(2,1)S(1)}, bf16[16,128,768]{2,1,0:T(8,128)(2,1)}, bf16[16,48,384]{2,1,0:T(8,128)(2,1)S(1)}, bf16[16,48,1536]{2...) custom-call(bf16[48,1280]{1,0:T(8,128)(2,1)S(1)} %pad_maximum_fusion, ...), custom_call_target="tpu_custom_call" | custom-call | tf_op jit(solution)/shard_map/pallas_call | solution.py:747
  72.4 1.3 copy-done.2
  73.7 0.3 fusion.52.refs_0_
  74.1 0.0 copy-start.33
  74.1 7.3 %shard_map.408 = f32[128,768]{1,0:T(8,128)S(1)} custom-call(f32[128,768]{1,0:T(8,128)S(1)} %fusion.52.refs_0_), custom_call_target="tpu_custom_call" | custom-call | tf_op jit(solution)/shard_map/pallas_call | solution.py:648
  81.4 0.1 slice_reduce_fusion.1
  81.5 0.1 convert_reduce_fusion
  81.6 0.2 fusion.11
  81.8 0.1 add.309
  81.9 0.1 div.174
  82.0 0.8 fusion.8
  82.9 0.2 multiply_reduce_fusion.1
  83.1 0.1 add_convert_fusion.2
  83.2 0.0 copy-start.11
  83.2 0.5 copy-done.20
  83.7 0.6 multiply_convert_fusion
  84.4 0.6 copy-done.19
  85.0 0.9 fusion.3.refs_7_
  86.0 0.9 fusion.54.refs_1_
  86.9 0.9 fusion.53.refs_0_
  87.7 10.8 %shard_map.409 = (f32[128,768]{1,0:T(8,128)S(1)}, f32[128,768]{1,0:T(8,128)S(1)}) custom-call(f32[128,768]{1,0:T(8,128)S(1)} %fusion.53.refs_0_, f32[128,768]{1,0:T(8,128)S(1)} %fusion.54.refs_1_), custom_call_target="tpu_custom_call" | custom-call | tf_op jit(solution)/shard_map/pallas_call | solution.py:648
  98.5 0.2 multiply_reduce_fusion
  98.7 0.8 fusion.50
  99.6 0.1 fusion.15.refs_4_
  99.7 0.3 convolution_convert_fusion
  100.0 0.3 fusion.18
  100.4 0.2 copy-done.22
  100.6 1.0 concatenate.15.refs_0_
  101.6 0.0 copy-start.10
  101.7 0.9 copy-done.10
  102.6 0.9 copy-done.12
  103.5 81.1 %shard_map.410 = (f32[128,768]{1,0:T(8,128)S(1)}, f32[48,384]{1,0:T(8,128)S(1)}, f32[48,1536]{1,0:T(8,128)S(1)}, f32[48,1536]{1,0:T(8,128)S(1)}, f32[48,1152]{1,0:T(8,128)S(1)}, /*index=5*/f32[16,16,768]{2,1,0:T(8,128)S(1)}) custom-call(bf16[128,512]{1,0:T(8,128)(2,1)S(1)} %concatenate.15.refs_0_, bf16[16,128,1152]{2,1,0:T(8,128)(2,1)} %get-tuple-element.47.refs_1_, ...), custom_call_target="tpu_custom_call" | custom-call | tf_op jit(solution)/shard_map/pallas_call | solution.py:911
  184.6 0.0 copy-start.21
  184.7 1.0 multiply_subtract_fusion.1
  185.8 1.0 multiply_subtract_fusion
  186.8 0.9 multiply_subtract_fusion.2
  187.8 0.0 copy-start.35
  187.8 0.0 copy-start.32
  187.9 0.2 fusion.9
  188.1 0.2 fusion.39
  188.4 1.0 add_add_fusion.2
  189.3 0.7 add_subtract_fusion
  190.1 0.7 add_subtract_fusion.2
  190.9 0.6 add_subtract_fusion.1
  191.5 0.6 add_subtract_fusion.3
  (88 shorter events, 0.4 us)
Async XLA Ops:
  0.7 80.8 %copy-start.1 = (bf16[2,64,768]{2,1,0:T(8,128)(2,1)S(1)}, bf16[2,64,768]{2,1,0:T(8,128)(2,1)}, u32[]{:S(2)}) copy-start(bf16[2,64,768]{2,1,0:T(8,128)(2,1)} %param.24) | copy-start | bytes 589828
  5.5 0.9 copy-start
  6.4 1.0 copy-start.4
  7.4 1.0 copy-start.6
  8.3 0.9 copy-start.13
  72.4 1.3 copy-start.2
  73.7 7.7 %copy-start.15 = (f32[128,128]{1,0:T(8,128)}, f32[128,128]{1,0:T(8,128)S(1)}, u32[]{:S(2)}) copy-start(f32[128,128]{1,0:T(8,128)S(1)} %get-tuple-element.46) | copy-start | bytes 196612
  74.1 9.2 %copy-start.33 = (f32[1536]{0:T(1024)S(1)}, f32[1536]{0:T(1024)}, u32[]{:S(2)}) copy-start(f32[1536]{0:T(1024)} %param.32) | copy-start | bytes 18436
  82.0 1.7 copy-start.20
  83.1 1.3 copy-start.3
  83.1 2.0 %copy-start.19 = (bf16[16,48,1536]{2,1,0:T(8,128)(2,1)S(1)}, bf16[16,48,1536]{2,1,0:T(8,128)(2,1)}, u32[]{:S(2)}) copy-start(bf16[16,48,1536]{2,1,0:T(8,128)(2,1)} %get-tuple-element.43) | copy-start | bytes 7077892
  83.2 2.8 %copy-start.11 = (bf16[128,768]{1,0:T(8,128)(2,1)}, bf16[128,768]{1,0:T(8,128)(2,1)S(1)}, u32[]{:S(2)}) copy-start(bf16[128,768]{1,0:T(8,128)(2,1)S(1)} %get-tuple-element.109.refs_6_) | copy-start | bytes 589828
  98.5 1.8 copy-start.16
  99.6 0.8 copy-start.17
  100.0 0.6 copy-start.22
  101.6 0.9 copy-start.10
  102.6 0.9 copy-start.12
  103.5 81.2 %copy-start.5 = (f32[48,1536]{1,0:T(8,128)S(1)}, f32[48,1536]{1,0:T(8,128)}, u32[]{:S(2)}) copy-start(f32[48,1536]{1,0:T(8,128)} %refs_3_.1) | copy-start | bytes 884740
  103.5 81.2 %copy-start.23 = (f32[48,1536]{1,0:T(8,128)S(1)}, f32[48,1536]{1,0:T(8,128)}, u32[]{:S(2)}) copy-start(f32[48,1536]{1,0:T(8,128)} %param.38) | copy-start | bytes 884740
  103.5 81.2 %copy-start.24 = (f32[48,1536]{1,0:T(8,128)S(1)}, f32[48,1536]{1,0:T(8,128)}, u32[]{:S(2)}) copy-start(f32[48,1536]{1,0:T(8,128)} %param.39) | copy-start | bytes 884740
  103.5 82.2 %copy-start.7 = (f32[1536,48]{0,1:T(8,128)S(1)}, f32[1536,48]{0,1:T(8,128)}, u32[]{:S(2)}) copy-start(f32[1536,48]{0,1:T(8,128)} %param.30) | copy-start | bytes 884740
  103.5 82.2 %copy-start.25 = (f32[1536,48]{0,1:T(8,128)S(1)}, f32[1536,48]{0,1:T(8,128)}, u32[]{:S(2)}) copy-start(f32[1536,48]{0,1:T(8,128)} %param.40) | copy-start | bytes 884740
  103.5 82.2 %copy-start.26 = (f32[1536,48]{0,1:T(8,128)S(1)}, f32[1536,48]{0,1:T(8,128)}, u32[]{:S(2)}) copy-start(f32[1536,48]{0,1:T(8,128)} %param.41) | copy-start | bytes 884740
  184.6 3.2 %copy-start.8 = (f32[16,16,768]{2,1,0:T(8,128)}, f32[16,16,768]{2,1,0:T(8,128)S(1)}, u32[]{:S(2)}) copy-start(f32[16,16,768]{2,1,0:T(8,128)S(1)} %get-tuple-element.54) | copy-start | bytes 2359300
  184.6 2.2 %copy-start.21 = (f32[48,3,384]{2,0,1:T(8,128)S(1)}, f32[48,3,384]{2,0,1:T(8,128)}, u32[]{:S(2)}) copy-start(f32[48,3,384]{2,0,1:T(8,128)} %param.27) | copy-start | bytes 663556
  184.6 2.2 %copy-start.27 = (f32[48,3,384]{2,0,1:T(8,128)S(1)}, f32[48,3,384]{2,0,1:T(8,128)}, u32[]{:S(2)}) copy-start(f32[48,3,384]{2,0,1:T(8,128)} %param.34) | copy-start | bytes 663556
  184.7 2.2 %copy-start.28 = (f32[48,3,384]{2,0,1:T(8,128)S(1)}, f32[48,3,384]{2,0,1:T(8,128)}, u32[]{:S(2)}) copy-start(f32[48,3,384]{2,0,1:T(8,128)} %param.35) | copy-start | bytes 663556
  185.8 2.6 %copy-start.18 = (f32[128,768]{1,0:T(8,128)S(1)}, f32[128,768]{1,0:T(8,128)}, u32[]{:S(2)}) copy-start(f32[128,768]{1,0:T(8,128)} %copy-done.17) | copy-start | bytes 1179652
  186.8 2.5 %copy-start.14 = (f32[384,48]{0,1:T(8,128)S(1)}, f32[384,48]{0,1:T(8,128)}, u32[]{:S(2)}) copy-start(f32[384,48]{0,1:T(8,128)} %param.28) | copy-start | bytes 221188
  186.8 2.5 %copy-start.29 = (f32[384,48]{0,1:T(8,128)S(1)}, f32[384,48]{0,1:T(8,128)}, u32[]{:S(2)}) copy-start(f32[384,48]{0,1:T(8,128)} %param.36) | copy-start | bytes 221188
  186.8 2.5 %copy-start.30 = (f32[384,48]{0,1:T(8,128)S(1)}, f32[384,48]{0,1:T(8,128)}, u32[]{:S(2)}) copy-start(f32[384,48]{0,1:T(8,128)} %param.37) | copy-start | bytes 221188
  187.8 2.3 %copy-start.31 = (f32[6,48]{1,0:T(8,128)S(1)}, f32[6,48]{1,0:T(8,128)}, u32[]{:S(2)}) copy-start(f32[6,48]{1,0:T(8,128)} %param.33) | copy-start | bytes 3460
  187.8 2.3 %copy-start.36 = (f32[6,48]{1,0:T(8,128)S(1)}, f32[6,48]{1,0:T(8,128)}, u32[]{:S(2)}) copy-start(f32[6,48]{1,0:T(8,128)} %param.46) | copy-start | bytes 3460
  187.8 2.3 %copy-start.37 = (f32[6,48]{1,0:T(8,128)S(1)}, f32[6,48]{1,0:T(8,128)}, u32[]{:S(2)}) copy-start(f32[6,48]{1,0:T(8,128)} %param.47) | copy-start | bytes 3460
  187.8 3.1 %copy-start.34 = (f32[1536]{0:T(1024)S(1)}, f32[1536]{0:T(1024)}, u32[]{:S(2)}) copy-start(f32[1536]{0:T(1024)} %param.44) | copy-start | bytes 18436
  187.8 3.1 %copy-start.35 = (f32[1536]{0:T(1024)S(1)}, f32[1536]{0:T(1024)}, u32[]{:S(2)}) copy-start(f32[1536]{0:T(1024)} %param.45) | copy-start | bytes 18436
  187.8 3.7 %copy-start.32 = (f32[2,384]{1,0:T(2,128)S(1)}, f32[2,384]{1,0:T(2,128)}, u32[]{:S(2)}) copy-start(f32[2,384]{1,0:T(2,128)} %param.31) | copy-start | bytes 9220
  187.8 3.7 %copy-start.38 = (f32[2,384]{1,0:T(2,128)S(1)}, f32[2,384]{1,0:T(2,128)}, u32[]{:S(2)}) copy-start(f32[2,384]{1,0:T(2,128)} %param.42) | copy-start | bytes 9220
  187.8 3.7 %copy-start.39 = (f32[2,384]{1,0:T(2,128)S(1)}, f32[2,384]{1,0:T(2,128)}, u32[]{:S(2)}) copy-start(f32[2,384]{1,0:T(2,128)} %param.43) | copy-start | bytes 9220
  187.9 2.2 %copy-start.9 = (f32[16,16,768]{2,1,0:T(8,128)S(1)}, f32[16,16,768]{2,1,0:T(8,128)}, u32[]{:S(2)}) copy-start(f32[16,16,768]{2,1,0:T(8,128)} %copy-done.8) | copy-start | bytes 2359300
